TPU v7x, 512 devices: a whole 4x8x8 slice. The times are simulated.
512 devices in a mesh: clip: 2 (over core), tower: 2 (over z_lo), seq: 128 (over x, y, z_hi).
Axes of the slice: x: 4, y: 8, z: 8 (z_hi: 4, z_lo: 2; z = z_hi * 2 + z_lo), core: 2. Of those that a mesh axis runs over, the one named last changes fastest.
Arguments:
- video_query: bfloat16 [65536, 1536], P(('clip', 'tower', 'seq')), parts along dimension 0, may hold values from -4.5 to 4.5
- video_keys: bfloat16 [65536, 1536], P(('clip', 'tower', 'seq')), parts along dimension 0, may hold values from -4.5 to 4.5
- video_value: bfloat16 [65536, 1536], P(('clip', 'tower', 'seq')), parts along dimension 0, may hold values from -6 to 6
- audio_query: bfloat16 [32768, 1536], P(('clip', 'tower', 'seq')), parts along dimension 0, may hold values from -4.5 to 4.5
- audio_key: bfloat16 [32768, 1536], P(('clip', 'tower', 'seq')), parts along dimension 0, may hold values from -4.5 to 4.5
- audio_value: bfloat16 [32768, 1536], P(('clip', 'tower', 'seq')), parts along dimension 0, may hold values from -6 to 6
- video_cotangent: bfloat16 [65536, 1536], P(('clip', 'tower', 'seq')), parts along dimension 0, may hold values from -6 to 6
- audio_cotangent: bfloat16 [32768, 1536], P(('clip', 'tower', 'seq')), parts along dimension 0, may hold values from -6 to 6
- video_lists: int32 [512, 2], P(('clip', 'tower', 'seq')), parts along dimension 0, may hold values from 0 to 255, as said below
- audio_lists: int32 [512, 2], P(('clip', 'tower', 'seq')), parts along dimension 0, may hold values from 0 to 255, as said below
Outputs:
- video_output: bfloat16 [65536, 1536], P(('clip', 'tower', 'seq')), parts along dimension 0
- audio_output: bfloat16 [32768, 1536], P(('clip', 'tower', 'seq')), parts along dimension 0
- video_query_grad: bfloat16 [65536, 1536], P(('clip', 'tower', 'seq')), parts along dimension 0
- video_key_grad: bfloat16 [65536, 1536], P(('clip', 'tower', 'seq')), parts along dimension 0
- video_value_grad: bfloat16 [65536, 1536], P(('clip', 'tower', 'seq')), parts along dimension 0
- audio_query_grad: bfloat16 [32768, 1536], P(('clip', 'tower', 'seq')), parts along dimension 0
- audio_key_grad: bfloat16 [32768, 1536], P(('clip', 'tower', 'seq')), parts along dimension 0
- audio_value_grad: bfloat16 [32768, 1536], P(('clip', 'tower', 'seq')), parts along dimension 0
There are 2 independent parts, one for each index of `clip`. A program takes and returns all parts, laid end to end along the dimension named above; each array names one. Nothing has to cross between parts.
Inputs may be any that keep to these rules, and one draw needn't show every extreme that they name: `video_lists`: row b holds 2 consecutive block numbers, the first between max(b - 2, 0) and min(b, 254). `audio_lists`: row b holds 2 consecutive block numbers, the first between max(b - 2, 0) and min(b, 254).
All inputs are finite; a program needn't handle non-finite values.
Results may differ from a plain program's by a relative error of at most 0.012.
Values may be sent and summed in bfloat16 or wider, within the bound.
No kernel may reach another device: no remote copies, remote signals or barrier semaphores. Data moves between devices by JAX's collectives and lax.ppermute only.
A program may use at most 64 MiB of HBM per device.

v0:
```python
import jax
import jax.numpy as jnp
from jax import lax
from jax.sharding import PartitionSpec as P

HEADS = 12
HEAD_SIZE = 128
WINDOW_BLOCKS = 4
HALF_WINDOW = 2


def from_behind(block, axis, distance):
    devices = range(lax.axis_size(axis))
    route = [(i - distance, i) for i in devices if i - distance in devices]
    return lax.ppermute(block, axis, route)


def attend_forward(queries, key_rows, value_rows, keep_mask):
    query_row_block = queries.shape[0]
    key_row_block = key_rows.shape[0]
    heads_query = queries.reshape(query_row_block, HEADS, HEAD_SIZE)
    heads_key = key_rows.reshape(key_row_block, HEADS, HEAD_SIZE)
    heads_value = value_rows.reshape(key_row_block, HEADS, HEAD_SIZE)
    score_matrix = jnp.einsum(
        "xfk,ifk->fxi", heads_query, heads_key, preferred_element_type=jnp.float32
    ) * HEAD_SIZE ** (-0.5)
    score_matrix = jnp.where(keep_mask[None, None, :], score_matrix, -1e30)
    row_max = jnp.max(score_matrix, axis=-1, keepdims=True)
    weights = jnp.exp(score_matrix - row_max)
    weights = weights / jnp.sum(weights, axis=-1, keepdims=True)
    rounded_values = weights.astype(jnp.bfloat16)
    final_output = jnp.einsum(
        "uwx,xue->wue", rounded_values, heads_value, preferred_element_type=jnp.float32
    )
    return (final_output, weights, rounded_values)


def attend_backward(
    queries, key_rows, value_rows, cotangent, final_output, weights, rounded_values
):
    query_row_block = queries.shape[0]
    key_row_block = key_rows.shape[0]
    heads_query = queries.reshape(query_row_block, HEADS, HEAD_SIZE)
    heads_key = key_rows.reshape(key_row_block, HEADS, HEAD_SIZE)
    heads_value = value_rows.reshape(key_row_block, HEADS, HEAD_SIZE)
    cotangent_heads = cotangent.reshape(query_row_block, HEADS, HEAD_SIZE)
    weight_gradient = jnp.einsum(
        "xfk,ifk->fxi", cotangent_heads, heads_value, preferred_element_type=jnp.float32
    )
    row_dots = jnp.sum(cotangent_heads.astype(jnp.float32) * final_output, axis=-1).T
    grad_scores = weights * (weight_gradient - row_dots[:, :, None]) * HEAD_SIZE ** (-0.5)
    gradient_rounded = grad_scores.astype(jnp.bfloat16)
    query_term = jnp.einsum(
        "uwx,xue->wue", gradient_rounded, heads_key, preferred_element_type=jnp.float32
    ).reshape(query_row_block, -1)
    key_term = jnp.einsum(
        "sxj,xsw->jsw", gradient_rounded, heads_query, preferred_element_type=jnp.float32
    ).reshape(key_row_block, -1)
    value_term = jnp.einsum(
        "sxj,xsw->jsw", rounded_values, cotangent_heads, preferred_element_type=jnp.float32
    ).reshape(key_row_block, -1)
    return (query_term, key_term, value_term)


def listed_mask(position, lists_row, rows):
    slots = position - HALF_WINDOW + jnp.arange(WINDOW_BLOCKS, dtype=jnp.int32)
    listed = jnp.any(lists_row[None, :] == slots[:, None], axis=1)
    return jnp.broadcast_to(listed[:, None], (WINDOW_BLOCKS, rows)).reshape(WINDOW_BLOCKS * rows)


def inside_mask(position, count, rows):
    slots = position - HALF_WINDOW + jnp.arange(WINDOW_BLOCKS, dtype=jnp.int32)
    inside = (slots >= 0) & (slots < count)
    return jnp.broadcast_to(inside[:, None], (WINDOW_BLOCKS, rows)).reshape(WINDOW_BLOCKS * rows)


def body(
    video_query,
    video_keys,
    video_value,
    audio_query,
    audio_key,
    audio_value,
    video_cotangent,
    audio_cotangent,
    video_lists,
    audio_lists,
):
    position = lax.axis_index(("tower", "seq"))
    block_count = lax.axis_size(("tower", "seq"))
    video_row_block = video_query.shape[0]
    audio_rows = audio_query.shape[0]
    window_width = video_query.shape[1]
    own_blocks = (video_keys, video_value, audio_key, audio_value)
    window_pieces = []
    for window_slot_index in range(WINDOW_BLOCKS):
        offset = window_slot_index - HALF_WINDOW
        if offset == 0:
            window_pieces.append(own_blocks)
        else:
            window_pieces.append(
                from_behind(
                    (own_blocks[0], own_blocks[1], own_blocks[2], own_blocks[3]),
                    ("tower", "seq"),
                    -offset,
                )
            )
    window_keys = jnp.concatenate([member[0] for member in window_pieces], axis=0)
    value_window = jnp.concatenate([member[1] for member in window_pieces], axis=0)
    akey_window = jnp.concatenate([member[2] for member in window_pieces], axis=0)
    avalue_window = jnp.concatenate([member[3] for member in window_pieces], axis=0)
    self_keep = inside_mask(position, block_count, video_row_block)
    cross_keep = listed_mask(position, video_lists[0], audio_rows)
    audio_keep = listed_mask(position, audio_lists[0], video_row_block)
    self_res, self_weights, self_rounded = attend_forward(
        video_query, window_keys, value_window, self_keep
    )
    cross_res, cross_weights, cross_rounded = attend_forward(
        video_query, akey_window, avalue_window, cross_keep
    )
    audio_res, audio_weights, audio_rounded = attend_forward(
        audio_query, window_keys, value_window, audio_keep
    )
    video_output = (
        (self_res + cross_res).reshape(video_row_block, window_width).astype(jnp.bfloat16)
    )
    audio_output = audio_res.reshape(audio_rows, window_width).astype(jnp.bfloat16)
    self_q, self_key_rows, self_v = attend_backward(
        video_query,
        window_keys,
        value_window,
        video_cotangent,
        self_res,
        self_weights,
        self_rounded,
    )
    cross_q, cross_k, cross_v = attend_backward(
        video_query,
        akey_window,
        avalue_window,
        video_cotangent,
        cross_res,
        cross_weights,
        cross_rounded,
    )
    audio_q, audio_key_rows, audio_v = attend_backward(
        audio_query,
        window_keys,
        value_window,
        audio_cotangent,
        audio_res,
        audio_weights,
        audio_rounded,
    )
    video_query_grad = (self_q + cross_q).astype(jnp.bfloat16)
    audio_query_grad = audio_q.astype(jnp.bfloat16)
    shared_video_key = (
        (self_key_rows + audio_key_rows)
        .astype(jnp.bfloat16)
        .reshape(WINDOW_BLOCKS, video_row_block, window_width)
    )
    share_vvalue = (
        (self_v + audio_v)
        .astype(jnp.bfloat16)
        .reshape(WINDOW_BLOCKS, video_row_block, window_width)
    )
    share_akey = cross_k.astype(jnp.bfloat16).reshape(WINDOW_BLOCKS, audio_rows, window_width)
    share_avalue = cross_v.astype(jnp.bfloat16).reshape(WINDOW_BLOCKS, audio_rows, window_width)
    totals = [
        shared_video_key[HALF_WINDOW].astype(jnp.float32),
        share_vvalue[HALF_WINDOW].astype(jnp.float32),
        share_akey[HALF_WINDOW].astype(jnp.float32),
        share_avalue[HALF_WINDOW].astype(jnp.float32),
    ]
    for window_slot_index in range(WINDOW_BLOCKS):
        offset = window_slot_index - HALF_WINDOW
        if offset != 0:
            received = from_behind(
                (
                    shared_video_key[window_slot_index],
                    share_vvalue[window_slot_index],
                    share_akey[window_slot_index],
                    share_avalue[window_slot_index],
                ),
                ("tower", "seq"),
                offset,
            )
            totals = [
                running + incoming.astype(jnp.float32)
                for running, incoming in zip(totals, received)
            ]
    video_key_grad = totals[0].astype(jnp.bfloat16)
    video_value_grad = totals[1].astype(jnp.bfloat16)
    audio_key_grad = totals[2].astype(jnp.bfloat16)
    audio_value_grad = totals[3].astype(jnp.bfloat16)
    return (
        video_output,
        audio_output,
        video_query_grad,
        video_key_grad,
        video_value_grad,
        audio_query_grad,
        audio_key_grad,
        audio_value_grad,
    )


def solution(mesh):
    placed = (
        P(("clip", "tower", "seq"), None),
        P(("clip", "tower", "seq"), None),
        P(("clip", "tower", "seq"), None),
        P(("clip", "tower", "seq"), None),
        P(("clip", "tower", "seq"), None),
        P(("clip", "tower", "seq"), None),
        P(("clip", "tower", "seq"), None),
        P(("clip", "tower", "seq"), None),
        P(("clip", "tower", "seq"), None),
        P(("clip", "tower", "seq"), None),
    )
    return jax.shard_map(
        body,
        mesh=mesh,
        in_specs=placed,
        out_specs=(
            P(("clip", "tower", "seq"), None),
            P(("clip", "tower", "seq"), None),
            P(("clip", "tower", "seq"), None),
            P(("clip", "tower", "seq"), None),
            P(("clip", "tower", "seq"), None),
            P(("clip", "tower", "seq"), None),
            P(("clip", "tower", "seq"), None),
            P(("clip", "tower", "seq"), None),
        ),
        check_vma=False,
    )
```

profile of v0, /device:TPU:73, one launch (start us, length us, event | category | flops | bytes accessed | tf_op | source)
XLA Modules:
  0.0 381.2 jit_solution(1067045923856403293)
XLA Ops:
  0.7 9.8 %collective-permute-start.8 = (bf16[64,1536]{1,0:T(8,128)(2,1)}, bf16[64,1536]{1,0:T(8,128)(2,1)}, u32[]{:S(2)}, u32[]{:S(2)}) collective-permute-start(bf16[64,1536]{1,0:T(8,128)(2,1)} %param.15), channel_id=1, source_target_pairs={{1,0},{2,1},{3,2},{4,3},{5,4},{6,5},{7,6},{8,7},{9,8},{10,9},{11,1... | collective-permute-start | bytes 589832 | tf_op jit(solution)/shard_map/ppermute | solution.py:15
  10.5 1.9 collective-permute-start.7
  12.4 4.4 %collective-permute-start.6 = (bf16[64,1536]{1,0:T(8,128)(2,1)}, bf16[64,1536]{1,0:T(8,128)(2,1)}, u32[]{:S(2)}, u32[]{:S(2)}) collective-permute-start(bf16[64,1536]{1,0:T(8,128)(2,1)} %param.15), channel_id=1, source_target_pairs={{0,2},{1,3},{2,4},{3,5},{4,6},{5,7},{6,8},{7,9},{8,10},{9,11},{10,... | collective-permute-start | bytes 589832 | tf_op jit(solution)/shard_map/ppermute | solution.py:15
  17.9 4.0 %collective-permute-start.11 = (bf16[64,1536]{0,1:T(8,128)(2,1)S(1)}, bf16[64,1536]{0,1:T(8,128)(2,1)S(1)}, u32[]{:S(2)}, u32[]{:S(2)}) collective-permute-start(bf16[64,1536]{0,1:T(8,128)(2,1)S(1)} %copy.119), channel_id=1, source_target_pairs={{1,0},{2,1},{3,2},{4,3},{5,4},{6,5},{7,6},{8,7},{9,8},{10,9},{11,1... | collective-permute-start | bytes 589832 | tf_op jit(solution)/shard_map/ppermute | solution.py:15
  22.0 4.0 %collective-permute-start.10 = (bf16[64,1536]{0,1:T(8,128)(2,1)S(1)}, bf16[64,1536]{0,1:T(8,128)(2,1)S(1)}, u32[]{:S(2)}, u32[]{:S(2)}) collective-permute-start(bf16[64,1536]{0,1:T(8,128)(2,1)S(1)} %copy.119), channel_id=1, source_target_pairs={{0,1},{1,2},{2,3},{3,4},{4,5},{5,6},{6,7},{7,8},{8,9},{9,10},{10,1... | collective-permute-start | bytes 589832 | tf_op jit(solution)/shard_map/ppermute | solution.py:15
  28.9 5.2 %collective-permute-start.9 = (bf16[64,1536]{0,1:T(8,128)(2,1)S(1)}, bf16[64,1536]{0,1:T(8,128)(2,1)}, u32[]{:S(2)}, u32[]{:S(2)}) collective-permute-start(bf16[64,1536]{0,1:T(8,128)(2,1)S(1)} %copy.119), channel_id=1, source_target_pairs={{0,2},{1,3},{2,4},{3,5},{4,6},{5,7},{6,8},{7,9},{8,10},{9,11},{10,... | collective-permute-start | bytes 589832 | tf_op jit(solution)/shard_map/ppermute | solution.py:15
  34.2 6.4 %collective-permute-start.2 = (bf16[128,1536]{1,0:T(8,128)(2,1)S(1)}, bf16[128,1536]{1,0:T(8,128)(2,1)}, u32[]{:S(2)}, u32[]{:S(2)}) collective-permute-start(bf16[128,1536]{1,0:T(8,128)(2,1)S(1)} %copy-done.16), channel_id=1, source_target_pairs={{1,0},{2,1},{3,2},{4,3},{5,4},{6,5},{7,6},{8,7},{9,8},{10,9},{11,1... | collective-permute-start | bytes 1179656 | tf_op jit(solution)/shard_map/ppermute | solution.py:15
  44.8 17.9 %collective-permute-done.11 = bf16[64,1536]{0,1:T(8,128)(2,1)S(1)} collective-permute-done((bf16[64,1536]{0,1:T(8,128)(2,1)S(1)}, bf16[64,1536]{0,1:T(8,128)(2,1)S(1)}, u32[]{:S(2)}, u32[]{:S(2)}) %collective-permute-start.11) | collective-permute-done | bytes 196640 | tf_op jit(solution)/shard_map/ppermute | solution.py:15
  62.7 100.3 %collective-permute-start = (bf16[128,1536]{1,0:T(8,128)(2,1)S(1)}, bf16[128,1536]{1,0:T(8,128)(2,1)}, u32[]{:S(2)}, u32[]{:S(2)}) collective-permute-start(bf16[128,1536]{1,0:T(8,128)(2,1)S(1)} %copy-done.16), channel_id=1, source_target_pairs={{0,2},{1,3},{2,4},{3,5},{4,6},{5,7},{6,8},{7,9},{8,10},{9,11},{10,... | collective-permute-start | bytes 1179656 | tf_op jit(solution)/shard_map/ppermute | solution.py:15
  163.0 3.3 collective-permute-start.5
  166.3 5.0 %collective-permute-start.4 = (bf16[128,1536]{0,1:T(8,128)(2,1)S(1)}, bf16[128,1536]{0,1:T(8,128)(2,1)}, u32[]{:S(2)}, u32[]{:S(2)}) collective-permute-start(bf16[128,1536]{0,1:T(8,128)(2,1)S(1)} %copy.110), channel_id=1, source_target_pairs={{0,1},{1,2},{2,3},{3,4},{4,5},{5,6},{6,7},{7,8},{8,9},{9,10},{10,1... | collective-permute-start | bytes 1179656 | tf_op jit(solution)/shard_map/ppermute | solution.py:15
  175.0 2.8 convolution_bitcast_fusion
  178.2 5.3 %collective-permute-start.3 = (bf16[128,1536]{0,1:T(8,128)(2,1)S(1)}, bf16[128,1536]{0,1:T(8,128)(2,1)}, u32[]{:S(2)}, u32[]{:S(2)}) collective-permute-start(bf16[128,1536]{0,1:T(8,128)(2,1)S(1)} %copy.110), channel_id=1, source_target_pairs={{0,2},{1,3},{2,4},{3,5},{4,6},{5,7},{6,8},{7,9},{8,10},{9,11},{10,... | collective-permute-start | bytes 1179656 | tf_op jit(solution)/shard_map/ppermute | solution.py:15
  186.6 3.1 collective-permute-start.23
  189.6 13.8 %collective-permute-done = bf16[128,1536]{1,0:T(8,128)(2,1)} collective-permute-done((bf16[128,1536]{1,0:T(8,128)(2,1)S(1)}, bf16[128,1536]{1,0:T(8,128)(2,1)}, u32[]{:S(2)}, u32[]{:S(2)}) %collective-permute-start) | collective-permute-done | bytes 393248 | tf_op jit(solution)/shard_map/ppermute | solution.py:15
  208.4 2.1 collective-permute-start.21
  210.5 35.8 %collective-permute-done.3 = bf16[128,1536]{0,1:T(8,128)(2,1)} collective-permute-done((bf16[128,1536]{0,1:T(8,128)(2,1)S(1)}, bf16[128,1536]{0,1:T(8,128)(2,1)}, u32[]{:S(2)}, u32[]{:S(2)}) %collective-permute-start.3) | collective-permute-done | bytes 393248 | tf_op jit(solution)/shard_map/ppermute | solution.py:15
  247.7 3.1 fusion.74
  250.8 4.2 %fusion.69 = f32[12,512,128]{1,2,0:T(8,128)} fusion(bf16[128,12,128]{0,2,1:T(8,128)(2,1)S(1)} %bitcast.240, f32[12,128,512]{1,2,0:T(8,128)} %get-tuple-element.56, f32[12,128]{1,0:T(8,128)S(1)} %get-tuple-element.55), kind=kOutput, calls=%fused_computation.109 | convolution fusion | flops 202899456 | bytes 6690816 | tf_op jit(solution)/shard_map/sxj,xsw->jsw/dot_general | solution.py:59
  262.7 4.2 %multiply_reduce_fusion = (f32[64,12]{0,1:T(8,128)}, bf16[12,8,8,128]{3,2,1,0:T(8,128)(2,1)}) fusion(bf16[512,12,128]{0,2,1:T(8,128)(2,1)} %bitcast.226, f32[12,64]{1,0:T(8,128)S(1)} %get-tuple-element.59, f32[12,512,64]{1,2,0:T(8,128)S(1)} %multiply_select_fusion.2, bf16[64,1536]{1,0:T(8,128)(2,1)S(1)} %copy-done), kind=kOutput, calls=%fused_computation.74 | convolution fusion | flops 102236672 | bytes 3545088 | tf_op jit(solution)/shard_map/uwx,xue->wue/dot_general | solution.py:32
  266.9 2.5 fusion.12
  272.3 2.3 fusion.82
  277.8 2.8 fusion.26
  285.6 6.4 %collective-permute-start.13 = (bf16[128,1536]{1,0:T(8,128)(2,1)}, bf16[128,1536]{1,0:T(8,128)(2,1)}, u32[]{:S(2)}, u32[]{:S(2)}) collective-permute-start(bf16[128,1536]{1,0:T(8,128)(2,1)} %copy.144), channel_id=1, source_target_pairs={{1,0},{2,1},{3,2},{4,3},{5,4},{6,5},{7,6},{8,7},{9,8},{10,9},{11,1... | collective-permute-start | bytes 1179656 | tf_op jit(solution)/shard_map/ppermute | solution.py:15
  292.0 4.7 %fusion.27 = bf16[512,12,128]{0,2,1:T(8,128)(2,1)} fusion(f32[12,512,128]{1,2,0:T(8,128)} %fusion.69, f32[12,64]{1,0:T(8,128)S(1)} %get-tuple-element.59, f32[12,512,64]{1,2,0:T(8,128)S(1)} %multiply_select_fusion.2, bf16[64,1536]{1,0:T(8,128)(2,1)S(1)} %copy-done), kind=kOutput, calls=%fused_computation.36 | convolution fusion | flops 103417088 | bytes 6491136 | tf_op jit(solution)/shard_map/sxj,xsw->jsw/dot_general | solution.py:59
  296.7 2.5 fusion.72
  302.7 8.2 %collective-permute-start.20 = (bf16[64,1536]{1,0:T(8,128)(2,1)}, bf16[64,1536]{1,0:T(8,128)(2,1)S(1)}, u32[]{:S(2)}, u32[]{:S(2)}) collective-permute-start(bf16[64,1536]{1,0:T(8,128)(2,1)} %bitcast.213), channel_id=1, source_target_pairs={{0,1},{1,2},{2,3},{3,4},{4,5},{5,6},{6,7},{7,8},{8,9},{9,10},{10,1... | collective-permute-start | bytes 589832 | tf_op jit(solution)/shard_map/ppermute | solution.py:15
  317.9 2.0 copy.151
  324.0 5.5 %collective-permute-start.17 = (bf16[128,1536]{1,0:T(8,128)(2,1)}, bf16[128,1536]{1,0:T(8,128)(2,1)S(1)}, u32[]{:S(2)}, u32[]{:S(2)}) collective-permute-start(bf16[128,1536]{1,0:T(8,128)(2,1)} %copy.151), channel_id=1, source_target_pairs={{0,1},{1,2},{2,3},{3,4},{4,5},{5,6},{6,7},{7,8},{8,9},{9,10},{10,1... | collective-permute-start | bytes 1179656 | tf_op jit(solution)/shard_map/ppermute | solution.py:15
  337.0 9.7 %collective-permute-done.12 = bf16[128,1536]{1,0:T(8,128)(2,1)S(1)} collective-permute-done((bf16[128,1536]{1,0:T(8,128)(2,1)}, bf16[128,1536]{1,0:T(8,128)(2,1)S(1)}, u32[]{:S(2)}, u32[]{:S(2)}) %collective-permute-start.12) | collective-permute-done | bytes 393248 | tf_op jit(solution)/shard_map/ppermute | solution.py:15
  346.7 2.0 add_convert_fusion.3
  348.7 31.6 %collective-permute-done.16 = bf16[128,1536]{1,0:T(8,128)(2,1)S(1)} collective-permute-done((bf16[128,1536]{1,0:T(8,128)(2,1)}, bf16[128,1536]{1,0:T(8,128)(2,1)S(1)}, u32[]{:S(2)}, u32[]{:S(2)}) %collective-permute-start.16) | collective-permute-done | bytes 393248 | tf_op jit(solution)/shard_map/ppermute | solution.py:15
  (153 shorter events, 63.3 us)
Async XLA Ops:
  0.6 262.0 %copy-start = (bf16[64,1536]{1,0:T(8,128)(2,1)S(1)}, bf16[64,1536]{1,0:T(8,128)(2,1)}, u32[]{:S(2)}) copy-start(bf16[64,1536]{1,0:T(8,128)(2,1)} %param.17) | copy-start | bytes 589828
  0.7 41.8 %copy-start.26 = (bf16[64,1536]{1,0:T(8,128)(2,1)S(1)}, bf16[64,1536]{1,0:T(8,128)(2,1)}, u32[]{:S(2)}) copy-start(bf16[64,1536]{1,0:T(8,128)(2,1)} %param.15) | copy-start | bytes 589828
  0.7 27.5 %copy-start.28 = (s32[1,2]{1,0:T(1,128)S(1)}, s32[1,2]{1,0:T(1,128)}, u32[]{:S(2)}) copy-start(s32[1,2]{1,0:T(1,128)} %param.19) | copy-start | bytes 28
  0.7 27.5 %copy-start.29 = (s32[1,2]{1,0:T(1,128)S(1)}, s32[1,2]{1,0:T(1,128)}, u32[]{:S(2)}) copy-start(s32[1,2]{1,0:T(1,128)} %param.18) | copy-start | bytes 28
  0.7 27.9 %copy-start.21 = (bf16[128,1536]{1,0:T(8,128)(2,1)S(1)}, bf16[128,1536]{1,0:T(8,128)(2,1)}, u32[]{:S(2)}) copy-start(bf16[128,1536]{1,0:T(8,128)(2,1)} %param.11) | copy-start | bytes 1179652
  0.7 33.5 %copy-start.16 = (bf16[128,1536]{1,0:T(8,128)(2,1)S(1)}, bf16[128,1536]{1,0:T(8,128)(2,1)}, u32[]{:S(2)}) copy-start(bf16[128,1536]{1,0:T(8,128)(2,1)} %param.12) | copy-start | bytes 1179652
  0.7 28.2 %collective-permute-start.8 = (bf16[64,1536]{1,0:T(8,128)(2,1)}, bf16[64,1536]{1,0:T(8,128)(2,1)}, u32[]{:S(2)}, u32[]{:S(2)}) collective-permute-start(bf16[64,1536]{1,0:T(8,128)(2,1)} %param.15), channel_id=1, source_target_pairs={{1,0},{2,1},{3,2},{4,3},{5,4},{6,5},{7,6},{8,7},{9,8},{10,9},{11,1... | collective-permute-start | bytes 589832 | tf_op jit(solution)/shard_map/ppermute | solution.py:15
  10.5 23.6 %collective-permute-start.7 = (bf16[64,1536]{1,0:T(8,128)(2,1)}, bf16[64,1536]{1,0:T(8,128)(2,1)}, u32[]{:S(2)}, u32[]{:S(2)}) collective-permute-start(bf16[64,1536]{1,0:T(8,128)(2,1)} %param.15), channel_id=1, source_target_pairs={{0,1},{1,2},{2,3},{3,4},{4,5},{5,6},{6,7},{7,8},{8,9},{9,10},{10,1... | collective-permute-start | bytes 589832 | tf_op jit(solution)/shard_map/ppermute | solution.py:15
  12.4 28.1 %collective-permute-start.6 = (bf16[64,1536]{1,0:T(8,128)(2,1)}, bf16[64,1536]{1,0:T(8,128)(2,1)}, u32[]{:S(2)}, u32[]{:S(2)}) collective-permute-start(bf16[64,1536]{1,0:T(8,128)(2,1)} %param.15), channel_id=1, source_target_pairs={{0,2},{1,3},{2,4},{3,5},{4,6},{5,7},{6,8},{7,9},{8,10},{9,11},{10,... | collective-permute-start | bytes 589832 | tf_op jit(solution)/shard_map/ppermute | solution.py:15
  17.9 44.7 %collective-permute-start.11 = (bf16[64,1536]{0,1:T(8,128)(2,1)S(1)}, bf16[64,1536]{0,1:T(8,128)(2,1)S(1)}, u32[]{:S(2)}, u32[]{:S(2)}) collective-permute-start(bf16[64,1536]{0,1:T(8,128)(2,1)S(1)} %copy.119), channel_id=1, source_target_pairs={{1,0},{2,1},{3,2},{4,3},{5,4},{6,5},{7,6},{8,7},{9,8},{10,9},{11,1... | collective-permute-start | bytes 589832 | tf_op jit(solution)/shard_map/ppermute | solution.py:15
  22.0 141.0 %collective-permute-start.10 = (bf16[64,1536]{0,1:T(8,128)(2,1)S(1)}, bf16[64,1536]{0,1:T(8,128)(2,1)S(1)}, u32[]{:S(2)}, u32[]{:S(2)}) collective-permute-start(bf16[64,1536]{0,1:T(8,128)(2,1)S(1)} %copy.119), channel_id=1, source_target_pairs={{0,1},{1,2},{2,3},{3,4},{4,5},{5,6},{6,7},{7,8},{8,9},{9,10},{10,1... | collective-permute-start | bytes 589832 | tf_op jit(solution)/shard_map/ppermute | solution.py:15
  28.2 230.5 %copy-start.1 = (bf16[128,1536]{0,1:T(8,128)(2,1)}, bf16[128,1536]{0,1:T(8,128)(2,1)S(1)}, u32[]{:S(2)}) copy-start(bf16[128,1536]{0,1:T(8,128)(2,1)S(1)} %copy.114) | copy-start | bytes 1179652
  28.9 137.4 %collective-permute-start.9 = (bf16[64,1536]{0,1:T(8,128)(2,1)S(1)}, bf16[64,1536]{0,1:T(8,128)(2,1)}, u32[]{:S(2)}, u32[]{:S(2)}) collective-permute-start(bf16[64,1536]{0,1:T(8,128)(2,1)S(1)} %copy.119), channel_id=1, source_target_pairs={{0,2},{1,3},{2,4},{3,5},{4,6},{5,7},{6,8},{7,9},{8,10},{9,11},{10,... | collective-permute-start | bytes 589832 | tf_op jit(solution)/shard_map/ppermute | solution.py:15
  34.2 144.0 %collective-permute-start.2 = (bf16[128,1536]{1,0:T(8,128)(2,1)S(1)}, bf16[128,1536]{1,0:T(8,128)(2,1)}, u32[]{:S(2)}, u32[]{:S(2)}) collective-permute-start(bf16[128,1536]{1,0:T(8,128)(2,1)S(1)} %copy-done.16), channel_id=1, source_target_pairs={{1,0},{2,1},{3,2},{4,3},{5,4},{6,5},{7,6},{8,7},{9,8},{10,9},{11,1... | collective-permute-start | bytes 1179656 | tf_op jit(solution)/shard_map/ppermute | solution.py:15
  40.5 146.0 %collective-permute-start.1 = (bf16[128,1536]{1,0:T(8,128)(2,1)S(1)}, bf16[128,1536]{1,0:T(8,128)(2,1)}, u32[]{:S(2)}, u32[]{:S(2)}) collective-permute-start(bf16[128,1536]{1,0:T(8,128)(2,1)S(1)} %copy-done.16), channel_id=1, source_target_pairs={{0,1},{1,2},{2,3},{3,4},{4,5},{5,6},{6,7},{7,8},{8,9},{9,10},{10,1... | collective-permute-start | bytes 1179656 | tf_op jit(solution)/shard_map/ppermute | solution.py:15
  62.7 103.6 %copy-start.18 = (bf16[64,1536]{0,1:T(8,128)(2,1)}, bf16[64,1536]{0,1:T(8,128)(2,1)S(1)}, u32[]{:S(2)}) copy-start(bf16[64,1536]{0,1:T(8,128)(2,1)S(1)} %collective-permute-done.11) | copy-start | bytes 589828
  62.7 140.8 %collective-permute-start = (bf16[128,1536]{1,0:T(8,128)(2,1)S(1)}, bf16[128,1536]{1,0:T(8,128)(2,1)}, u32[]{:S(2)}, u32[]{:S(2)}) collective-permute-start(bf16[128,1536]{1,0:T(8,128)(2,1)S(1)} %copy-done.16), channel_id=1, source_target_pairs={{0,2},{1,3},{2,4},{3,5},{4,6},{5,7},{6,8},{7,9},{8,10},{9,11},{10,... | collective-permute-start | bytes 1179656 | tf_op jit(solution)/shard_map/ppermute | solution.py:15
  163.0 45.3 %collective-permute-start.5 = (bf16[128,1536]{0,1:T(8,128)(2,1)S(1)}, bf16[128,1536]{0,1:T(8,128)(2,1)}, u32[]{:S(2)}, u32[]{:S(2)}) collective-permute-start(bf16[128,1536]{0,1:T(8,128)(2,1)S(1)} %copy.110), channel_id=1, source_target_pairs={{1,0},{2,1},{3,2},{4,3},{5,4},{6,5},{7,6},{8,7},{9,8},{10,9},{11,1... | collective-permute-start | bytes 1179656 | tf_op jit(solution)/shard_map/ppermute | solution.py:15
  166.3 44.1 %collective-permute-start.4 = (bf16[128,1536]{0,1:T(8,128)(2,1)S(1)}, bf16[128,1536]{0,1:T(8,128)(2,1)}, u32[]{:S(2)}, u32[]{:S(2)}) collective-permute-start(bf16[128,1536]{0,1:T(8,128)(2,1)S(1)} %copy.110), channel_id=1, source_target_pairs={{0,1},{1,2},{2,3},{3,4},{4,5},{5,6},{6,7},{7,8},{8,9},{9,10},{10,1... | collective-permute-start | bytes 1179656 | tf_op jit(solution)/shard_map/ppermute | solution.py:15
  178.2 68.1 %collective-permute-start.3 = (bf16[128,1536]{0,1:T(8,128)(2,1)S(1)}, bf16[128,1536]{0,1:T(8,128)(2,1)}, u32[]{:S(2)}, u32[]{:S(2)}) collective-permute-start(bf16[128,1536]{0,1:T(8,128)(2,1)S(1)} %copy.110), channel_id=1, source_target_pairs={{0,2},{1,3},{2,4},{3,5},{4,6},{5,7},{6,8},{7,9},{8,10},{9,11},{10,... | collective-permute-start | bytes 1179656 | tf_op jit(solution)/shard_map/ppermute | solution.py:15
  186.6 116.2 %collective-permute-start.23 = (bf16[64,1536]{1,0:T(8,128)(2,1)}, bf16[64,1536]{1,0:T(8,128)(2,1)}, u32[]{:S(2)}, u32[]{:S(2)}) collective-permute-start(bf16[64,1536]{1,0:T(8,128)(2,1)} %bitcast.210), channel_id=1, source_target_pairs={{0,1},{1,2},{2,3},{3,4},{4,5},{5,6},{6,7},{7,8},{8,9},{9,10},{10,1... | collective-permute-start | bytes 589832 | tf_op jit(solution)/shard_map/ppermute | solution.py:15
  203.5 107.5 %collective-permute-start.22 = (bf16[64,1536]{1,0:T(8,128)(2,1)}, bf16[64,1536]{1,0:T(8,128)(2,1)}, u32[]{:S(2)}, u32[]{:S(2)}) collective-permute-start(bf16[64,1536]{1,0:T(8,128)(2,1)} %bitcast.211), channel_id=1, source_target_pairs={{1,0},{2,1},{3,2},{4,3},{5,4},{6,5},{7,6},{8,7},{9,8},{10,9},{11,1... | collective-permute-start | bytes 589832 | tf_op jit(solution)/shard_map/ppermute | solution.py:15
  208.4 104.5 %collective-permute-start.21 = (bf16[64,1536]{1,0:T(8,128)(2,1)}, bf16[64,1536]{1,0:T(8,128)(2,1)}, u32[]{:S(2)}, u32[]{:S(2)}) collective-permute-start(bf16[64,1536]{1,0:T(8,128)(2,1)} %bitcast.212), channel_id=1, source_target_pairs={{2,0},{3,1},{4,2},{5,3},{6,4},{7,5},{8,6},{9,7},{10,8},{11,9},{12,... | collective-permute-start | bytes 589832 | tf_op jit(solution)/shard_map/ppermute | solution.py:15
  282.7 52.3 %collective-permute-start.14 = (bf16[128,1536]{1,0:T(8,128)(2,1)}, bf16[128,1536]{1,0:T(8,128)(2,1)}, u32[]{:S(2)}, u32[]{:S(2)}) collective-permute-start(bf16[128,1536]{1,0:T(8,128)(2,1)} %copy.145), channel_id=1, source_target_pairs={{0,1},{1,2},{2,3},{3,4},{4,5},{5,6},{6,7},{7,8},{8,9},{9,10},{10,1... | collective-permute-start | bytes 1179656 | tf_op jit(solution)/shard_map/ppermute | solution.py:15
  285.6 51.4 %collective-permute-start.13 = (bf16[128,1536]{1,0:T(8,128)(2,1)}, bf16[128,1536]{1,0:T(8,128)(2,1)}, u32[]{:S(2)}, u32[]{:S(2)}) collective-permute-start(bf16[128,1536]{1,0:T(8,128)(2,1)} %copy.144), channel_id=1, source_target_pairs={{1,0},{2,1},{3,2},{4,3},{5,4},{6,5},{7,6},{8,7},{9,8},{10,9},{11,1... | collective-permute-start | bytes 1179656 | tf_op jit(solution)/shard_map/ppermute | solution.py:15
  302.7 19.3 %collective-permute-start.20 = (bf16[64,1536]{1,0:T(8,128)(2,1)}, bf16[64,1536]{1,0:T(8,128)(2,1)S(1)}, u32[]{:S(2)}, u32[]{:S(2)}) collective-permute-start(bf16[64,1536]{1,0:T(8,128)(2,1)} %bitcast.213), channel_id=1, source_target_pairs={{0,1},{1,2},{2,3},{3,4},{4,5},{5,6},{6,7},{7,8},{8,9},{9,10},{10,1... | collective-permute-start | bytes 589832 | tf_op jit(solution)/shard_map/ppermute | solution.py:15
  311.0 13.0 %collective-permute-start.19 = (bf16[64,1536]{1,0:T(8,128)(2,1)}, bf16[64,1536]{1,0:T(8,128)(2,1)}, u32[]{:S(2)}, u32[]{:S(2)}) collective-permute-start(bf16[64,1536]{1,0:T(8,128)(2,1)} %bitcast.214), channel_id=1, source_target_pairs={{1,0},{2,1},{3,2},{4,3},{5,4},{6,5},{7,6},{8,7},{9,8},{10,9},{11,1... | collective-permute-start | bytes 589832 | tf_op jit(solution)/shard_map/ppermute | solution.py:15
  312.9 18.4 %collective-permute-start.18 = (bf16[64,1536]{1,0:T(8,128)(2,1)}, bf16[64,1536]{1,0:T(8,128)(2,1)}, u32[]{:S(2)}, u32[]{:S(2)}) collective-permute-start(bf16[64,1536]{1,0:T(8,128)(2,1)} %bitcast.215), channel_id=1, source_target_pairs={{2,0},{3,1},{4,2},{5,3},{6,4},{7,5},{8,6},{9,7},{10,8},{11,9},{12,... | collective-permute-start | bytes 589832 | tf_op jit(solution)/shard_map/ppermute | solution.py:15
  322.1 24.6 %collective-permute-start.12 = (bf16[128,1536]{1,0:T(8,128)(2,1)}, bf16[128,1536]{1,0:T(8,128)(2,1)S(1)}, u32[]{:S(2)}, u32[]{:S(2)}) collective-permute-start(bf16[128,1536]{1,0:T(8,128)(2,1)} %copy.142), channel_id=1, source_target_pairs={{2,0},{3,1},{4,2},{5,3},{6,4},{7,5},{8,6},{9,7},{10,8},{11,9},{12,... | collective-permute-start | bytes 1179656 | tf_op jit(solution)/shard_map/ppermute | solution.py:15
  324.0 24.7 %collective-permute-start.17 = (bf16[128,1536]{1,0:T(8,128)(2,1)}, bf16[128,1536]{1,0:T(8,128)(2,1)S(1)}, u32[]{:S(2)}, u32[]{:S(2)}) collective-permute-start(bf16[128,1536]{1,0:T(8,128)(2,1)} %copy.151), channel_id=1, source_target_pairs={{0,1},{1,2},{2,3},{3,4},{4,5},{5,6},{6,7},{7,8},{8,9},{9,10},{10,1... | collective-permute-start | bytes 1179656 | tf_op jit(solution)/shard_map/ppermute | solution.py:15
  331.3 48.9 %collective-permute-start.16 = (bf16[128,1536]{1,0:T(8,128)(2,1)}, bf16[128,1536]{1,0:T(8,128)(2,1)S(1)}, u32[]{:S(2)}, u32[]{:S(2)}) collective-permute-start(bf16[128,1536]{1,0:T(8,128)(2,1)} %copy.150), channel_id=1, source_target_pairs={{1,0},{2,1},{3,2},{4,3},{5,4},{6,5},{7,6},{8,7},{9,8},{10,9},{11,1... | collective-permute-start | bytes 1179656 | tf_op jit(solution)/shard_map/ppermute | solution.py:15
  335.0 45.2 %collective-permute-start.15 = (bf16[128,1536]{1,0:T(8,128)(2,1)}, bf16[128,1536]{1,0:T(8,128)(2,1)S(1)}, u32[]{:S(2)}, u32[]{:S(2)}) collective-permute-start(bf16[128,1536]{1,0:T(8,128)(2,1)} %copy.148), channel_id=1, source_target_pairs={{2,0},{3,1},{4,2},{5,3},{6,4},{7,5},{8,6},{9,7},{10,8},{11,9},{12,... | collective-permute-start | bytes 1179656 | tf_op jit(solution)/shard_map/ppermute | solution.py:15
  (29 other events, 148.2 us)
where the time goes:
time: 383 us; the launch traced here: 381 us
  starting transfers between devices  190 us (50%)
  waiting for transfers between devices  111 us (29%)
  matrix products  37.2 us (10%)
  local copies, waits for them, and re-layouts  26.9 us (7%)
  other arithmetic  15 us (4%)
    ppermute x24, starting transfers between devices, from_behind(): return lax.ppermute(block, axis, route)  190 us
    ppermute x24, waiting for transfers between devices, from_behind(): return lax.ppermute(block, axis, route)  111 us
    dot_general x3, matrix products, attend_backward(): jnp.einsum('sxj,xsw->jsw', rounded_values, cotangent_heads, preferred_ele...  9.36 us
    dot_general x3, matrix products, attend_forward(): jnp.einsum('uwx,xue->wue', rounded_values, heads_value, preferred_element...  8.34 us
    unnamed x80, local copies, waits for them, and re-layouts  7.85 us
  transfers between devices with their start and end apart: 24, of which 6 were waited for; matrix products, arithmetic and copies ran while one was open for 20% of the time, Pallas kernels for 0%

commit v1 on v0

v1 whole, which is shorter than its diff:
```python
import functools

import jax
import jax.numpy as jnp
from jax import lax
from jax.experimental import pallas as pl
from jax.experimental.pallas import tpu as pltpu
from jax.sharding import Mesh
from jax.sharding import PartitionSpec as P

HEADS = 12
HEAD_SIZE = 128
WINDOW_BLOCKS = 4
HALF_WINDOW = 2
MEMBERS = 4
GROUP_HEADS = HEADS // MEMBERS
GROUP_WIDTH = GROUP_HEADS * HEAD_SIZE
EXTENDED = MEMBERS + WINDOW_BLOCKS - 1
VIDEO = 128
AUDIO = 64
STACK = VIDEO + AUDIO
ROWS = 2 * STACK
LIST_ROWS = 16
SCALE = HEAD_SIZE ** -0.5
LOG2_SCALE = SCALE * 1.4426950408889634
MASKED = -1e30
PARAMS = pltpu.CompilerParams(vmem_limit_bytes=40 * 1024 * 1024)


def product(left, right, left_dim, right_dim):
    return lax.dot_general(
        left,
        right,
        (((left_dim,), (right_dim,)), ((), ())),
        preferred_element_type=jnp.float32,
    )


def pack_kernel(
    video_list, audio_list, vq, vk, vv, aq, ak, av, vg, ag, kv_out, qg_out
):
    video_first = jnp.full((8, GROUP_WIDTH), video_list[0, 0].astype(jnp.float32))
    audio_first = jnp.full((8, GROUP_WIDTH), audio_list[0, 0].astype(jnp.float32))
    firsts = jnp.concatenate([video_first, audio_first], axis=0).astype(jnp.bfloat16)
    for member in range(MEMBERS):
        columns = slice(member * GROUP_WIDTH, (member + 1) * GROUP_WIDTH)
        kv_out[member, 0:128] = vk[:, columns]
        kv_out[member, 128:256] = vv[:, columns]
        kv_out[member, 256:320] = ak[:, columns]
        kv_out[member, 320:384] = av[:, columns]
        qg_out[member, 0:128] = vq[:, columns]
        qg_out[member, 128:192] = aq[:, columns]
        qg_out[member, 192:320] = vg[:, columns]
        qg_out[member, 320:384] = ag[:, columns]
        qg_out[member, 384:400] = firsts


def unpack_kernel(kv, qg, vo, ao, vqg, vkg, vvg, aqg, akg, avg):
    for member in range(MEMBERS):
        columns = slice(member * GROUP_WIDTH, (member + 1) * GROUP_WIDTH)
        vkg[:, columns] = kv[member, 0:128]
        vvg[:, columns] = kv[member, 128:256]
        akg[:, columns] = kv[member, 256:320]
        avg[:, columns] = kv[member, 320:384]
        vo[:, columns] = qg[member, 0:128]
        ao[:, columns] = qg[member, 128:192]
        vqg[:, columns] = qg[member, 192:320]
        aqg[:, columns] = qg[member, 320:384]


def merge_kernel(own, from_after, from_before, out):
    out[0] = (own[0] + from_before[...].astype(jnp.float32)).astype(jnp.bfloat16)
    out[1] = own[1].astype(jnp.bfloat16)
    out[2] = (own[2] + from_after[0].astype(jnp.float32)).astype(jnp.bfloat16)
    out[3] = (own[3] + from_after[1].astype(jnp.float32)).astype(jnp.bfloat16)


def weights_of(scaled):
    top = jnp.max(scaled, axis=1, keepdims=True)
    powers = jnp.exp2(scaled - top)
    return powers * (1.0 / jnp.sum(powers, axis=1, keepdims=True))


def attention_kernel(
    last_group,
    group_ref,
    kv,
    qg,
    before,
    after,
    qg_out,
    kv_out,
    before_out,
    after_out,
    vk,
    vv,
    ak,
    av,
    vk_sum,
    vv_sum,
    ak_sum,
    av_sum,
):
    group = group_ref[0]
    for block in range(EXTENDED):
        if block < HALF_WINDOW:
            source = before.at[block]
        elif block < HALF_WINDOW + MEMBERS:
            source = kv.at[block - HALF_WINDOW]
        else:
            source = after
        vk[block * VIDEO : (block + 1) * VIDEO] = source[0:128]
        vv[block * VIDEO : (block + 1) * VIDEO] = source[128:256]
        ak[block * AUDIO : (block + 1) * AUDIO] = source[256:320]
        av[block * AUDIO : (block + 1) * AUDIO] = source[320:384]
    vk_sum[...] = jnp.zeros_like(vk_sum)
    vv_sum[...] = jnp.zeros_like(vv_sum)
    ak_sum[...] = jnp.zeros_like(ak_sum)
    av_sum[...] = jnp.zeros_like(av_sum)
    bias_before = jnp.where(group == 0, MASKED, 0.0)
    bias_after = jnp.where(group == last_group, MASKED, 0.0)

    for member in range(MEMBERS):
        window_start = group * MEMBERS + member - HALF_WINDOW
        firsts = qg[member, ROWS : ROWS + LIST_ROWS].astype(jnp.float32)
        video_slot = jnp.max(firsts[0:8]).astype(jnp.int32) - window_start
        audio_slot = jnp.max(firsts[8:16]).astype(jnp.int32) - window_start
        queries = qg[member, 0:STACK]
        cotangents = qg[member, STACK:ROWS]
        window = slice(member * VIDEO, (member + WINDOW_BLOCKS) * VIDEO)
        keys = vk[window]
        values = vv[window]

        scaled = product(queries, keys, 1, 1) * LOG2_SCALE
        video_parts, audio_parts = [], []
        for slot in range(WINDOW_BLOCKS):
            block = member + slot
            part = scaled[:, slot * VIDEO : (slot + 1) * VIDEO]
            video_part = part[0:VIDEO]
            if block < HALF_WINDOW:
                video_part = video_part + bias_before
            elif block >= HALF_WINDOW + MEMBERS:
                video_part = video_part + bias_after
            listed = (audio_slot == slot) | (audio_slot + 1 == slot)
            video_parts.append(video_part)
            audio_parts.append(part[VIDEO:STACK] + jnp.where(listed, 0.0, MASKED))
        weights = jnp.concatenate(
            [
                weights_of(jnp.concatenate(video_parts, axis=1)),
                weights_of(jnp.concatenate(audio_parts, axis=1)),
            ],
            axis=0,
        )
        rounded = weights.astype(jnp.bfloat16)
        result = product(rounded, values, 1, 0)
        row_dot = jnp.sum(cotangents.astype(jnp.float32) * result, axis=1, keepdims=True)
        weight_grad = product(cotangents, values, 1, 1)
        score_grad = (weights * (weight_grad - row_dot)).astype(jnp.bfloat16)
        query_term = product(score_grad, keys, 1, 0)
        vk_sum[window] += product(score_grad, queries, 0, 0)
        vv_sum[window] += product(rounded, cotangents, 0, 0)

        listed_rows = pl.ds(pl.multiple_of((member + video_slot) * AUDIO, AUDIO), 2 * AUDIO)
        cross_keys = ak[listed_rows]
        cross_values = av[listed_rows]
        video_queries = queries[0:VIDEO]
        video_cotangents = cotangents[0:VIDEO]
        cross_weights = weights_of(product(video_queries, cross_keys, 1, 1) * LOG2_SCALE)
        cross_rounded = cross_weights.astype(jnp.bfloat16)
        cross_result = product(cross_rounded, cross_values, 1, 0)
        cross_dot = jnp.sum(
            video_cotangents.astype(jnp.float32) * cross_result, axis=1, keepdims=True
        )
        cross_grad = product(video_cotangents, cross_values, 1, 1)
        cross_score_grad = (cross_weights * (cross_grad - cross_dot)).astype(jnp.bfloat16)
        cross_query_term = product(cross_score_grad, cross_keys, 1, 0)
        ak_sum[listed_rows] += product(cross_score_grad, video_queries, 0, 0)
        av_sum[listed_rows] += product(cross_rounded, video_cotangents, 0, 0)

        qg_out[member, 0:128] = (result[0:VIDEO] + cross_result).astype(jnp.bfloat16)
        qg_out[member, 128:192] = result[VIDEO:STACK].astype(jnp.bfloat16)
        qg_out[member, 192:320] = (
            (query_term[0:VIDEO] + cross_query_term) * SCALE
        ).astype(jnp.bfloat16)
        qg_out[member, 320:384] = (query_term[VIDEO:STACK] * SCALE).astype(jnp.bfloat16)

    for block in range(EXTENDED):
        if block < HALF_WINDOW:
            target = before_out.at[block]
        elif block < HALF_WINDOW + MEMBERS:
            target = kv_out.at[block - HALF_WINDOW]
        else:
            target = after_out
        video_rows = slice(block * VIDEO, (block + 1) * VIDEO)
        audio_rows = slice(block * AUDIO, (block + 1) * AUDIO)
        target[0:128] = (vk_sum[video_rows] * SCALE).astype(target.dtype)
        target[128:256] = vv_sum[video_rows].astype(target.dtype)
        target[256:320] = (ak_sum[audio_rows] * SCALE).astype(target.dtype)
        target[320:384] = av_sum[audio_rows].astype(target.dtype)


def whole(memory=pltpu.VMEM):
    return pl.BlockSpec(memory_space=memory)


def pack(video_lists, audio_lists, *arrays):
    return pl.pallas_call(
        pack_kernel,
        out_shape=(
            jax.ShapeDtypeStruct((MEMBERS, ROWS, GROUP_WIDTH), jnp.bfloat16),
            jax.ShapeDtypeStruct((MEMBERS, ROWS + LIST_ROWS, GROUP_WIDTH), jnp.bfloat16),
        ),
        in_specs=[whole(pltpu.SMEM)] * 2 + [whole()] * 8,
        out_specs=(whole(), whole()),
        compiler_params=PARAMS,
        name="pack",
    )(video_lists, audio_lists, *arrays)


def unpack(kv, qg):
    video = jax.ShapeDtypeStruct((VIDEO, HEADS * HEAD_SIZE), jnp.bfloat16)
    audio = jax.ShapeDtypeStruct((AUDIO, HEADS * HEAD_SIZE), jnp.bfloat16)
    shapes = (video, audio, video, video, video, audio, audio, audio)
    return pl.pallas_call(
        unpack_kernel,
        out_shape=shapes,
        in_specs=[whole()] * 2,
        out_specs=[whole()] * 8,
        compiler_params=PARAMS,
        name="unpack",
    )(kv, qg)


def merge(own, from_after, from_before):
    return pl.pallas_call(
        merge_kernel,
        out_shape=jax.ShapeDtypeStruct(own.shape, jnp.bfloat16),
        in_specs=[whole()] * 3,
        out_specs=whole(),
        compiler_params=PARAMS,
        name="merge",
    )(own, from_after, from_before)


def attention(groups, group, kv, qg, before, after):
    def head_block(*leading):
        zeros = (0,) * len(leading)
        return pl.BlockSpec(leading + (HEAD_SIZE,), lambda head: zeros + (head,))

    video_sum = pltpu.VMEM((EXTENDED * VIDEO, HEAD_SIZE), jnp.float32)
    audio_sum = pltpu.VMEM((EXTENDED * AUDIO, HEAD_SIZE), jnp.float32)
    video_rows = pltpu.VMEM((EXTENDED * VIDEO, HEAD_SIZE), jnp.bfloat16)
    audio_rows = pltpu.VMEM((EXTENDED * AUDIO, HEAD_SIZE), jnp.bfloat16)
    return pl.pallas_call(
        functools.partial(attention_kernel, groups - 1),
        grid=(GROUP_HEADS,),
        out_shape=(
            jax.ShapeDtypeStruct((MEMBERS, ROWS, GROUP_WIDTH), jnp.bfloat16),
            jax.ShapeDtypeStruct((MEMBERS, ROWS, GROUP_WIDTH), jnp.float32),
            jax.ShapeDtypeStruct((HALF_WINDOW, ROWS, GROUP_WIDTH), jnp.bfloat16),
            jax.ShapeDtypeStruct((ROWS, GROUP_WIDTH), jnp.bfloat16),
        ),
        in_specs=[
            whole(pltpu.SMEM),
            head_block(MEMBERS, ROWS),
            head_block(MEMBERS, ROWS + LIST_ROWS),
            head_block(HALF_WINDOW, ROWS),
            head_block(ROWS),
        ],
        out_specs=(
            head_block(MEMBERS, ROWS),
            head_block(MEMBERS, ROWS),
            head_block(HALF_WINDOW, ROWS),
            head_block(ROWS),
        ),
        scratch_shapes=[video_rows] * 2 + [audio_rows] * 2 + [video_sum] * 2 + [audio_sum] * 2,
        compiler_params=PARAMS,
        name="attention",
    )(group, kv, qg, before, after)


def to_group(block, groups, distance):
    route = [(i, i + distance) for i in range(groups) if 0 <= i + distance < groups]
    return lax.ppermute(block, ("tower", "group"), route)


def exchange(packed):
    return lax.all_to_all(packed, "member", 0, 0)


def body(
    video_query,
    video_keys,
    video_value,
    audio_query,
    audio_key,
    audio_value,
    video_cotangent,
    audio_cotangent,
    video_lists,
    audio_lists,
):
    groups = lax.axis_size(("tower", "group"))
    group = lax.axis_index(("tower", "group")).astype(jnp.int32).reshape(1)
    kv_packed, qg_packed = pack(
        video_lists,
        audio_lists,
        video_query,
        video_keys,
        video_value,
        audio_query,
        audio_key,
        audio_value,
        video_cotangent,
        audio_cotangent,
    )
    kv = exchange(kv_packed)
    before = to_group(kv[MEMBERS - HALF_WINDOW :], groups, 1)
    after = to_group(kv[0], groups, -1)
    qg = exchange(qg_packed)
    qg_part, kv_part, before_part, after_part = attention(
        groups, group, kv, qg, before, after
    )
    from_after = to_group(before_part, groups, -1)
    from_before = to_group(after_part, groups, 1)
    qg_back = exchange(qg_part)
    kv_back = exchange(merge(kv_part, from_after, from_before))
    return unpack(kv_back, qg_back)


def solution(mesh):
    shape = mesh.devices.shape
    fine = Mesh(
        mesh.devices.reshape(shape[0], shape[1], shape[2] // MEMBERS, MEMBERS),
        ("clip", "tower", "group", "member"),
    )
    placed = P(("clip", "tower", "group", "member"), None)
    return jax.shard_map(
        body,
        mesh=fine,
        in_specs=(placed,) * 10,
        out_specs=(placed,) * 8,
        check_vma=False,
    )
```

time: 383 us -> 185 us (0.48)
  the two profiles are of different devices: /device:TPU:73 before, /device:TPU:120 now
where the time goes in v1:
time: 185 us; the launch traced here: 184 us
  blocking collectives  73.2 us (40%)
  waiting for transfers between devices  52.3 us (28%)
  starting transfers between devices  21 us (11%)
  Pallas kernels  20.3 us (11%)
  local copies, waits for them, and re-layouts  16.3 us (9%)
    all_to_all x2, blocking collectives, exchange(): return lax.all_to_all(packed, 'member', 0, 0)  73.2 us
    all_to_all x2, waiting for transfers between devices, exchange(): return lax.all_to_all(packed, 'member', 0, 0)  44.3 us
    pallas_call x1, Pallas kernels, attention(): pl.pallas_call(functools.partial(attention_kernel, groups - 1), grid=(GRO...  17.8 us
    unnamed x36, local copies, waits for them, and re-layouts  14.6 us
    ppermute x4, starting transfers between devices, to_group(): return lax.ppermute(block, ('tower', 'group'), route)  13.8 us
    ppermute x4, waiting for transfers between devices, to_group(): return lax.ppermute(block, ('tower', 'group'), route)  8.05 us
    all_to_all x2, starting transfers between devices, exchange(): return lax.all_to_all(packed, 'member', 0, 0)  7.19 us
  transfers between devices with their start and end apart: 6, of which 4 were waited for; matrix products, arithmetic and copies ran while one was open for 1% of the time, Pallas kernels for 0%

profile of v1, /device:TPU:120, one launch (start us, length us, event | category | flops | bytes accessed | tf_op | source)
XLA Modules:
  0.0 183.8 jit_solution(3704304042940437736)
XLA Ops:
  0.6 1.0 copy-done.4
  1.6 1.0 copy-done.5
  2.6 1.0 copy-done.6
  3.6 1.0 copy-done.7
  4.6 0.9 copy-done.8
  5.6 0.9 copy-done.9
  6.5 0.9 copy-done.10
  7.4 0.9 copy-done.11
  8.3 0.7 copy-done.12
  9.0 0.7 copy-done.13
  9.6 0.7 pack.1
  10.4 39.8 %all_to_all.20.kv = bf16[4,384,384]{2,1,0:T(8,128)(2,1)S(1)} all-to-all(bf16[4,384,384]{2,1,0:T(8,128)(2,1)S(1)} %get-tuple-element.14), channel_id=1, replica_groups=mesh['clip'=2,'tower'=2,'group'=32,'member'=4] {'member'}, dimensions={0} | all-to-all | bytes 2359296 | tf_op jit(solution)/shard_map/all_to_all | solution.py:288
  50.2 3.5 %all-to-all-start.1 = ((bf16[4,400,384]{2,1,0:T(8,128)(2,1)}), bf16[4,400,384]{2,1,0:T(8,128)(2,1)S(1)}, u32[]{:S(2)}, u32[]{:S(2)}) async-start(bf16[4,400,384]{2,1,0:T(8,128)(2,1)} %copy-done.2), calls=%async_computation.1 | async-start | bytes 2457600 | tf_op jit(solution)/shard_map/all_to_all | solution.py:288
  53.8 0.9 slice.8
  54.7 2.6 %collective-permute-start = (bf16[2,384,384]{2,1,0:T(8,128)(2,1)}, bf16[2,384,384]{2,1,0:T(8,128)(2,1)S(1)}, u32[]{:S(2)}, u32[]{:S(2)}) collective-permute-start(bf16[2,384,384]{2,1,0:T(8,128)(2,1)} %slice.8), channel_id=1, source_target_pairs={{0,4},{4,8},{8,12},{12,16},{16,20},{20,24},{24,28},{28,32},{32,36}... | collective-permute-start | bytes 1769480 | tf_op jit(solution)/shard_map/ppermute | solution.py:284
  57.3 0.7 slice_bitcast_fusion
  58.0 3.2 %collective-permute-start.1 = (bf16[384,384]{1,0:T(8,128)(2,1)}, bf16[384,384]{1,0:T(8,128)(2,1)S(1)}, u32[]{:S(2)}, u32[]{:S(2)}) collective-permute-start(bf16[384,384]{1,0:T(8,128)(2,1)} %slice_bitcast_fusion), channel_id=1, source_target_pairs={{4,0},{8,4},{12,8},{16,12},{20,16},{24,20},{28,24},{32,28},{36,32}... | collective-permute-start | bytes 884744 | tf_op jit(solution)/shard_map/ppermute | solution.py:284
  61.3 27.7 %all-to-all-done.1.qg = bf16[4,400,384]{2,1,0:T(8,128)(2,1)S(1)} async-done(((bf16[4,400,384]{2,1,0:T(8,128)(2,1)}), bf16[4,400,384]{2,1,0:T(8,128)(2,1)S(1)}, u32[]{:S(2)}, u32[]{:S(2)}) %all-to-all-start.1) | async-done | bytes 1228832 | tf_op jit(solution)/shard_map/all_to_all | solution.py:288
  88.9 17.8 %attention.1 = (bf16[4,384,384]{2,1,0:T(8,128)(2,1)S(1)}, f32[4,384,384]{2,1,0:T(8,128)S(1)}, bf16[2,384,384]{2,1,0:T(8,128)(2,1)S(1)}, bf16[384,384]{1,0:T(8,128)(2,1)S(1)}) custom-call(s32[1]{0:T(128)} %bitcast.group_ref, bf16[4,384,384]{2,1,0:T(8,128)(2,1)S(1)} %all_to_all.20.kv, bf16[4,400,384]{2,1,0:T(8,128)(2,1)S(1)} %all-to-all-done.1.qg, ...), custom_call_target="tpu_custom_call" | custom-call | tf_op jit(solution)/shard_map/attention/pallas_call | solution.py:254
  106.7 1.4 copy-done
  108.2 1.0 copy-done.3
  109.2 0.8 copy-done.14
  110.0 0.7 copy-done.16
  110.7 3.7 %all-to-all-start.3 = ((bf16[4,384,384]{2,1,0:T(8,128)(2,1)}), bf16[4,384,384]{2,1,0:T(8,128)(2,1)S(1)}, u32[]{:S(2)}, u32[]{:S(2)}) async-start(bf16[4,384,384]{2,1,0:T(8,128)(2,1)} %copy-done.3), calls=%async_computation.3 | async-start | bytes 2359296 | tf_op jit(solution)/shard_map/all_to_all | solution.py:288
  114.4 1.9 %collective-permute-start.2 = (bf16[2,384,384]{2,1,0:T(8,128)(2,1)S(1)}, bf16[2,384,384]{2,1,0:T(8,128)(2,1)S(1)}, u32[]{:S(2)}, u32[]{:S(2)}) collective-permute-start(bf16[2,384,384]{2,1,0:T(8,128)(2,1)S(1)} %copy-done.15), channel_id=1, source_target_pairs={{4,0},{8,4},{12,8},{16,12},{20,16},{24,20},{28,24},{32,28},{36,32}... | collective-permute-start | bytes 1769480 | tf_op jit(solution)/shard_map/ppermute | solution.py:284
  116.3 6.0 %collective-permute-start.3 = (bf16[384,384]{1,0:T(8,128)(2,1)S(1)}, bf16[384,384]{1,0:T(8,128)(2,1)S(1)}, u32[]{:S(2)}, u32[]{:S(2)}) collective-permute-start(bf16[384,384]{1,0:T(8,128)(2,1)S(1)} %copy-done.17), channel_id=1, source_target_pairs={{0,4},{4,8},{8,12},{12,16},{16,20},{20,24},{24,28},{28,32},{32,36}... | collective-permute-start | bytes 884744 | tf_op jit(solution)/shard_map/ppermute | solution.py:284
  122.4 4.2 %collective-permute-done.3.from_before = bf16[384,384]{1,0:T(8,128)(2,1)S(1)} collective-permute-done((bf16[384,384]{1,0:T(8,128)(2,1)S(1)}, bf16[384,384]{1,0:T(8,128)(2,1)S(1)}, u32[]{:S(2)}, u32[]{:S(2)}) %collective-permute-start.3) | collective-permute-done | bytes 294944 | tf_op jit(solution)/shard_map/ppermute | solution.py:284
  126.6 3.8 %collective-permute-done.2.from_after = bf16[2,384,384]{2,1,0:T(8,128)(2,1)S(1)} collective-permute-done((bf16[2,384,384]{2,1,0:T(8,128)(2,1)S(1)}, bf16[2,384,384]{2,1,0:T(8,128)(2,1)S(1)}, u32[]{:S(2)}, u32[]{:S(2)}) %collective-permute-start.2) | collective-permute-done | bytes 589856 | tf_op jit(solution)/shard_map/ppermute | solution.py:284
  130.4 1.7 copy-done.1
  132.3 16.6 %all-to-all-done.3.qg = bf16[4,384,384]{2,1,0:T(8,128)(2,1)S(1)} async-done(((bf16[4,384,384]{2,1,0:T(8,128)(2,1)}), bf16[4,384,384]{2,1,0:T(8,128)(2,1)S(1)}, u32[]{:S(2)}, u32[]{:S(2)}) %all-to-all-start.3) | async-done | bytes 1179680 | tf_op jit(solution)/shard_map/all_to_all | solution.py:288
  148.9 33.3 %all_to_all.21.kv = bf16[4,384,384]{2,1,0:T(8,128)(2,1)S(1)} all-to-all(bf16[4,384,384]{2,1,0:T(8,128)(2,1)S(1)} %merge.1), channel_id=1, replica_groups=mesh['clip'=2,'tower'=2,'group'=32,'member'=4] {'member'}, dimensions={0} | all-to-all | bytes 2359296 | tf_op jit(solution)/shard_map/all_to_all | solution.py:288
  182.2 1.6 unpack.1
  (24 shorter events, 0.2 us)
Async XLA Ops:
  0.6 1.0 copy-start.4
  1.6 1.0 copy-start.5
  2.6 1.0 copy-start.6
  3.6 1.0 copy-start.7
  4.6 0.9 copy-start.8
  5.5 0.9 copy-start.9
  6.5 0.9 copy-start.10
  7.4 0.9 copy-start.11
  8.3 0.7 copy-start.12
  9.0 0.7 copy-start.13
  10.4 39.8 %copy-start.2 = (bf16[4,400,384]{2,1,0:T(8,128)(2,1)}, bf16[4,400,384]{2,1,0:T(8,128)(2,1)S(1)}, u32[]{:S(2)}) copy-start(bf16[4,400,384]{2,1,0:T(8,128)(2,1)S(1)} %get-tuple-element.15) | copy-start | bytes 3686404
  50.2 38.7 %all-to-all-start.1 = ((bf16[4,400,384]{2,1,0:T(8,128)(2,1)}), bf16[4,400,384]{2,1,0:T(8,128)(2,1)S(1)}, u32[]{:S(2)}, u32[]{:S(2)}) async-start(bf16[4,400,384]{2,1,0:T(8,128)(2,1)} %copy-done.2), calls=%async_computation.1 | async-start | bytes 2457600 | tf_op jit(solution)/shard_map/all_to_all | solution.py:288
  54.7 34.3 %collective-permute-start = (bf16[2,384,384]{2,1,0:T(8,128)(2,1)}, bf16[2,384,384]{2,1,0:T(8,128)(2,1)S(1)}, u32[]{:S(2)}, u32[]{:S(2)}) collective-permute-start(bf16[2,384,384]{2,1,0:T(8,128)(2,1)} %slice.8), channel_id=1, source_target_pairs={{0,4},{4,8},{8,12},{12,16},{16,20},{20,24},{24,28},{28,32},{32,36}... | collective-permute-start | bytes 1769480 | tf_op jit(solution)/shard_map/ppermute | solution.py:284
  58.0 30.9 %collective-permute-start.1 = (bf16[384,384]{1,0:T(8,128)(2,1)}, bf16[384,384]{1,0:T(8,128)(2,1)S(1)}, u32[]{:S(2)}, u32[]{:S(2)}) collective-permute-start(bf16[384,384]{1,0:T(8,128)(2,1)} %slice_bitcast_fusion), channel_id=1, source_target_pairs={{4,0},{8,4},{12,8},{16,12},{20,16},{24,20},{28,24},{32,28},{36,32}... | collective-permute-start | bytes 884744 | tf_op jit(solution)/shard_map/ppermute | solution.py:284
  106.7 1.4 copy-start
  108.2 1.0 copy-start.3
  109.2 0.8 copy-start.14
  110.0 0.7 copy-start.16
  110.7 3.7 %copy-start.15 = (bf16[2,384,384]{2,1,0:T(8,128)(2,1)S(1)}, bf16[2,384,384]{2,1,0:T(8,128)(2,1)}, u32[]{:S(2)}) copy-start(bf16[2,384,384]{2,1,0:T(8,128)(2,1)} %copy-done.14) | copy-start | bytes 1769476
  110.7 5.6 %copy-start.17 = (bf16[384,384]{1,0:T(8,128)(2,1)S(1)}, bf16[384,384]{1,0:T(8,128)(2,1)}, u32[]{:S(2)}) copy-start(bf16[384,384]{1,0:T(8,128)(2,1)} %copy-done.16) | copy-start | bytes 884740
  110.7 38.1 %all-to-all-start.3 = ((bf16[4,384,384]{2,1,0:T(8,128)(2,1)}), bf16[4,384,384]{2,1,0:T(8,128)(2,1)S(1)}, u32[]{:S(2)}, u32[]{:S(2)}) async-start(bf16[4,384,384]{2,1,0:T(8,128)(2,1)} %copy-done.3), calls=%async_computation.3 | async-start | bytes 2359296 | tf_op jit(solution)/shard_map/all_to_all | solution.py:288
  114.4 16.0 %collective-permute-start.2 = (bf16[2,384,384]{2,1,0:T(8,128)(2,1)S(1)}, bf16[2,384,384]{2,1,0:T(8,128)(2,1)S(1)}, u32[]{:S(2)}, u32[]{:S(2)}) collective-permute-start(bf16[2,384,384]{2,1,0:T(8,128)(2,1)S(1)} %copy-done.15), channel_id=1, source_target_pairs={{4,0},{8,4},{12,8},{16,12},{20,16},{24,20},{28,24},{32,28},{36,32}... | collective-permute-start | bytes 1769480 | tf_op jit(solution)/shard_map/ppermute | solution.py:284
  116.3 10.3 %collective-permute-start.3 = (bf16[384,384]{1,0:T(8,128)(2,1)S(1)}, bf16[384,384]{1,0:T(8,128)(2,1)S(1)}, u32[]{:S(2)}, u32[]{:S(2)}) collective-permute-start(bf16[384,384]{1,0:T(8,128)(2,1)S(1)} %copy-done.17), channel_id=1, source_target_pairs={{0,4},{4,8},{8,12},{12,16},{16,20},{20,24},{24,28},{28,32},{32,36}... | collective-permute-start | bytes 884744 | tf_op jit(solution)/shard_map/ppermute | solution.py:284
  130.4 1.7 copy-start.1

commit v2 on v1

v2 whole, which is shorter than its diff:
```python
import functools

import jax
import jax.numpy as jnp
from jax import lax
from jax.experimental import pallas as pl
from jax.experimental.pallas import tpu as pltpu
from jax.sharding import Mesh
from jax.sharding import PartitionSpec as P

HEADS = 12
HEAD_SIZE = 128
WINDOW_BLOCKS = 4
HALF_WINDOW = 2
MEMBERS = 4
GROUP_HEADS = HEADS // MEMBERS
GROUP_WIDTH = GROUP_HEADS * HEAD_SIZE
EXTENDED = MEMBERS + WINDOW_BLOCKS - 1
VIDEO = 128
AUDIO = 64
STACK = VIDEO + AUDIO
ROWS = 2 * STACK
LIST_ROWS = 16
SCALE = HEAD_SIZE ** -0.5
LOG2_SCALE = SCALE * 1.4426950408889634
MASKED = -1e30
LARGE = pltpu.CompilerParams(vmem_limit_bytes=60 * 1024 * 1024)
SMALL = pltpu.CompilerParams(vmem_limit_bytes=16 * 1024 * 1024)


def product(left, right, left_dim, right_dim):
    return lax.dot_general(
        left,
        right,
        (((left_dim,), (right_dim,)), ((), ())),
        preferred_element_type=jnp.float32,
    )


PLACES = (
    (1, 0, 128),
    (0, 0, 128),
    (0, 128, 128),
    (1, 128, 64),
    (0, 256, 64),
    (0, 320, 64),
    (1, 192, 128),
    (1, 320, 64),
)


def pack_kernel(shift_ref, video_list, audio_list, *refs):
    arrays, (kv_out, qg_out, sems) = refs[:8], refs[8:]
    copies = []
    for member in range(MEMBERS):
        first = lax.rem(shift_ref[0] + member, MEMBERS) * GROUP_WIDTH
        columns = pl.ds(pl.multiple_of(first, GROUP_WIDTH), GROUP_WIDTH)
        for index, (array, (queried, start, rows)) in enumerate(zip(arrays, PLACES)):
            target = qg_out if queried else kv_out
            copies.append(
                pltpu.make_async_copy(
                    array.at[:, columns],
                    target.at[member, start : start + rows],
                    sems.at[member, index],
                )
            )
            copies[-1].start()
    video_first = jnp.full((8, GROUP_WIDTH), video_list[0, 0].astype(jnp.float32))
    audio_first = jnp.full((8, GROUP_WIDTH), audio_list[0, 0].astype(jnp.float32))
    firsts = jnp.concatenate([video_first, audio_first], axis=0).astype(jnp.bfloat16)
    for member in range(MEMBERS):
        qg_out[member, ROWS : ROWS + LIST_ROWS] = firsts
    for copy in copies:
        copy.wait()


def unpack_kernel(shift_ref, kv, qg, vo, ao, vqg, vkg, vvg, aqg, akg, avg):
    for shift in (0, 1):

        @pl.when(shift_ref[0] == shift)
        def _():
            for member in range(MEMBERS):
                first = (member + shift) % MEMBERS * GROUP_WIDTH
                columns = slice(first, first + GROUP_WIDTH)
                vkg[:, columns] = kv[member, 0:128]
                vvg[:, columns] = kv[member, 128:256]
                akg[:, columns] = kv[member, 256:320]
                avg[:, columns] = kv[member, 320:384]
                vo[:, columns] = qg[member, 0:128]
                ao[:, columns] = qg[member, 128:192]
                vqg[:, columns] = qg[member, 192:320]
                aqg[:, columns] = qg[member, 320:384]


def merge_kernel(own, from_after, from_before, out):
    out[0] = (own[0].astype(jnp.float32) + from_before[...].astype(jnp.float32)).astype(
        jnp.bfloat16
    )
    out[1] = own[1]
    out[2:4] = (own[2:4].astype(jnp.float32) + from_after[...].astype(jnp.float32)).astype(
        jnp.bfloat16
    )


def weights_of(scaled):
    top = jnp.max(scaled, axis=1, keepdims=True)
    powers = jnp.exp2(scaled - top)
    return powers * (1.0 / jnp.sum(powers, axis=1, keepdims=True))


def stacked(parts):
    return parts[0] if len(parts) == 1 else jnp.concatenate(parts, axis=0)


def attention_kernel(
    last_group,
    group_ref,
    kv,
    qg,
    before,
    after,
    qg_out,
    kv_out,
    before_out,
    after_out,
    ak_sum,
    av_sum,
):
    group = group_ref[0]
    sources = [before.at[0], before.at[1]] + [kv.at[m] for m in range(MEMBERS)] + [after]
    targets = [before_out.at[0], before_out.at[1]]
    targets += [kv_out.at[m] for m in range(MEMBERS)] + [after_out]
    ak_sum[...] = jnp.zeros_like(ak_sum)
    av_sum[...] = jnp.zeros_like(av_sum)
    bias_before = jnp.where(group == 0, MASKED, 0.0)
    bias_after = jnp.where(group == last_group, MASKED, 0.0)
    video_slot = lax.broadcasted_iota(jnp.int32, (1, WINDOW_BLOCKS * VIDEO), 1) // VIDEO
    audio_slot = lax.broadcasted_iota(jnp.int32, (1, WINDOW_BLOCKS * AUDIO), 1) // AUDIO
    all_queries, all_cotangents, all_rounded, all_score_grads = [], [], [], []

    for member in range(MEMBERS):
        window_start = group * MEMBERS + member - HALF_WINDOW
        firsts = qg[member, ROWS : ROWS + LIST_ROWS].astype(jnp.float32)
        video_first = jnp.concatenate([firsts[0:1]] * 2, axis=1)
        audio_first = jnp.concatenate([firsts[8:9]] * 4, axis=1)
        video_place = (audio_slot + window_start).astype(jnp.float32) - video_first
        audio_place = (video_slot + window_start).astype(jnp.float32) - audio_first
        cross_bias = jnp.where((video_place == 0.0) | (video_place == 1.0), 0.0, MASKED)
        audio_bias = jnp.where((audio_place == 0.0) | (audio_place == 1.0), 0.0, MASKED)
        queries = qg[member, 0:STACK]
        cotangents = qg[member, STACK:ROWS]
        window = sources[member : member + WINDOW_BLOCKS]
        keys = jnp.concatenate([block[0:128] for block in window], axis=0)
        values = jnp.concatenate([block[128:256] for block in window], axis=0)
        audio_keys = jnp.concatenate([block[256:320] for block in window], axis=0)
        audio_values = jnp.concatenate([block[320:384] for block in window], axis=0)

        scaled = product(queries, keys, 1, 1) * LOG2_SCALE
        video_scaled = scaled[0:VIDEO]
        if member < HALF_WINDOW:
            split = (HALF_WINDOW - member) * VIDEO
            video_scaled = jnp.concatenate(
                [video_scaled[:, :split] + bias_before, video_scaled[:, split:]], axis=1
            )
        elif member == MEMBERS - 1:
            split = (WINDOW_BLOCKS - 1) * VIDEO
            video_scaled = jnp.concatenate(
                [video_scaled[:, :split], video_scaled[:, split:] + bias_after], axis=1
            )
        weights = weights_of(
            jnp.concatenate([video_scaled, scaled[VIDEO:STACK] + audio_bias], axis=0)
        )
        rounded = weights.astype(jnp.bfloat16)
        weight_grad = product(cotangents, values, 1, 1)
        row_dot = jnp.sum(rounded.astype(jnp.float32) * weight_grad, axis=1, keepdims=True)
        score_grad = (weights * (weight_grad - row_dot)).astype(jnp.bfloat16)
        result = product(rounded, values, 1, 0)
        query_term = product(score_grad, keys, 1, 0)
        all_queries.append(queries)
        all_cotangents.append(cotangents)
        all_rounded.append(rounded)
        all_score_grads.append(score_grad)

        video_queries = queries[0:VIDEO]
        video_cotangents = cotangents[0:VIDEO]
        cross_scaled = product(video_queries, audio_keys, 1, 1) * LOG2_SCALE
        cross_weights = weights_of(cross_scaled + cross_bias)
        cross_rounded = cross_weights.astype(jnp.bfloat16)
        cross_grad = product(video_cotangents, audio_values, 1, 1)
        cross_dot = jnp.sum(
            cross_rounded.astype(jnp.float32) * cross_grad, axis=1, keepdims=True
        )
        cross_score_grad = (cross_weights * (cross_grad - cross_dot)).astype(jnp.bfloat16)
        cross_result = product(cross_rounded, audio_values, 1, 0)
        cross_query_term = product(cross_score_grad, audio_keys, 1, 0)
        rows = slice(member * AUDIO, (member + WINDOW_BLOCKS) * AUDIO)
        ak_sum[rows] += product(cross_score_grad, video_queries, 0, 0)
        av_sum[rows] += product(cross_rounded, video_cotangents, 0, 0)

        qg_out[member, 0:128] = (result[0:VIDEO] + cross_result).astype(jnp.bfloat16)
        qg_out[member, 128:192] = result[VIDEO:STACK].astype(jnp.bfloat16)
        qg_out[member, 192:320] = (
            (query_term[0:VIDEO] + cross_query_term) * SCALE
        ).astype(jnp.bfloat16)
        qg_out[member, 320:384] = (query_term[VIDEO:STACK] * SCALE).astype(jnp.bfloat16)

    for block in range(EXTENDED):
        target = targets[block]
        members = [m for m in range(MEMBERS) if 0 <= block - m < WINDOW_BLOCKS]
        columns = {m: slice((block - m) * VIDEO, (block - m + 1) * VIDEO) for m in members}
        score_grads = stacked([all_score_grads[m][:, columns[m]] for m in members])
        rounded = stacked([all_rounded[m][:, columns[m]] for m in members])
        queries = stacked([all_queries[m] for m in members])
        cotangents = stacked([all_cotangents[m] for m in members])
        target[0:128] = (product(score_grads, queries, 0, 0) * SCALE).astype(target.dtype)
        target[128:256] = product(rounded, cotangents, 0, 0).astype(target.dtype)
        rows = slice(block * AUDIO, (block + 1) * AUDIO)
        target[256:320] = (ak_sum[rows] * SCALE).astype(target.dtype)
        target[320:384] = av_sum[rows].astype(target.dtype)


def whole(memory=pltpu.VMEM):
    return pl.BlockSpec(memory_space=memory)


def pack(shift, video_lists, audio_lists, *arrays):
    return pl.pallas_call(
        pack_kernel,
        out_shape=(
            jax.ShapeDtypeStruct((MEMBERS, ROWS, GROUP_WIDTH), jnp.bfloat16),
            jax.ShapeDtypeStruct((MEMBERS, ROWS + LIST_ROWS, GROUP_WIDTH), jnp.bfloat16),
        ),
        in_specs=[whole(pltpu.SMEM)] * 3 + [whole(pl.ANY)] * 8,
        out_specs=(whole(), whole()),
        scratch_shapes=[pltpu.SemaphoreType.DMA((MEMBERS, 8))],
        compiler_params=LARGE,
        name="pack",
    )(shift, video_lists, audio_lists, *arrays)


def unpack(shift, kv, qg):
    video = jax.ShapeDtypeStruct((VIDEO, HEADS * HEAD_SIZE), jnp.bfloat16)
    audio = jax.ShapeDtypeStruct((AUDIO, HEADS * HEAD_SIZE), jnp.bfloat16)
    shapes = (video, audio, video, video, video, audio, audio, audio)
    return pl.pallas_call(
        unpack_kernel,
        out_shape=shapes,
        in_specs=[whole(pltpu.SMEM)] + [whole()] * 2,
        out_specs=[whole()] * 8,
        compiler_params=SMALL,
        name="unpack",
    )(shift, kv, qg)


def merge(own, from_after, from_before):
    return pl.pallas_call(
        merge_kernel,
        out_shape=jax.ShapeDtypeStruct(own.shape, jnp.bfloat16),
        in_specs=[whole()] * 3,
        out_specs=whole(),
        compiler_params=SMALL,
        name="merge",
    )(own, from_after, from_before)


def attention(groups, group, *arrays):
    def head_block(*leading):
        zeros = (0,) * len(leading)
        return pl.BlockSpec(leading + (HEAD_SIZE,), lambda head: zeros + (head,))

    audio_sum = pltpu.VMEM((EXTENDED * AUDIO, HEAD_SIZE), jnp.float32)
    halo = (head_block(HALF_WINDOW, ROWS), head_block(ROWS))
    return pl.pallas_call(
        functools.partial(attention_kernel, groups - 1),
        grid=(GROUP_HEADS,),
        out_shape=(
            jax.ShapeDtypeStruct((MEMBERS, ROWS, GROUP_WIDTH), jnp.bfloat16),
            jax.ShapeDtypeStruct((MEMBERS, ROWS, GROUP_WIDTH), jnp.bfloat16),
            jax.ShapeDtypeStruct((HALF_WINDOW, ROWS, GROUP_WIDTH), jnp.bfloat16),
            jax.ShapeDtypeStruct((ROWS, GROUP_WIDTH), jnp.bfloat16),
        ),
        in_specs=[
            whole(pltpu.SMEM),
            head_block(MEMBERS, ROWS),
            head_block(MEMBERS, ROWS + LIST_ROWS),
            *halo,
        ],
        out_specs=(head_block(MEMBERS, ROWS), head_block(MEMBERS, ROWS), *halo),
        scratch_shapes=[audio_sum, audio_sum],
        compiler_params=LARGE,
        name="attention",
    )(group, *arrays)


def slice_shift(clip, tower, clips):
    return jnp.where((clip == clips - 1) & (tower == 1), 1, 0).astype(jnp.int32).reshape(1)


def to_group(block, distance):
    clips, towers = lax.axis_size("clip"), lax.axis_size("tower")
    per_tower = lax.axis_size("group")
    groups = towers * per_tower
    route = []
    for clip in range(clips):
        for group in range(groups):
            target = group + distance
            if not 0 <= target < groups:
                continue
            turn = target // per_tower - group // per_tower if clip == clips - 1 else 0
            for member in range(MEMBERS):
                route.append(
                    (
                        (clip * groups + group) * MEMBERS + member,
                        (clip * groups + target) * MEMBERS + (member - turn) % MEMBERS,
                    )
                )
    return lax.ppermute(block, ("clip", "tower", "group", "member"), route)


def exchange(packed):
    return lax.all_to_all(packed, "member", 0, 0)


def body(
    video_query,
    video_keys,
    video_value,
    audio_query,
    audio_key,
    audio_value,
    video_cotangent,
    audio_cotangent,
    video_lists,
    audio_lists,
):
    groups = lax.axis_size(("tower", "group"))
    group = lax.axis_index(("tower", "group")).astype(jnp.int32).reshape(1)
    shift = slice_shift(lax.axis_index("clip"), lax.axis_index("tower"), lax.axis_size("clip"))
    kv_packed, qg_packed = pack(
        shift,
        video_lists,
        audio_lists,
        video_query,
        video_keys,
        video_value,
        audio_query,
        audio_key,
        audio_value,
        video_cotangent,
        audio_cotangent,
    )
    kv = exchange(kv_packed)
    before = to_group(kv[MEMBERS - HALF_WINDOW :], 1)
    after = to_group(kv[0], -1)
    qg = exchange(qg_packed)
    qg_part, kv_part, before_part, after_part = attention(
        groups, group, kv, qg, before, after
    )
    qg_back = exchange(qg_part)
    from_after = to_group(before_part, -1)
    from_before = to_group(after_part, 1)
    kv_back = exchange(merge(kv_part, from_after, from_before))
    return unpack(shift, kv_back, qg_back)


def solution(mesh):
    shape = mesh.devices.shape
    fine = Mesh(
        mesh.devices.reshape(shape[0], shape[1], shape[2] // MEMBERS, MEMBERS),
        ("clip", "tower", "group", "member"),
    )
    placed = P(("clip", "tower", "group", "member"), None)
    return jax.shard_map(
        body,
        mesh=fine,
        in_specs=(placed,) * 10,
        out_specs=(placed,) * 8,
        check_vma=False,
    )
```

time: 185 us -> 164 us (0.89)
  local copies, waits for them, and re-layouts: 16.3 us -> 1.22 us
  blocking collectives: 73.2 us -> 66.1 us
    unnamed x36 -> x12, local copies, waits for them, and re-layouts: 14.6 us -> 1.12 us
    all_to_all x2, blocking collectives: 73.2 us -> 66.1 us  [exchange(): return lax.all_to_all(packed, 'member', 0, 0)]
    pallas_call x1, Pallas kernels: 0.75 us -> 4.08 us  [pack(): pl.pallas_call(pack_kernel, out_shape=(jax.ShapeDtypeStruct((MEMBERS, ROW...]
    pallas_call x1, Pallas kernels: 17.8 us -> 15.5 us  [attention(): pl.pallas_call(functools.partial(attention_kernel, groups - 1), grid=(GRO...]
  transfers between devices with their start and end apart: 6 -> 6, of which waited for: 4 -> 4; matrix products, arithmetic and copies ran while one was open for 1% -> 0% of each run, Pallas kernels for 0% -> 0%
where the time goes in v2:
time: 164 us; the launch traced here: 163 us
  blocking collectives  66.1 us (40%)
  waiting for transfers between devices  52.8 us (32%)
  Pallas kernels  21.4 us (13%)
  starting transfers between devices  21 us (13%)
    all_to_all x2, blocking collectives, exchange(): return lax.all_to_all(packed, 'member', 0, 0)  66.1 us
    all_to_all x2, waiting for transfers between devices, exchange(): return lax.all_to_all(packed, 'member', 0, 0)  43.8 us
    pallas_call x1, Pallas kernels, attention(): pl.pallas_call(functools.partial(attention_kernel, groups - 1), grid=(GRO...  15.5 us
    ppermute x4, starting transfers between devices, to_group(): return lax.ppermute(block, ('clip', 'tower', 'group', 'member'), route)  13.8 us
    ppermute x4, waiting for transfers between devices, to_group(): return lax.ppermute(block, ('clip', 'tower', 'group', 'member'), route)  9.01 us
    all_to_all x2, starting transfers between devices, exchange(): return lax.all_to_all(packed, 'member', 0, 0)  7.2 us
    pallas_call x1, Pallas kernels, pack(): pl.pallas_call(pack_kernel, out_shape=(jax.ShapeDtypeStruct((MEMBERS, ROW...  4.08 us
  transfers between devices with their start and end apart: 6, of which 4 were waited for; matrix products, arithmetic and copies ran while one was open for 0% of the time, Pallas kernels for 0%

profile of v2, /device:TPU:120, one launch (start us, length us, event | category | flops | bytes accessed | tf_op | source)
XLA Modules:
  0.0 163.3 jit_solution(18400267816000215282)
XLA Ops:
  0.6 4.1 %pack.1 = (bf16[4,384,384]{2,1,0:T(8,128)(2,1)}, bf16[4,400,384]{2,1,0:T(8,128)(2,1)}) custom-call(s32[1]{0:T(128)} %bitcast.shift_ref, s32[1,2]{1,0:T(1,128)} %video_list.1, s32[1,2]{1,0:T(1,128)} %audio_list.1, bf16[128,1536]{1,0:T(8,128)(2,1)} %refs_0_.1, bf16[128,1536]{1,0:T(8,128)(2,1)} %refs_1_.1, bf16[128,1536]{1,0:T(8,128)(2,1)} %refs_2_.1, ...), custom_call_target="tpu_custom_call" | custom-call | tf_op jit(solution)/shard_map/pack/pallas_call | solution.py:227
  4.7 40.0 %all_to_all.20.kv = bf16[4,384,384]{2,1,0:T(8,128)(2,1)S(1)} all-to-all(bf16[4,384,384]{2,1,0:T(8,128)(2,1)} %get-tuple-element.14), channel_id=1, replica_groups=mesh['clip'=2,'tower'=2,'group'=32,'member'=4] {'member'}, dimensions={0} | all-to-all | bytes 2359296 | tf_op jit(solution)/shard_map/all_to_all | solution.py:321
  44.8 0.0 copy-start.1
  44.8 3.5 %all-to-all-start.1 = ((bf16[4,400,384]{2,1,0:T(8,128)(2,1)}), bf16[4,400,384]{2,1,0:T(8,128)(2,1)S(1)}, u32[]{:S(2)}, u32[]{:S(2)}) async-start(bf16[4,400,384]{2,1,0:T(8,128)(2,1)} %get-tuple-element.15), calls=%async_computation.1 | async-start | bytes 2457600 | tf_op jit(solution)/shard_map/all_to_all | solution.py:321
  48.3 0.1 slice.8
  48.4 2.6 %collective-permute-start = (bf16[2,384,384]{2,1,0:T(8,128)(2,1)S(1)}, bf16[2,384,384]{2,1,0:T(8,128)(2,1)}, u32[]{:S(2)}, u32[]{:S(2)}) collective-permute-start(bf16[2,384,384]{2,1,0:T(8,128)(2,1)S(1)} %slice.8), channel_id=1, source_target_pairs={{0,4},{1,5},{2,6},{3,7},{4,8},{5,9},{6,10},{7,11},{8,12},{9,13},{1... | collective-permute-start | bytes 1769480 | tf_op jit(solution)/shard_map/ppermute | solution.py:317
  51.0 0.0 copy-done.1
  51.1 3.2 %collective-permute-start.1 = (bf16[384,384]{1,0:T(8,128)(2,1)S(1)}, bf16[384,384]{1,0:T(8,128)(2,1)S(1)}, u32[]{:S(2)}, u32[]{:S(2)}) collective-permute-start(bf16[384,384]{1,0:T(8,128)(2,1)S(1)} %slice_bitcast_fusion), channel_id=1, source_target_pairs={{4,0},{5,1},{6,2},{7,3},{8,4},{9,5},{10,6},{11,7},{12,8},{13,9},{1... | collective-permute-start | bytes 884744 | tf_op jit(solution)/shard_map/ppermute | solution.py:317
  54.3 26.0 %all-to-all-done.1.qg = bf16[4,400,384]{2,1,0:T(8,128)(2,1)S(1)} async-done(((bf16[4,400,384]{2,1,0:T(8,128)(2,1)}), bf16[4,400,384]{2,1,0:T(8,128)(2,1)S(1)}, u32[]{:S(2)}, u32[]{:S(2)}) %all-to-all-start.1) | async-done | bytes 1228832 | tf_op jit(solution)/shard_map/all_to_all | solution.py:321
  80.3 0.0 copy-start.2
  80.3 0.0 collective-permute-done.1.after
  80.3 0.0 copy-start.3
  80.3 0.0 collective-permute-done.before
  80.3 1.1 copy-done.2
  81.4 0.0 copy-done.3
  81.4 15.5 %attention.1 = (bf16[4,384,384]{2,1,0:T(8,128)(2,1)}, bf16[4,384,384]{2,1,0:T(8,128)(2,1)}, bf16[2,384,384]{2,1,0:T(8,128)(2,1)}, bf16[384,384]{1,0:T(8,128)(2,1)}) custom-call(s32[1]{0:T(128)} %bitcast.1.group_ref, bf16[4,384,384]{2,1,0:T(8,128)(2,1)} %copy-done.1, bf16[4,400,384]{2,1,0:T(8,128)(2,1)} %copy-done.2, ...), custom_call_target="tpu_custom_call" | custom-call | tf_op jit(solution)/shard_map/attention/pallas_call | solution.py:273
  96.9 0.0 copy-start.4
  96.9 0.0 copy-start.5
  96.9 0.0 copy-start
  96.9 3.7 %all-to-all-start.3 = ((bf16[4,384,384]{2,1,0:T(8,128)(2,1)}), bf16[4,384,384]{2,1,0:T(8,128)(2,1)S(1)}, u32[]{:S(2)}, u32[]{:S(2)}) async-start(bf16[4,384,384]{2,1,0:T(8,128)(2,1)} %get-tuple-element.19), calls=%async_computation.3 | async-start | bytes 2359296 | tf_op jit(solution)/shard_map/all_to_all | solution.py:321
  100.6 0.0 copy-done.4
  100.6 1.9 %collective-permute-start.2 = (bf16[2,384,384]{2,1,0:T(8,128)(2,1)S(1)}, bf16[2,384,384]{2,1,0:T(8,128)(2,1)S(1)}, u32[]{:S(2)}, u32[]{:S(2)}) collective-permute-start(bf16[2,384,384]{2,1,0:T(8,128)(2,1)S(1)} %copy-done.4), channel_id=1, source_target_pairs={{4,0},{5,1},{6,2},{7,3},{8,4},{9,5},{10,6},{11,7},{12,8},{13,9},{1... | collective-permute-start | bytes 1769480 | tf_op jit(solution)/shard_map/ppermute | solution.py:317
  102.5 0.0 copy-done.5
  102.6 6.0 %collective-permute-start.3 = (bf16[384,384]{1,0:T(8,128)(2,1)S(1)}, bf16[384,384]{1,0:T(8,128)(2,1)S(1)}, u32[]{:S(2)}, u32[]{:S(2)}) collective-permute-start(bf16[384,384]{1,0:T(8,128)(2,1)S(1)} %copy-done.5), channel_id=1, source_target_pairs={{0,4},{1,5},{2,6},{3,7},{4,8},{5,9},{6,10},{7,11},{8,12},{9,13},{1... | collective-permute-start | bytes 884744 | tf_op jit(solution)/shard_map/ppermute | solution.py:317
  108.6 4.2 %collective-permute-done.3.from_before = bf16[384,384]{1,0:T(8,128)(2,1)S(1)} collective-permute-done((bf16[384,384]{1,0:T(8,128)(2,1)S(1)}, bf16[384,384]{1,0:T(8,128)(2,1)S(1)}, u32[]{:S(2)}, u32[]{:S(2)}) %collective-permute-start.3) | collective-permute-done | bytes 294944 | tf_op jit(solution)/shard_map/ppermute | solution.py:317
  112.8 4.8 %collective-permute-done.2.from_after = bf16[2,384,384]{2,1,0:T(8,128)(2,1)S(1)} collective-permute-done((bf16[2,384,384]{2,1,0:T(8,128)(2,1)S(1)}, bf16[2,384,384]{2,1,0:T(8,128)(2,1)S(1)}, u32[]{:S(2)}, u32[]{:S(2)}) %collective-permute-start.2) | collective-permute-done | bytes 589856 | tf_op jit(solution)/shard_map/ppermute | solution.py:317
  117.6 0.0 copy-done
  117.6 0.2 merge.1
  117.8 17.8 %all-to-all-done.3.qg = bf16[4,384,384]{2,1,0:T(8,128)(2,1)S(1)} async-done(((bf16[4,384,384]{2,1,0:T(8,128)(2,1)}), bf16[4,384,384]{2,1,0:T(8,128)(2,1)S(1)}, u32[]{:S(2)}, u32[]{:S(2)}) %all-to-all-start.3) | async-done | bytes 1179680 | tf_op jit(solution)/shard_map/all_to_all | solution.py:321
  135.6 26.1 %all_to_all.21.kv = bf16[4,384,384]{2,1,0:T(8,128)(2,1)S(1)} all-to-all(bf16[4,384,384]{2,1,0:T(8,128)(2,1)S(1)} %merge.1), channel_id=1, replica_groups=mesh['clip'=2,'tower'=2,'group'=32,'member'=4] {'member'}, dimensions={0} | all-to-all | bytes 2359296 | tf_op jit(solution)/shard_map/all_to_all | solution.py:321
  161.7 1.6 unpack.1
  (1 shorter events, 0.0 us)
Async XLA Ops:
  44.8 6.2 %copy-start.1 = (bf16[4,384,384]{2,1,0:T(8,128)(2,1)}, bf16[4,384,384]{2,1,0:T(8,128)(2,1)S(1)}, u32[]{:S(2)}) copy-start(bf16[4,384,384]{2,1,0:T(8,128)(2,1)S(1)} %all_to_all.20.kv) | copy-start | bytes 3538948
  44.8 35.5 %all-to-all-start.1 = ((bf16[4,400,384]{2,1,0:T(8,128)(2,1)}), bf16[4,400,384]{2,1,0:T(8,128)(2,1)S(1)}, u32[]{:S(2)}, u32[]{:S(2)}) async-start(bf16[4,400,384]{2,1,0:T(8,128)(2,1)} %get-tuple-element.15), calls=%async_computation.1 | async-start | bytes 2457600 | tf_op jit(solution)/shard_map/all_to_all | solution.py:321
  48.4 31.9 %collective-permute-start = (bf16[2,384,384]{2,1,0:T(8,128)(2,1)S(1)}, bf16[2,384,384]{2,1,0:T(8,128)(2,1)}, u32[]{:S(2)}, u32[]{:S(2)}) collective-permute-start(bf16[2,384,384]{2,1,0:T(8,128)(2,1)S(1)} %slice.8), channel_id=1, source_target_pairs={{0,4},{1,5},{2,6},{3,7},{4,8},{5,9},{6,10},{7,11},{8,12},{9,13},{1... | collective-permute-start | bytes 1769480 | tf_op jit(solution)/shard_map/ppermute | solution.py:317
  51.1 29.3 %collective-permute-start.1 = (bf16[384,384]{1,0:T(8,128)(2,1)S(1)}, bf16[384,384]{1,0:T(8,128)(2,1)S(1)}, u32[]{:S(2)}, u32[]{:S(2)}) collective-permute-start(bf16[384,384]{1,0:T(8,128)(2,1)S(1)} %slice_bitcast_fusion), channel_id=1, source_target_pairs={{4,0},{5,1},{6,2},{7,3},{8,4},{9,5},{10,6},{11,7},{12,8},{13,9},{1... | collective-permute-start | bytes 884744 | tf_op jit(solution)/shard_map/ppermute | solution.py:317
  80.3 1.1 copy-start.2
  80.3 1.1 copy-start.3
  96.9 3.7 %copy-start.4 = (bf16[2,384,384]{2,1,0:T(8,128)(2,1)S(1)}, bf16[2,384,384]{2,1,0:T(8,128)(2,1)}, u32[]{:S(2)}) copy-start(bf16[2,384,384]{2,1,0:T(8,128)(2,1)} %get-tuple-element.17) | copy-start | bytes 1769476
  96.9 5.6 %copy-start.5 = (bf16[384,384]{1,0:T(8,128)(2,1)S(1)}, bf16[384,384]{1,0:T(8,128)(2,1)}, u32[]{:S(2)}) copy-start(bf16[384,384]{1,0:T(8,128)(2,1)} %get-tuple-element.18) | copy-start | bytes 884740
  96.9 20.7 %copy-start = (bf16[4,384,384]{2,1,0:T(8,128)(2,1)S(1)}, bf16[4,384,384]{2,1,0:T(8,128)(2,1)}, u32[]{:S(2)}) copy-start(bf16[4,384,384]{2,1,0:T(8,128)(2,1)} %get-tuple-element.16.own) | copy-start | bytes 3538948
  96.9 38.7 %all-to-all-start.3 = ((bf16[4,384,384]{2,1,0:T(8,128)(2,1)}), bf16[4,384,384]{2,1,0:T(8,128)(2,1)S(1)}, u32[]{:S(2)}, u32[]{:S(2)}) async-start(bf16[4,384,384]{2,1,0:T(8,128)(2,1)} %get-tuple-element.19), calls=%async_computation.3 | async-start | bytes 2359296 | tf_op jit(solution)/shard_map/all_to_all | solution.py:321
  100.6 17.0 %collective-permute-start.2 = (bf16[2,384,384]{2,1,0:T(8,128)(2,1)S(1)}, bf16[2,384,384]{2,1,0:T(8,128)(2,1)S(1)}, u32[]{:S(2)}, u32[]{:S(2)}) collective-permute-start(bf16[2,384,384]{2,1,0:T(8,128)(2,1)S(1)} %copy-done.4), channel_id=1, source_target_pairs={{4,0},{5,1},{6,2},{7,3},{8,4},{9,5},{10,6},{11,7},{12,8},{13,9},{1... | collective-permute-start | bytes 1769480 | tf_op jit(solution)/shard_map/ppermute | solution.py:317
  102.6 10.3 %collective-permute-start.3 = (bf16[384,384]{1,0:T(8,128)(2,1)S(1)}, bf16[384,384]{1,0:T(8,128)(2,1)S(1)}, u32[]{:S(2)}, u32[]{:S(2)}) collective-permute-start(bf16[384,384]{1,0:T(8,128)(2,1)S(1)} %copy-done.5), channel_id=1, source_target_pairs={{0,4},{1,5},{2,6},{3,7},{4,8},{5,9},{6,10},{7,11},{8,12},{9,13},{1... | collective-permute-start | bytes 884744 | tf_op jit(solution)/shard_map/ppermute | solution.py:317

commit v3 on v2

v3 whole, which is shorter than its diff:
```python
import functools

import jax
import jax.numpy as jnp
from jax import lax
from jax.experimental import pallas as pl
from jax.experimental.pallas import tpu as pltpu
from jax.sharding import Mesh
from jax.sharding import PartitionSpec as P

HEADS = 12
HEAD_SIZE = 128
WINDOW_BLOCKS = 4
HALF_WINDOW = 2
MEMBERS = 4
GROUP_HEADS = HEADS // MEMBERS
GROUP_WIDTH = GROUP_HEADS * HEAD_SIZE
EXTENDED = MEMBERS + WINDOW_BLOCKS - 1
VIDEO = 128
AUDIO = 64
STACK = VIDEO + AUDIO
ROWS = 2 * STACK
LIST_ROWS = 16
SCALE = HEAD_SIZE ** -0.5
LOG2_SCALE = SCALE * 1.4426950408889634
MASKED = -1e30
LARGE = pltpu.CompilerParams(vmem_limit_bytes=60 * 1024 * 1024)
SMALL = pltpu.CompilerParams(vmem_limit_bytes=16 * 1024 * 1024)


def product(left, right, left_dim, right_dim):
    return lax.dot_general(
        left,
        right,
        (((left_dim,), (right_dim,)), ((), ())),
        preferred_element_type=jnp.float32,
    )


def start_packing(copies, sems, first, arrays, target):
    columns = pl.ds(pl.multiple_of(first, GROUP_WIDTH), GROUP_WIDTH)
    row = 0
    for index, array in enumerate(arrays):
        rows = array.shape[0]
        copy = pltpu.make_async_copy(
            array.at[:, columns], target.at[row : row + rows], sems.at[index]
        )
        copy.start()
        copies.append(copy)
        row += rows


def pack_kv_kernel(place, vk, vv, ak, av, out, sems):
    copies = []
    for member in range(MEMBERS):
        first = lax.rem(place[2] + member, MEMBERS) * GROUP_WIDTH
        start_packing(copies, sems.at[member], first, (vk, vv, ak, av), out.at[member])
    for copy in copies:
        copy.wait()


def pack_qg_kernel(place, video_list, audio_list, vq, aq, vg, ag, out, sems):
    copies = []
    for member in range(MEMBERS):
        first = lax.rem(place[2] + member, MEMBERS) * GROUP_WIDTH
        start_packing(copies, sems.at[member], first, (vq, aq, vg, ag), out.at[member])
    video_first = jnp.full((8, GROUP_WIDTH), video_list[0, 0].astype(jnp.float32))
    audio_first = jnp.full((8, GROUP_WIDTH), audio_list[0, 0].astype(jnp.float32))
    firsts = jnp.concatenate([video_first, audio_first], axis=0).astype(jnp.bfloat16)
    for member in range(MEMBERS):
        out[member, ROWS : ROWS + LIST_ROWS] = firsts
    for copy in copies:
        copy.wait()


def unpack_kernel(place, kv, qg, vo, ao, vqg, vkg, vvg, aqg, akg, avg):
    for member in range(MEMBERS):
        first = lax.rem(place[2] + member, MEMBERS) * GROUP_WIDTH
        columns = pl.ds(pl.multiple_of(first, GROUP_WIDTH), GROUP_WIDTH)
        vo[:, columns] = qg[member, 0:128]
        ao[:, columns] = qg[member, 128:192]
        vqg[:, columns] = qg[member, 192:320]
        aqg[:, columns] = qg[member, 320:384]
        vkg[:, columns] = kv[member, 0:128]
        vvg[:, columns] = kv[member, 128:256]
        akg[:, columns] = kv[member, 256:320]
        avg[:, columns] = kv[member, 320:384]


def merge_kernel(own, from_after, from_before, out):
    out[0] = (own[0].astype(jnp.float32) + from_before[...].astype(jnp.float32)).astype(
        jnp.bfloat16
    )
    out[1] = own[1]
    out[2:4] = (own[2:4].astype(jnp.float32) + from_after[...].astype(jnp.float32)).astype(
        jnp.bfloat16
    )


def stacked(parts):
    return parts[0] if len(parts) == 1 else jnp.concatenate(parts, axis=0)


def masks_of(window_start, firsts):
    firsts = firsts.astype(jnp.float32)
    video_slot = lax.broadcasted_iota(jnp.int32, (1, WINDOW_BLOCKS * VIDEO), 1) // VIDEO
    audio_slot = lax.broadcasted_iota(jnp.int32, (1, WINDOW_BLOCKS * AUDIO), 1) // AUDIO
    video_first = jnp.concatenate([firsts[0:1]] * 2, axis=1)
    audio_first = jnp.concatenate([firsts[8:9]] * 4, axis=1)
    video_place = (audio_slot + window_start).astype(jnp.float32) - video_first
    audio_place = (video_slot + window_start).astype(jnp.float32) - audio_first
    cross_mask = jnp.where((video_place == 0.0) | (video_place == 1.0), 0.0, MASKED)
    audio_mask = jnp.where((audio_place == 0.0) | (audio_place == 1.0), 0.0, MASKED)
    return cross_mask, audio_mask


def softmax_and_grad(scaled, weight_grad):
    top = [jnp.max(s, axis=1, keepdims=True) for s in scaled]
    powers = [jnp.exp2(s - t) for s, t in zip(scaled, top)]
    scale = [1.0 / jnp.sum(p, axis=1, keepdims=True) for p in powers]
    weights = [p * s for p, s in zip(powers, scale)]
    rounded = [w.astype(jnp.bfloat16) for w in weights]
    row_dot = [
        jnp.sum(r.astype(jnp.float32) * g, axis=1, keepdims=True)
        for r, g in zip(rounded, weight_grad)
    ]
    score_grad = [
        (w * (g - d)).astype(jnp.bfloat16) for w, g, d in zip(weights, weight_grad, row_dot)
    ]
    return rounded, score_grad


def attention_kernel(
    last_group, place, kv, qg, before, after, qg_out, kv_out, before_out, after_out
):
    group = place[0]
    members = range(MEMBERS)
    sources = [before.at[0], before.at[1]] + [kv.at[m] for m in members] + [after]
    targets = [before_out.at[0], before_out.at[1]]
    targets += [kv_out.at[m] for m in members] + [after_out]
    bias_before = jnp.where(group == 0, MASKED, 0.0)
    bias_after = jnp.where(group == last_group, MASKED, 0.0)

    queries = [qg[m, 0:STACK] for m in members]
    cotangents = [qg[m, STACK:ROWS] for m in members]
    video_queries = [q[0:VIDEO] for q in queries]
    video_cotangents = [g[0:VIDEO] for g in cotangents]
    windows = [sources[m : m + WINDOW_BLOCKS] for m in members]
    keys = [jnp.concatenate([b[0:128] for b in w], axis=0) for w in windows]
    values = [jnp.concatenate([b[128:256] for b in w], axis=0) for w in windows]
    audio_keys = [jnp.concatenate([b[256:320] for b in w], axis=0) for w in windows]
    audio_values = [jnp.concatenate([b[320:384] for b in w], axis=0) for w in windows]

    rounded, score_grads, cross_rounded, cross_score_grads = [], [], [], []
    for m in members:
        cross_mask, audio_mask = masks_of(
            group * MEMBERS + m - HALF_WINDOW, qg[m, ROWS : ROWS + LIST_ROWS]
        )
        scaled = product(queries[m], keys[m], 1, 1) * LOG2_SCALE
        cross_scaled = product(video_queries[m], audio_keys[m], 1, 1) * LOG2_SCALE
        video_scaled = scaled[0:VIDEO]
        if m < HALF_WINDOW:
            split = (HALF_WINDOW - m) * VIDEO
            video_scaled = jnp.concatenate(
                [video_scaled[:, :split] + bias_before, video_scaled[:, split:]], axis=1
            )
        elif m == MEMBERS - 1:
            split = (WINDOW_BLOCKS - 1) * VIDEO
            video_scaled = jnp.concatenate(
                [video_scaled[:, :split], video_scaled[:, split:] + bias_after], axis=1
            )
        scaled = jnp.concatenate([video_scaled, scaled[VIDEO:STACK] + audio_mask], axis=0)
        weight_grad = product(cotangents[m], values[m], 1, 1)
        cross_grad = product(video_cotangents[m], audio_values[m], 1, 1)
        (r, cr), (s, cs) = softmax_and_grad(
            (scaled, cross_scaled + cross_mask), (weight_grad, cross_grad)
        )
        rounded.append(r)
        score_grads.append(s)
        cross_rounded.append(cr)
        cross_score_grads.append(cs)

    result = [product(rounded[m], values[m], 1, 0) for m in members]
    cross_result = [product(cross_rounded[m], audio_values[m], 1, 0) for m in members]
    query_term = [product(score_grads[m], keys[m], 1, 0) for m in members]
    cross_query = [product(cross_score_grads[m], audio_keys[m], 1, 0) for m in members]
    ak_terms = [product(cross_score_grads[m], video_queries[m], 0, 0) for m in members]
    av_terms = [product(cross_rounded[m], video_cotangents[m], 0, 0) for m in members]
    for m in members:
        qg_out[m, 0:128] = (result[m][0:VIDEO] + cross_result[m]).astype(jnp.bfloat16)
        qg_out[m, 128:192] = result[m][VIDEO:STACK].astype(jnp.bfloat16)
        qg_out[m, 192:320] = (
            (query_term[m][0:VIDEO] + cross_query[m]) * SCALE
        ).astype(jnp.bfloat16)
        qg_out[m, 320:384] = (query_term[m][VIDEO:STACK] * SCALE).astype(jnp.bfloat16)

    for block in range(EXTENDED):
        target = targets[block]
        users = [m for m in members if 0 <= block - m < WINDOW_BLOCKS]
        columns = {m: slice((block - m) * VIDEO, (block - m + 1) * VIDEO) for m in users}
        rows = {m: slice((block - m) * AUDIO, (block - m + 1) * AUDIO) for m in users}
        vk_sum = product(
            stacked([score_grads[m][:, columns[m]] for m in users]),
            stacked([queries[m] for m in users]),
            0,
            0,
        )
        vv_sum = product(
            stacked([rounded[m][:, columns[m]] for m in users]),
            stacked([cotangents[m] for m in users]),
            0,
            0,
        )
        ak_sum = sum(ak_terms[m][rows[m]] for m in users)
        av_sum = sum(av_terms[m][rows[m]] for m in users)
        target[0:128] = (vk_sum * SCALE).astype(target.dtype)
        target[128:256] = vv_sum.astype(target.dtype)
        target[256:320] = (ak_sum * SCALE).astype(target.dtype)
        target[320:384] = av_sum.astype(target.dtype)


def whole(memory=pltpu.VMEM):
    return pl.BlockSpec(memory_space=memory)


PACKED_KV = jax.ShapeDtypeStruct((MEMBERS, ROWS, GROUP_WIDTH), jnp.bfloat16)
BLOCK_KV = jax.ShapeDtypeStruct((ROWS, GROUP_WIDTH), jnp.bfloat16)
PACKED_QG = jax.ShapeDtypeStruct((MEMBERS, ROWS + LIST_ROWS, GROUP_WIDTH), jnp.bfloat16)


def pack_kv(place, *arrays):
    return pl.pallas_call(
        pack_kv_kernel,
        out_shape=PACKED_KV,
        in_specs=[whole(pltpu.SMEM)] + [whole(pl.ANY)] * 4,
        out_specs=whole(),
        scratch_shapes=[pltpu.SemaphoreType.DMA((MEMBERS, 4))],
        compiler_params=LARGE,
        name="pack_kv",
    )(place, *arrays)


def pack_qg(place, *arrays):
    return pl.pallas_call(
        pack_qg_kernel,
        out_shape=PACKED_QG,
        in_specs=[whole(pltpu.SMEM)] * 3 + [whole(pl.ANY)] * 4,
        out_specs=whole(),
        scratch_shapes=[pltpu.SemaphoreType.DMA((MEMBERS, 4))],
        compiler_params=LARGE,
        name="pack_qg",
    )(place, *arrays)


def unpack(place, kv, qg):
    video = jax.ShapeDtypeStruct((VIDEO, HEADS * HEAD_SIZE), jnp.bfloat16)
    audio = jax.ShapeDtypeStruct((AUDIO, HEADS * HEAD_SIZE), jnp.bfloat16)
    shapes = (video, audio, video, video, video, audio, audio, audio)
    return pl.pallas_call(
        unpack_kernel,
        out_shape=shapes,
        in_specs=[whole(pltpu.SMEM)] + [whole()] * 2,
        out_specs=[whole()] * 8,
        compiler_params=SMALL,
        name="unpack",
    )(place, kv, qg)


def merge(own, from_after, from_before):
    return pl.pallas_call(
        merge_kernel,
        out_shape=PACKED_KV,
        in_specs=[whole()] * 3,
        out_specs=whole(),
        compiler_params=SMALL,
        name="merge",
    )(own, from_after, from_before)


def attention(groups, place, kv, qg, before, after):
    def head_block(*leading):
        zeros = (0,) * len(leading)
        return pl.BlockSpec(leading + (HEAD_SIZE,), lambda head: zeros + (head,))

    halo = (head_block(HALF_WINDOW, ROWS), head_block(ROWS))
    return pl.pallas_call(
        functools.partial(attention_kernel, groups - 1),
        grid=(GROUP_HEADS,),
        out_shape=(
            PACKED_KV,
            PACKED_KV,
            jax.ShapeDtypeStruct((HALF_WINDOW, ROWS, GROUP_WIDTH), jnp.bfloat16),
            BLOCK_KV,
        ),
        in_specs=[
            whole(pltpu.SMEM),
            head_block(MEMBERS, ROWS),
            head_block(MEMBERS, ROWS + LIST_ROWS),
            *halo,
        ],
        out_specs=(head_block(MEMBERS, ROWS), head_block(MEMBERS, ROWS), *halo),
        compiler_params=LARGE,
        name="attention",
    )(place, kv, qg, before, after)


def place_of():
    clip, tower = lax.axis_index("clip"), lax.axis_index("tower")
    group, member = lax.axis_index(("tower", "group")), lax.axis_index("member")
    shifted = (clip == lax.axis_size("clip") - 1) & (tower == 1)
    return jnp.stack([group, member, shifted.astype(jnp.int32)]).astype(jnp.int32)


def to_group(block, distance):
    clips, towers = lax.axis_size("clip"), lax.axis_size("tower")
    per_tower = lax.axis_size("group")
    groups = towers * per_tower
    route = []
    for clip in range(clips):
        for group in range(groups):
            target = group + distance
            if not 0 <= target < groups:
                continue
            turn = target // per_tower - group // per_tower if clip == clips - 1 else 0
            for member in range(MEMBERS):
                route.append(
                    (
                        (clip * groups + group) * MEMBERS + member,
                        (clip * groups + target) * MEMBERS + (member - turn) % MEMBERS,
                    )
                )
    return lax.ppermute(block, ("clip", "tower", "group", "member"), route)


def exchange(packed):
    return lax.all_to_all(packed, "member", 0, 0)


def body(
    video_query,
    video_keys,
    video_value,
    audio_query,
    audio_key,
    audio_value,
    video_cotangent,
    audio_cotangent,
    video_lists,
    audio_lists,
):
    groups = lax.axis_size(("tower", "group"))
    place = place_of()
    kv_packed = pack_kv(place, video_keys, video_value, audio_key, audio_value)
    kv = exchange(kv_packed)
    qg_packed = pack_qg(
        place,
        video_lists,
        audio_lists,
        video_query,
        audio_query,
        video_cotangent,
        audio_cotangent,
    )
    before = to_group(kv[MEMBERS - HALF_WINDOW :], 1)
    after = to_group(kv[0], -1)
    qg = exchange(qg_packed)
    qg_part, kv_part, before_part, after_part = attention(
        groups, place, kv, qg, before, after
    )
    qg_back = exchange(qg_part)
    from_after = to_group(before_part, -1)
    from_before = to_group(after_part, 1)
    kv_back = exchange(merge(kv_part, from_after, from_before))
    return unpack(place, kv_back, qg_back)


def solution(mesh):
    shape = mesh.devices.shape
    fine = Mesh(
        mesh.devices.reshape(shape[0], shape[1], shape[2] // MEMBERS, MEMBERS),
        ("clip", "tower", "group", "member"),
    )
    placed = P(("clip", "tower", "group", "member"), None)
    return jax.shard_map(
        body,
        mesh=fine,
        in_specs=(placed,) * 10,
        out_specs=(placed,) * 8,
        check_vma=False,
    )
```

time: 164 us -> 162 us (0.988)
  blocking collectives: 66.1 us -> 25.8 us
  waiting for transfers between devices: 52.8 us -> 85.4 us
  starting transfers between devices: 21 us -> 30.6 us
  Pallas kernels: 21.4 us -> 17.4 us
    all_to_all x2 -> x1, blocking collectives: 66.1 us -> 25.8 us  [exchange(): return lax.all_to_all(packed, 'member', 0, 0)]
    all_to_all x2 -> x3, waiting for transfers between devices: 43.8 us -> 74.5 us  [exchange(): return lax.all_to_all(packed, 'member', 0, 0)]
    all_to_all x2 -> x3, starting transfers between devices: 7.2 us -> 16.8 us  [exchange(): return lax.all_to_all(packed, 'member', 0, 0)]
    pallas_call x1, Pallas kernels: 15.5 us -> 8.65 us  [attention(): pl.pallas_call(functools.partial(attention_kernel, groups - 1), grid=(GRO...]
    pallas_call x2 -> x3, Pallas kernels: 4.3 us -> 6.55 us  [the longest x1 3.21 us: pack_qg(): pl.pallas_call(pack_qg_kernel, out_shape=PACKED_QG, in_specs=[whole(pltpu...]
    ppermute x4, waiting for transfers between devices: 9.01 us -> 10.9 us  [to_group(): return lax.ppermute(block, ('clip', 'tower', 'group', 'member'), route)]
  transfers between devices with their start and end apart: 6 -> 7, of which waited for: 4 -> 5; matrix products, arithmetic and copies ran while one was open for 0% -> 0% of each run, Pallas kernels for 0% -> 2%
where the time goes in v3:
time: 162 us
  waiting for transfers between devices  85.4 us (53%)
  starting transfers between devices  30.6 us (19%)
  blocking collectives  25.8 us (16%)
  Pallas kernels  17.4 us (11%)
    all_to_all x3, waiting for transfers between devices, exchange(): return lax.all_to_all(packed, 'member', 0, 0)  74.5 us
    all_to_all x1, blocking collectives, exchange(): return lax.all_to_all(packed, 'member', 0, 0)  25.8 us
    all_to_all x3, starting transfers between devices, exchange(): return lax.all_to_all(packed, 'member', 0, 0)  16.8 us
    ppermute x4, starting transfers between devices, to_group(): return lax.ppermute(block, ('clip', 'tower', 'group', 'member'), route)  13.8 us
    ppermute x4, waiting for transfers between devices, to_group(): return lax.ppermute(block, ('clip', 'tower', 'group', 'member'), route)  10.9 us
    pallas_call x1, Pallas kernels, attention(): pl.pallas_call(functools.partial(attention_kernel, groups - 1), grid=(GRO...  8.65 us
  transfers between devices with their start and end apart: 7, of which 5 were waited for; matrix products, arithmetic and copies ran while one was open for 0% of the time, Pallas kernels for 2%

profile of v3, /device:TPU:120, one launch (start us, length us, event | category | flops | bytes accessed | tf_op | source)
XLA Modules:
  0.0 161.8 jit_solution(2659353991254940557)
XLA Ops:
  0.6 0.6 pad_add_fusion.place
  1.2 3.1 %pack_kv.1 = bf16[4,384,384]{2,1,0:T(8,128)(2,1)} custom-call(s32[3]{0:T(128)} %pad_add_fusion.place, bf16[128,1536]{1,0:T(8,128)(2,1)} %vk.1, bf16[128,1536]{1,0:T(8,128)(2,1)} %vv.1, bf16[64,1536]{1,0:T(8,128)(2,1)} %ak.1, bf16[64,1536]{1,0:T(8,128)(2,1)} %av.1), custom_call_target="tpu_custom_call" | custom-call | tf_op jit(solution)/shard_map/pack_kv/pallas_call | solution.py:232
  4.4 9.4 %all-to-all-start = ((bf16[4,384,384]{2,1,0:T(8,128)(2,1)}), bf16[4,384,384]{2,1,0:T(8,128)(2,1)S(1)}, u32[]{:S(2)}, u32[]{:S(2)}) async-start(bf16[4,384,384]{2,1,0:T(8,128)(2,1)} %pack_kv.1), calls=%async_computation | async-start | bytes 2359296 | tf_op jit(solution)/shard_map/all_to_all | solution.py:336
  13.8 3.2 %pack_qg.1 = bf16[4,400,384]{2,1,0:T(8,128)(2,1)} custom-call(s32[3]{0:T(128)} %pad_add_fusion.place, s32[1,2]{1,0:T(1,128)} %video_list.1, s32[1,2]{1,0:T(1,128)} %audio_list.1, bf16[128,1536]{1,0:T(8,128)(2,1)} %vq.1, bf16[64,1536]{1,0:T(8,128)(2,1)} %aq.1, bf16[128,1536]{1,0:T(8,128)(2,1)} %vg.1, bf16[64,1536]{1,0:T(8,128)(2,1)} %ag.1), custom_call_target="tpu_custom_call" | custom-call | tf_op jit(solution)/shard_map/pack_qg/pallas_call | solution.py:244
  17.0 27.1 %all-to-all-done.kv = bf16[4,384,384]{2,1,0:T(8,128)(2,1)S(1)} async-done(((bf16[4,384,384]{2,1,0:T(8,128)(2,1)}), bf16[4,384,384]{2,1,0:T(8,128)(2,1)S(1)}, u32[]{:S(2)}, u32[]{:S(2)}) %all-to-all-start) | async-done | bytes 1179680 | tf_op jit(solution)/shard_map/all_to_all | solution.py:336
  44.1 3.5 %all-to-all-start.1 = ((bf16[4,400,384]{2,1,0:T(8,128)(2,1)}), bf16[4,400,384]{2,1,0:T(8,128)(2,1)S(1)}, u32[]{:S(2)}, u32[]{:S(2)}) async-start(bf16[4,400,384]{2,1,0:T(8,128)(2,1)} %pack_qg.1), calls=%async_computation.1 | async-start | bytes 2457600 | tf_op jit(solution)/shard_map/all_to_all | solution.py:336
  47.7 0.1 slice.8
  47.7 2.6 %collective-permute-start = (bf16[2,384,384]{2,1,0:T(8,128)(2,1)S(1)}, bf16[2,384,384]{2,1,0:T(8,128)(2,1)}, u32[]{:S(2)}, u32[]{:S(2)}) collective-permute-start(bf16[2,384,384]{2,1,0:T(8,128)(2,1)S(1)} %slice.8), channel_id=1, source_target_pairs={{0,4},{1,5},{2,6},{3,7},{4,8},{5,9},{6,10},{7,11},{8,12},{9,13},{1... | collective-permute-start | bytes 1769480 | tf_op jit(solution)/shard_map/ppermute | solution.py:332
  50.4 0.0 copy-done.2
  50.4 3.2 %collective-permute-start.1 = (bf16[384,384]{1,0:T(8,128)(2,1)S(1)}, bf16[384,384]{1,0:T(8,128)(2,1)S(1)}, u32[]{:S(2)}, u32[]{:S(2)}) collective-permute-start(bf16[384,384]{1,0:T(8,128)(2,1)S(1)} %slice_bitcast_fusion), channel_id=1, source_target_pairs={{4,0},{5,1},{6,2},{7,3},{8,4},{9,5},{10,6},{11,7},{12,8},{13,9},{1... | collective-permute-start | bytes 884744 | tf_op jit(solution)/shard_map/ppermute | solution.py:332
  53.7 26.4 %all-to-all-done.1.qg = bf16[4,400,384]{2,1,0:T(8,128)(2,1)S(1)} async-done(((bf16[4,400,384]{2,1,0:T(8,128)(2,1)}), bf16[4,400,384]{2,1,0:T(8,128)(2,1)S(1)}, u32[]{:S(2)}, u32[]{:S(2)}) %all-to-all-start.1) | async-done | bytes 1228832 | tf_op jit(solution)/shard_map/all_to_all | solution.py:336
  80.1 0.0 collective-permute-done.1.after
  80.1 0.0 collective-permute-done.before
  80.1 1.0 copy-done.3
  81.1 0.1 copy-done.4
  81.2 8.7 %attention.1 = (bf16[4,384,384]{2,1,0:T(8,128)(2,1)}, bf16[4,384,384]{2,1,0:T(8,128)(2,1)}, bf16[2,384,384]{2,1,0:T(8,128)(2,1)}, bf16[384,384]{1,0:T(8,128)(2,1)}) custom-call(s32[3]{0:T(128)} %pad_add_fusion.place, bf16[4,384,384]{2,1,0:T(8,128)(2,1)} %copy-done.2, bf16[4,400,384]{2,1,0:T(8,128)(2,1)} %copy-done.3, ...), custom_call_target="tpu_custom_call" | custom-call | tf_op jit(solution)/shard_map/attention/pallas_call | solution.py:286
  89.8 0.0 copy-start.6
  89.8 0.0 copy-start
  89.9 3.9 %all-to-all-start.3 = ((bf16[4,384,384]{2,1,0:T(8,128)(2,1)}), bf16[4,384,384]{2,1,0:T(8,128)(2,1)S(1)}, u32[]{:S(2)}, u32[]{:S(2)}) async-start(bf16[4,384,384]{2,1,0:T(8,128)(2,1)} %get-tuple-element.15), calls=%async_computation.3 | async-start | bytes 2359296 | tf_op jit(solution)/shard_map/all_to_all | solution.py:336
  93.7 0.0 copy-done.5
  93.7 1.9 %collective-permute-start.2 = (bf16[2,384,384]{2,1,0:T(8,128)(2,1)S(1)}, bf16[2,384,384]{2,1,0:T(8,128)(2,1)S(1)}, u32[]{:S(2)}, u32[]{:S(2)}) collective-permute-start(bf16[2,384,384]{2,1,0:T(8,128)(2,1)S(1)} %copy-done.5), channel_id=1, source_target_pairs={{4,0},{5,1},{6,2},{7,3},{8,4},{9,5},{10,6},{11,7},{12,8},{13,9},{1... | collective-permute-start | bytes 1769480 | tf_op jit(solution)/shard_map/ppermute | solution.py:332
  95.7 0.0 copy-done.6
  95.7 6.0 %collective-permute-start.3 = (bf16[384,384]{1,0:T(8,128)(2,1)S(1)}, bf16[384,384]{1,0:T(8,128)(2,1)S(1)}, u32[]{:S(2)}, u32[]{:S(2)}) collective-permute-start(bf16[384,384]{1,0:T(8,128)(2,1)S(1)} %copy-done.6), channel_id=1, source_target_pairs={{0,4},{1,5},{2,6},{3,7},{4,8},{5,9},{6,10},{7,11},{8,12},{9,13},{1... | collective-permute-start | bytes 884744 | tf_op jit(solution)/shard_map/ppermute | solution.py:332
  101.7 5.8 %collective-permute-done.3.from_before = bf16[384,384]{1,0:T(8,128)(2,1)S(1)} collective-permute-done((bf16[384,384]{1,0:T(8,128)(2,1)S(1)}, bf16[384,384]{1,0:T(8,128)(2,1)S(1)}, u32[]{:S(2)}, u32[]{:S(2)}) %collective-permute-start.3) | collective-permute-done | bytes 294944 | tf_op jit(solution)/shard_map/ppermute | solution.py:332
  107.5 5.1 %collective-permute-done.2.from_after = bf16[2,384,384]{2,1,0:T(8,128)(2,1)S(1)} collective-permute-done((bf16[2,384,384]{2,1,0:T(8,128)(2,1)S(1)}, bf16[2,384,384]{2,1,0:T(8,128)(2,1)S(1)}, u32[]{:S(2)}, u32[]{:S(2)}) %collective-permute-start.2) | collective-permute-done | bytes 589856 | tf_op jit(solution)/shard_map/ppermute | solution.py:332
  112.6 0.0 copy-done
  112.6 0.2 merge.1
  112.8 0.0 copy-start.1
  112.9 20.9 %all-to-all-done.3.qg = bf16[4,384,384]{2,1,0:T(8,128)(2,1)S(1)} async-done(((bf16[4,384,384]{2,1,0:T(8,128)(2,1)}), bf16[4,384,384]{2,1,0:T(8,128)(2,1)S(1)}, u32[]{:S(2)}, u32[]{:S(2)}) %all-to-all-start.3) | async-done | bytes 1179680 | tf_op jit(solution)/shard_map/all_to_all | solution.py:336
  133.8 25.8 %all_to_all.20.kv = bf16[4,384,384]{2,1,0:T(8,128)(2,1)S(1)} all-to-all(bf16[4,384,384]{2,1,0:T(8,128)(2,1)S(1)} %merge.1), channel_id=1, replica_groups=mesh['clip'=2,'tower'=2,'group'=32,'member'=4] {'member'}, dimensions={0} | all-to-all | bytes 2359296 | tf_op jit(solution)/shard_map/all_to_all | solution.py:336
  159.6 0.0 copy-done.1
  159.6 2.2 %unpack.1 = (bf16[128,1536]{1,0:T(8,128)(2,1)}, bf16[64,1536]{1,0:T(8,128)(2,1)}, bf16[128,1536]{1,0:T(8,128)(2,1)}, bf16[128,1536]{1,0:T(8,128)(2,1)}, bf16[128...) custom-call(s32[3]{0:T(128)S(1)} %copy-done.1, ...), custom_call_target="tpu_custom_call" | custom-call | tf_op jit(solution)/shard_map/unpack/pallas_call | solution.py:259
  (5 shorter events, 0.0 us)
Async XLA Ops:
  4.4 39.8 %all-to-all-start = ((bf16[4,384,384]{2,1,0:T(8,128)(2,1)}), bf16[4,384,384]{2,1,0:T(8,128)(2,1)S(1)}, u32[]{:S(2)}, u32[]{:S(2)}) async-start(bf16[4,384,384]{2,1,0:T(8,128)(2,1)} %pack_kv.1), calls=%async_computation | async-start | bytes 2359296 | tf_op jit(solution)/shard_map/all_to_all | solution.py:336
  44.1 6.2 %copy-start.2 = (bf16[4,384,384]{2,1,0:T(8,128)(2,1)}, bf16[4,384,384]{2,1,0:T(8,128)(2,1)S(1)}, u32[]{:S(2)}) copy-start(bf16[4,384,384]{2,1,0:T(8,128)(2,1)S(1)} %all-to-all-done.kv) | copy-start | bytes 3538948
  44.1 35.9 %all-to-all-start.1 = ((bf16[4,400,384]{2,1,0:T(8,128)(2,1)}), bf16[4,400,384]{2,1,0:T(8,128)(2,1)S(1)}, u32[]{:S(2)}, u32[]{:S(2)}) async-start(bf16[4,400,384]{2,1,0:T(8,128)(2,1)} %pack_qg.1), calls=%async_computation.1 | async-start | bytes 2457600 | tf_op jit(solution)/shard_map/all_to_all | solution.py:336
  47.7 32.3 %collective-permute-start = (bf16[2,384,384]{2,1,0:T(8,128)(2,1)S(1)}, bf16[2,384,384]{2,1,0:T(8,128)(2,1)}, u32[]{:S(2)}, u32[]{:S(2)}) collective-permute-start(bf16[2,384,384]{2,1,0:T(8,128)(2,1)S(1)} %slice.8), channel_id=1, source_target_pairs={{0,4},{1,5},{2,6},{3,7},{4,8},{5,9},{6,10},{7,11},{8,12},{9,13},{1... | collective-permute-start | bytes 1769480 | tf_op jit(solution)/shard_map/ppermute | solution.py:332
  50.4 29.7 %collective-permute-start.1 = (bf16[384,384]{1,0:T(8,128)(2,1)S(1)}, bf16[384,384]{1,0:T(8,128)(2,1)S(1)}, u32[]{:S(2)}, u32[]{:S(2)}) collective-permute-start(bf16[384,384]{1,0:T(8,128)(2,1)S(1)} %slice_bitcast_fusion), channel_id=1, source_target_pairs={{4,0},{5,1},{6,2},{7,3},{8,4},{9,5},{10,6},{11,7},{12,8},{13,9},{1... | collective-permute-start | bytes 884744 | tf_op jit(solution)/shard_map/ppermute | solution.py:332
  80.1 1.1 copy-start.3
  80.1 1.1 copy-start.4
  89.8 3.9 %copy-start.5 = (bf16[2,384,384]{2,1,0:T(8,128)(2,1)S(1)}, bf16[2,384,384]{2,1,0:T(8,128)(2,1)}, u32[]{:S(2)}) copy-start(bf16[2,384,384]{2,1,0:T(8,128)(2,1)} %get-tuple-element.13) | copy-start | bytes 1769476
  89.8 5.8 %copy-start.6 = (bf16[384,384]{1,0:T(8,128)(2,1)S(1)}, bf16[384,384]{1,0:T(8,128)(2,1)}, u32[]{:S(2)}) copy-start(bf16[384,384]{1,0:T(8,128)(2,1)} %get-tuple-element.14) | copy-start | bytes 884740
  89.8 22.8 %copy-start = (bf16[4,384,384]{2,1,0:T(8,128)(2,1)S(1)}, bf16[4,384,384]{2,1,0:T(8,128)(2,1)}, u32[]{:S(2)}) copy-start(bf16[4,384,384]{2,1,0:T(8,128)(2,1)} %get-tuple-element.12.own) | copy-start | bytes 3538948
  89.9 43.9 %all-to-all-start.3 = ((bf16[4,384,384]{2,1,0:T(8,128)(2,1)}), bf16[4,384,384]{2,1,0:T(8,128)(2,1)S(1)}, u32[]{:S(2)}, u32[]{:S(2)}) async-start(bf16[4,384,384]{2,1,0:T(8,128)(2,1)} %get-tuple-element.15), calls=%async_computation.3 | async-start | bytes 2359296 | tf_op jit(solution)/shard_map/all_to_all | solution.py:336
  93.7 18.9 %collective-permute-start.2 = (bf16[2,384,384]{2,1,0:T(8,128)(2,1)S(1)}, bf16[2,384,384]{2,1,0:T(8,128)(2,1)S(1)}, u32[]{:S(2)}, u32[]{:S(2)}) collective-permute-start(bf16[2,384,384]{2,1,0:T(8,128)(2,1)S(1)} %copy-done.5), channel_id=1, source_target_pairs={{4,0},{5,1},{6,2},{7,3},{8,4},{9,5},{10,6},{11,7},{12,8},{13,9},{1... | collective-permute-start | bytes 1769480 | tf_op jit(solution)/shard_map/ppermute | solution.py:332
  95.7 11.8 %collective-permute-start.3 = (bf16[384,384]{1,0:T(8,128)(2,1)S(1)}, bf16[384,384]{1,0:T(8,128)(2,1)S(1)}, u32[]{:S(2)}, u32[]{:S(2)}) collective-permute-start(bf16[384,384]{1,0:T(8,128)(2,1)S(1)} %copy-done.6), channel_id=1, source_target_pairs={{0,4},{1,5},{2,6},{3,7},{4,8},{5,9},{6,10},{7,11},{8,12},{9,13},{1... | collective-permute-start | bytes 884744 | tf_op jit(solution)/shard_map/ppermute | solution.py:332
  112.8 46.8 %copy-start.1 = (s32[3]{0:T(128)S(1)}, s32[3]{0:T(128)}, u32[]{:S(2)}) copy-start(s32[3]{0:T(128)} %pad_add_fusion.place) | copy-start | bytes 40

commit v4 on v3

--- a/solution.py
+++ b/solution.py
@@ -50,19 +50,19 @@
         row += rows
 
 
-def pack_kv_kernel(place, vk, vv, ak, av, out, sems):
+def pack_kv_kernel(shift, vk, vv, ak, av, out, sems):
     copies = []
     for member in range(MEMBERS):
-        first = lax.rem(place[2] + member, MEMBERS) * GROUP_WIDTH
+        first = lax.rem(shift[0] + member, MEMBERS) * GROUP_WIDTH
         start_packing(copies, sems.at[member], first, (vk, vv, ak, av), out.at[member])
     for copy in copies:
         copy.wait()
 
 
-def pack_qg_kernel(place, video_list, audio_list, vq, aq, vg, ag, out, sems):
+def pack_qg_kernel(shift, video_list, audio_list, vq, aq, vg, ag, out, sems):
     copies = []
     for member in range(MEMBERS):
-        first = lax.rem(place[2] + member, MEMBERS) * GROUP_WIDTH
+        first = lax.rem(shift[0] + member, MEMBERS) * GROUP_WIDTH
         start_packing(copies, sems.at[member], first, (vq, aq, vg, ag), out.at[member])
     video_first = jnp.full((8, GROUP_WIDTH), video_list[0, 0].astype(jnp.float32))
     audio_first = jnp.full((8, GROUP_WIDTH), audio_list[0, 0].astype(jnp.float32))
@@ -73,9 +73,9 @@
         copy.wait()
 
 
-def unpack_kernel(place, kv, qg, vo, ao, vqg, vkg, vvg, aqg, akg, avg):
+def unpack_kernel(shift, kv, qg, vo, ao, vqg, vkg, vvg, aqg, akg, avg):
     for member in range(MEMBERS):
-        first = lax.rem(place[2] + member, MEMBERS) * GROUP_WIDTH
+        first = lax.rem(shift[0] + member, MEMBERS) * GROUP_WIDTH
         columns = pl.ds(pl.multiple_of(first, GROUP_WIDTH), GROUP_WIDTH)
         vo[:, columns] = qg[member, 0:128]
         ao[:, columns] = qg[member, 128:192]
@@ -87,14 +87,22 @@
         avg[:, columns] = kv[member, 320:384]
 
 
-def merge_kernel(own, from_after, from_before, out):
-    out[0] = (own[0].astype(jnp.float32) + from_before[...].astype(jnp.float32)).astype(
-        jnp.bfloat16
-    )
+def merge_kernel(
+    last_group, group_ref, own, from_after_2, from_after_3, relayed_3, from_before, out
+):
+    def total(member, *received):
+        parts = [own[member].astype(jnp.float32)]
+        parts += [r[...].astype(jnp.float32) for r in received]
+        out[member] = sum(parts).astype(jnp.bfloat16)
+
+    total(0, from_before)
     out[1] = own[1]
-    out[2:4] = (own[2:4].astype(jnp.float32) + from_after[...].astype(jnp.float32)).astype(
-        jnp.bfloat16
-    )
+    total(2, from_after_2)
+    total(3, relayed_3)
+
+    @pl.when(group_ref[0] != last_group)
+    def _():
+        total(3, from_after_3, relayed_3)
 
 
 def stacked(parts):
@@ -131,13 +139,26 @@
 
 
 def attention_kernel(
-    last_group, place, kv, qg, before, after, qg_out, kv_out, before_out, after_out
+    last_group,
+    group_ref,
+    kv,
+    qg,
+    before_2,
+    before_3,
+    relayed_3,
+    after,
+    qg_out,
+    kv_out,
+    before_2_out,
+    before_3_out,
+    after_out,
+    before_sum,
 ):
-    group = place[0]
+    group = group_ref[0]
+    before_sum[...] = before_3[...] + relayed_3[...]
     members = range(MEMBERS)
-    sources = [before.at[0], before.at[1]] + [kv.at[m] for m in members] + [after]
-    targets = [before_out.at[0], before_out.at[1]]
-    targets += [kv_out.at[m] for m in members] + [after_out]
+    sources = [before_2, before_sum] + [kv.at[m] for m in members] + [after]
+    targets = [before_2_out, before_3_out] + [kv_out.at[m] for m in members] + [after_out]
     bias_before = jnp.where(group == 0, MASKED, 0.0)
     bias_after = jnp.where(group == last_group, MASKED, 0.0)
 
@@ -228,7 +249,7 @@
 PACKED_QG = jax.ShapeDtypeStruct((MEMBERS, ROWS + LIST_ROWS, GROUP_WIDTH), jnp.bfloat16)
 
 
-def pack_kv(place, *arrays):
+def pack_kv(shift, *arrays):
     return pl.pallas_call(
         pack_kv_kernel,
         out_shape=PACKED_KV,
@@ -237,10 +258,10 @@
         scratch_shapes=[pltpu.SemaphoreType.DMA((MEMBERS, 4))],
         compiler_params=LARGE,
         name="pack_kv",
-    )(place, *arrays)
-
-
-def pack_qg(place, *arrays):
+    )(shift, *arrays)
+
+
+def pack_qg(shift, *arrays):
     return pl.pallas_call(
         pack_qg_kernel,
         out_shape=PACKED_QG,
@@ -249,10 +270,10 @@
         scratch_shapes=[pltpu.SemaphoreType.DMA((MEMBERS, 4))],
         compiler_params=LARGE,
         name="pack_qg",
-    )(place, *arrays)
-
-
-def unpack(place, kv, qg):
+    )(shift, *arrays)
+
+
+def unpack(shift, kv, qg):
     video = jax.ShapeDtypeStruct((VIDEO, HEADS * HEAD_SIZE), jnp.bfloat16)
     audio = jax.ShapeDtypeStruct((AUDIO, HEADS * HEAD_SIZE), jnp.bfloat16)
     shapes = (video, audio, video, video, video, audio, audio, audio)
@@ -263,73 +284,87 @@
         out_specs=[whole()] * 8,
         compiler_params=SMALL,
         name="unpack",
-    )(place, kv, qg)
-
-
-def merge(own, from_after, from_before):
+    )(shift, kv, qg)
+
+
+def merge(groups, group, *arrays):
     return pl.pallas_call(
-        merge_kernel,
+        functools.partial(merge_kernel, groups - 1),
         out_shape=PACKED_KV,
-        in_specs=[whole()] * 3,
+        in_specs=[whole(pltpu.SMEM)] + [whole()] * 5,
         out_specs=whole(),
         compiler_params=SMALL,
         name="merge",
-    )(own, from_after, from_before)
-
-
-def attention(groups, place, kv, qg, before, after):
+    )(group, *arrays)
+
+
+def attention(groups, group, *arrays):
     def head_block(*leading):
         zeros = (0,) * len(leading)
         return pl.BlockSpec(leading + (HEAD_SIZE,), lambda head: zeros + (head,))
 
-    halo = (head_block(HALF_WINDOW, ROWS), head_block(ROWS))
     return pl.pallas_call(
         functools.partial(attention_kernel, groups - 1),
         grid=(GROUP_HEADS,),
-        out_shape=(
-            PACKED_KV,
-            PACKED_KV,
-            jax.ShapeDtypeStruct((HALF_WINDOW, ROWS, GROUP_WIDTH), jnp.bfloat16),
-            BLOCK_KV,
-        ),
+        out_shape=[PACKED_KV] * 2 + [BLOCK_KV] * 3,
         in_specs=[
             whole(pltpu.SMEM),
             head_block(MEMBERS, ROWS),
             head_block(MEMBERS, ROWS + LIST_ROWS),
-            *halo,
+            *[head_block(ROWS)] * 4,
         ],
-        out_specs=(head_block(MEMBERS, ROWS), head_block(MEMBERS, ROWS), *halo),
+        out_specs=[head_block(MEMBERS, ROWS)] * 2 + [head_block(ROWS)] * 3,
+        scratch_shapes=[pltpu.VMEM((ROWS, HEAD_SIZE), jnp.bfloat16)],
         compiler_params=LARGE,
         name="attention",
-    )(place, kv, qg, before, after)
-
-
-def place_of():
+    )(group, *arrays)
+
+
+def slice_shift():
     clip, tower = lax.axis_index("clip"), lax.axis_index("tower")
-    group, member = lax.axis_index(("tower", "group")), lax.axis_index("member")
     shifted = (clip == lax.axis_size("clip") - 1) & (tower == 1)
-    return jnp.stack([group, member, shifted.astype(jnp.int32)]).astype(jnp.int32)
-
-
-def to_group(block, distance):
+    return jnp.where(shifted, 1, 0).astype(jnp.int32).reshape(1)
+
+
+def moved(block, hops):
     clips, towers = lax.axis_size("clip"), lax.axis_size("tower")
     per_tower = lax.axis_size("group")
-    groups = towers * per_tower
     route = []
     for clip in range(clips):
-        for group in range(groups):
-            target = group + distance
-            if not 0 <= target < groups:
-                continue
+        for group, target in hops:
             turn = target // per_tower - group // per_tower if clip == clips - 1 else 0
             for member in range(MEMBERS):
                 route.append(
                     (
-                        (clip * groups + group) * MEMBERS + member,
-                        (clip * groups + target) * MEMBERS + (member - turn) % MEMBERS,
+                        (clip * towers * per_tower + group) * MEMBERS + member,
+                        (clip * towers * per_tower + target) * MEMBERS
+                        + (member - turn) % MEMBERS,
                     )
                 )
     return lax.ppermute(block, ("clip", "tower", "group", "member"), route)
+
+
+def to_group(block, distance):
+    groups = lax.axis_size(("tower", "group"))
+    hops = [(g, g + distance) for g in range(groups) if 0 <= g + distance < groups]
+    return moved(block, hops)
+
+
+def to_group_by_relay(block, distance):
+    groups, per_tower = lax.axis_size(("tower", "group")), lax.axis_size("group")
+    relay = 0 if distance > 0 else groups - 1
+    first, second = [], []
+    for group in range(groups):
+        target = group + distance
+        if not 0 <= target < groups:
+            continue
+        if group // per_tower == target // per_tower:
+            first.append((group, target))
+        else:
+            first.append((group, relay))
+            second.append((relay, target))
+    arrived = moved(block, first)
+    return arrived, moved(arrived, second)
 
 
 def exchange(packed):
@@ -349,11 +384,12 @@
     audio_lists,
 ):
     groups = lax.axis_size(("tower", "group"))
-    place = place_of()
-    kv_packed = pack_kv(place, video_keys, video_value, audio_key, audio_value)
+    group = lax.axis_index(("tower", "group")).astype(jnp.int32).reshape(1)
+    shift = slice_shift()
+    kv_packed = pack_kv(shift, video_keys, video_value, audio_key, audio_value)
     kv = exchange(kv_packed)
     qg_packed = pack_qg(
-        place,
+        shift,
         video_lists,
         audio_lists,
         video_query,
@@ -361,17 +397,22 @@
         video_cotangent,
         audio_cotangent,
     )
-    before = to_group(kv[MEMBERS - HALF_WINDOW :], 1)
+    before_3, relayed_3 = to_group_by_relay(kv[3], 1)
+    before_2 = to_group(kv[2], 1)
     after = to_group(kv[0], -1)
     qg = exchange(qg_packed)
-    qg_part, kv_part, before_part, after_part = attention(
-        groups, place, kv, qg, before, after
+    qg_part, kv_part, part_2, part_3, after_part = attention(
+        groups, group, kv, qg, before_2, before_3, relayed_3, after
     )
     qg_back = exchange(qg_part)
-    from_after = to_group(before_part, -1)
+    from_after_3, relayed_back = to_group_by_relay(part_3, -1)
+    from_after_2 = to_group(part_2, -1)
     from_before = to_group(after_part, 1)
-    kv_back = exchange(merge(kv_part, from_after, from_before))
-    return unpack(place, kv_back, qg_back)
+    merged = merge(
+        groups, group, kv_part, from_after_2, from_after_3, relayed_back, from_before
+    )
+    kv_back = exchange(merged)
+    return unpack(shift, kv_back, qg_back)
 
 
 def solution(mesh):

time: 162 us -> 158 us (0.975)
  waiting for transfers between devices: 85.4 us -> 69.2 us
  starting transfers between devices: 30.6 us -> 38.6 us
  blocking collectives: 25.8 us -> 30.8 us
    all_to_all x3, waiting for transfers between devices: 74.5 us -> 60.3 us  [exchange(): return lax.all_to_all(packed, 'member', 0, 0)]
    ppermute x4 -> x8, starting transfers between devices: 13.8 us -> 21.8 us  [moved(): return lax.ppermute(block, ('clip', 'tower', 'group', 'member'), route)]
    all_to_all x1, blocking collectives: 25.8 us -> 30.8 us  [exchange(): return lax.all_to_all(packed, 'member', 0, 0)]
    ppermute x4 -> x8, waiting for transfers between devices: 10.9 us -> 8.9 us  [moved(): return lax.ppermute(block, ('clip', 'tower', 'group', 'member'), route)]
  transfers between devices with their start and end apart: 7 -> 11, of which waited for: 5 -> 6; matrix products, arithmetic and copies ran while one was open for 0% -> 0% of each run, Pallas kernels for 2% -> 2%
where the time goes in v4:
time: 158 us; the launch traced here: 157 us
  waiting for transfers between devices  69.2 us (44%)
  starting transfers between devices  38.6 us (24%)
  blocking collectives  30.8 us (19%)
  Pallas kernels  16.4 us (10%)
    all_to_all x3, waiting for transfers between devices, exchange(): return lax.all_to_all(packed, 'member', 0, 0)  60.3 us
    all_to_all x1, blocking collectives, exchange(): return lax.all_to_all(packed, 'member', 0, 0)  30.8 us
    ppermute x8, starting transfers between devices, moved(): return lax.ppermute(block, ('clip', 'tower', 'group', 'member'), route)  21.8 us
    all_to_all x3, starting transfers between devices, exchange(): return lax.all_to_all(packed, 'member', 0, 0)  16.8 us
    ppermute x8, waiting for transfers between devices, moved(): return lax.ppermute(block, ('clip', 'tower', 'group', 'member'), route)  8.9 us
    pallas_call x1, Pallas kernels, attention(): pl.pallas_call(functools.partial(attention_kernel, groups - 1), grid=(GRO...  8.81 us
    pallas_call x1, Pallas kernels, pack_qg(): pl.pallas_call(pack_qg_kernel, out_shape=PACKED_QG, in_specs=[whole(pltpu...  3.2 us
  transfers between devices with their start and end apart: 11, of which 6 were waited for; matrix products, arithmetic and copies ran while one was open for 0% of the time, Pallas kernels for 2%

profile of v4, /device:TPU:120, one launch (start us, length us, event | category | flops | bytes accessed | tf_op | source)
XLA Modules:
  0.0 157.3 jit_solution(6039092827457381370)
XLA Ops:
  0.6 2.5 %pack_kv.1 = bf16[4,384,384]{2,1,0:T(8,128)(2,1)} custom-call(s32[1]{0:T(128)} %bitcast.shift, bf16[128,1536]{1,0:T(8,128)(2,1)} %vk.1, bf16[128,1536]{1,0:T(8,128)(2,1)} %vv.1, bf16[64,1536]{1,0:T(8,128)(2,1)} %ak.1, bf16[64,1536]{1,0:T(8,128)(2,1)} %av.1), custom_call_target="tpu_custom_call" | custom-call | tf_op jit(solution)/shard_map/pack_kv/pallas_call | solution.py:253
  3.1 9.4 %all-to-all-start = ((bf16[4,384,384]{2,1,0:T(8,128)(2,1)}), bf16[4,384,384]{2,1,0:T(8,128)(2,1)S(1)}, u32[]{:S(2)}, u32[]{:S(2)}) async-start(bf16[4,384,384]{2,1,0:T(8,128)(2,1)} %pack_kv.1), calls=%async_computation | async-start | bytes 2359296 | tf_op jit(solution)/shard_map/all_to_all | solution.py:371
  12.5 3.2 %pack_qg.1 = bf16[4,400,384]{2,1,0:T(8,128)(2,1)} custom-call(s32[1]{0:T(128)} %bitcast.shift, s32[1,2]{1,0:T(1,128)} %video_list.1, s32[1,2]{1,0:T(1,128)} %audio_list.1, bf16[128,1536]{1,0:T(8,128)(2,1)} %vq.1, bf16[64,1536]{1,0:T(8,128)(2,1)} %aq.1, bf16[128,1536]{1,0:T(8,128)(2,1)} %vg.1, bf16[64,1536]{1,0:T(8,128)(2,1)} %ag.1), custom_call_target="tpu_custom_call" | custom-call | tf_op jit(solution)/shard_map/pack_qg/pallas_call | solution.py:265
  15.8 27.2 %all-to-all-done.kv = bf16[4,384,384]{2,1,0:T(8,128)(2,1)S(1)} async-done(((bf16[4,384,384]{2,1,0:T(8,128)(2,1)}), bf16[4,384,384]{2,1,0:T(8,128)(2,1)S(1)}, u32[]{:S(2)}, u32[]{:S(2)}) %all-to-all-start) | async-done | bytes 1179680 | tf_op jit(solution)/shard_map/all_to_all | solution.py:371
  42.9 3.5 %all-to-all-start.1 = ((bf16[4,400,384]{2,1,0:T(8,128)(2,1)}), bf16[4,400,384]{2,1,0:T(8,128)(2,1)S(1)}, u32[]{:S(2)}, u32[]{:S(2)}) async-start(bf16[4,400,384]{2,1,0:T(8,128)(2,1)} %pack_qg.1), calls=%async_computation.1 | async-start | bytes 2457600 | tf_op jit(solution)/shard_map/all_to_all | solution.py:371
  46.5 0.1 slice_bitcast_fusion
  46.6 2.6 %collective-permute-start.1 = (bf16[384,384]{1,0:T(8,128)(2,1)S(1)}, bf16[384,384]{1,0:T(8,128)(2,1)S(1)}, u32[]{:S(2)}, u32[]{:S(2)}) collective-permute-start(bf16[384,384]{1,0:T(8,128)(2,1)S(1)} %get-tuple-element.19), channel_id=1, source_target_pairs={{0,4},{1,5},{2,6},{3,7},{4,8},{5,9},{6,10},{7,11},{8,12},{9,13},{1... | collective-permute-start | bytes 884744 | tf_op jit(solution)/shard_map/ppermute | solution.py:344
  49.2 3.2 %collective-permute-start.3 = (bf16[384,384]{1,0:T(8,128)(2,1)S(1)}, bf16[384,384]{1,0:T(8,128)(2,1)S(1)}, u32[]{:S(2)}, u32[]{:S(2)}) collective-permute-start(bf16[384,384]{1,0:T(8,128)(2,1)S(1)} %get-tuple-element.18), channel_id=1, source_target_pairs={{4,0},{5,1},{6,2},{7,3},{8,4},{9,5},{10,6},{11,7},{12,8},{13,9},{1... | collective-permute-start | bytes 884744 | tf_op jit(solution)/shard_map/ppermute | solution.py:344
  52.4 4.7 %collective-permute-start = (bf16[384,384]{1,0:T(8,128)(2,1)S(1)}, bf16[384,384]{1,0:T(8,128)(2,1)S(1)}, u32[]{:S(2)}, u32[]{:S(2)}) collective-permute-start(bf16[384,384]{1,0:T(8,128)(2,1)S(1)} %get-tuple-element.20), channel_id=1, source_target_pairs={{0,4},{1,5},{2,6},{3,7},{4,8},{5,9},{6,10},{7,11},{8,12},{9,13},{1... | collective-permute-start | bytes 884744 | tf_op jit(solution)/shard_map/ppermute | solution.py:344
  57.1 0.6 collective-permute-done.1.before_3
  57.7 0.7 collective-permute-start.2
  58.4 20.4 %all-to-all-done.1.qg = bf16[4,400,384]{2,1,0:T(8,128)(2,1)S(1)} async-done(((bf16[4,400,384]{2,1,0:T(8,128)(2,1)}), bf16[4,400,384]{2,1,0:T(8,128)(2,1)S(1)}, u32[]{:S(2)}, u32[]{:S(2)}) %all-to-all-start.1) | async-done | bytes 1228832 | tf_op jit(solution)/shard_map/all_to_all | solution.py:371
  78.8 0.0 collective-permute-done.3.after
  78.8 0.0 collective-permute-done.before_2
  78.8 0.0 copy-start.5
  78.8 0.0 copy-start.6
  78.9 1.0 copy-done.2
  79.9 0.1 copy-done.4
  79.9 0.1 copy-done.5
  80.0 0.1 copy-done.6
  80.1 8.8 %attention.1 = (bf16[4,384,384]{2,1,0:T(8,128)(2,1)}, bf16[4,384,384]{2,1,0:T(8,128)(2,1)}, bf16[384,384]{1,0:T(8,128)(2,1)}, bf16[384,384]{1,0:T(8,128)(2,1)}, bf16[384,384]{1,0:T(8,128)(2,1)}) custom-call(s32[1]{0:T(128)} %bitcast.1.group_ref, bf16[4,384,384]{2,1,0:T(8,128)(2,1)} %copy-done.1, bf16[4,400,384]{2,1,0:T(8,128)(2,1)} %copy-done.2, ...), custom_call_target="tpu_custom_call" | custom-call | tf_op jit(solution)/shard_map/attention/pallas_call | solution.py:306
  89.0 3.9 %all-to-all-start.3 = ((bf16[4,384,384]{2,1,0:T(8,128)(2,1)}), bf16[4,384,384]{2,1,0:T(8,128)(2,1)S(1)}, u32[]{:S(2)}, u32[]{:S(2)}) async-start(bf16[4,384,384]{2,1,0:T(8,128)(2,1)} %get-tuple-element.17), calls=%async_computation.3 | async-start | bytes 2359296 | tf_op jit(solution)/shard_map/all_to_all | solution.py:371
  92.8 1.9 %collective-permute-start.5 = (bf16[384,384]{1,0:T(8,128)(2,1)S(1)}, bf16[384,384]{1,0:T(8,128)(2,1)S(1)}, u32[]{:S(2)}, u32[]{:S(2)}) collective-permute-start(bf16[384,384]{1,0:T(8,128)(2,1)S(1)} %copy-done.9), channel_id=1, source_target_pairs={{4,0},{5,1},{6,2},{7,3},{8,4},{9,5},{10,6},{11,7},{12,8},{13,9},{1... | collective-permute-start | bytes 884744 | tf_op jit(solution)/shard_map/ppermute | solution.py:344
  94.7 1.9 %collective-permute-start.4 = (bf16[384,384]{1,0:T(8,128)(2,1)S(1)}, bf16[384,384]{1,0:T(8,128)(2,1)S(1)}, u32[]{:S(2)}, u32[]{:S(2)}) collective-permute-start(bf16[384,384]{1,0:T(8,128)(2,1)S(1)} %copy-done.8), channel_id=1, source_target_pairs={{4,0},{5,1},{6,2},{7,3},{8,4},{9,5},{10,6},{11,7},{12,8},{13,9},{1... | collective-permute-start | bytes 884744 | tf_op jit(solution)/shard_map/ppermute | solution.py:344
  96.7 6.0 %collective-permute-start.7 = (bf16[384,384]{1,0:T(8,128)(2,1)S(1)}, bf16[384,384]{1,0:T(8,128)(2,1)S(1)}, u32[]{:S(2)}, u32[]{:S(2)}) collective-permute-start(bf16[384,384]{1,0:T(8,128)(2,1)S(1)} %copy-done.7), channel_id=1, source_target_pairs={{0,4},{1,5},{2,6},{3,7},{4,8},{5,9},{6,10},{7,11},{8,12},{9,13},{1... | collective-permute-start | bytes 884744 | tf_op jit(solution)/shard_map/ppermute | solution.py:344
  102.7 4.0 %collective-permute-done.5.from_after_3 = bf16[384,384]{1,0:T(8,128)(2,1)S(1)} collective-permute-done((bf16[384,384]{1,0:T(8,128)(2,1)S(1)}, bf16[384,384]{1,0:T(8,128)(2,1)S(1)}, u32[]{:S(2)}, u32[]{:S(2)}) %collective-permute-start.5) | collective-permute-done | bytes 294944 | tf_op jit(solution)/shard_map/ppermute | solution.py:344
  106.7 0.7 collective-permute-start.6
  107.4 4.3 %collective-permute-done.4.from_after_2 = bf16[384,384]{1,0:T(8,128)(2,1)S(1)} collective-permute-done((bf16[384,384]{1,0:T(8,128)(2,1)S(1)}, bf16[384,384]{1,0:T(8,128)(2,1)S(1)}, u32[]{:S(2)}, u32[]{:S(2)}) %collective-permute-start.4) | collective-permute-done | bytes 294944 | tf_op jit(solution)/shard_map/ppermute | solution.py:344
  111.7 0.3 merge.1
  112.1 12.8 %all-to-all-done.3.qg = bf16[4,384,384]{2,1,0:T(8,128)(2,1)S(1)} async-done(((bf16[4,384,384]{2,1,0:T(8,128)(2,1)}), bf16[4,384,384]{2,1,0:T(8,128)(2,1)S(1)}, u32[]{:S(2)}, u32[]{:S(2)}) %all-to-all-start.3) | async-done | bytes 1179680 | tf_op jit(solution)/shard_map/all_to_all | solution.py:371
  124.8 30.8 %all_to_all.20.kv = bf16[4,384,384]{2,1,0:T(8,128)(2,1)S(1)} all-to-all(bf16[4,384,384]{2,1,0:T(8,128)(2,1)S(1)} %merge.1), channel_id=1, replica_groups=mesh['clip'=2,'tower'=2,'group'=32,'member'=4] {'member'}, dimensions={0} | all-to-all | bytes 2359296 | tf_op jit(solution)/shard_map/all_to_all | solution.py:371
  155.7 1.6 %unpack.1 = (bf16[128,1536]{1,0:T(8,128)(2,1)}, bf16[64,1536]{1,0:T(8,128)(2,1)}, bf16[128,1536]{1,0:T(8,128)(2,1)}, bf16[128,1536]{1,0:T(8,128)(2,1)}, bf16[128...) custom-call(s32[1]{0:T(128)} %bitcast.shift, ...), custom_call_target="tpu_custom_call" | custom-call | tf_op jit(solution)/shard_map/unpack/pallas_call | solution.py:280
  (17 shorter events, 0.0 us)
Async XLA Ops:
  3.1 39.8 %all-to-all-start = ((bf16[4,384,384]{2,1,0:T(8,128)(2,1)}), bf16[4,384,384]{2,1,0:T(8,128)(2,1)S(1)}, u32[]{:S(2)}, u32[]{:S(2)}) async-start(bf16[4,384,384]{2,1,0:T(8,128)(2,1)} %pack_kv.1), calls=%async_computation | async-start | bytes 2359296 | tf_op jit(solution)/shard_map/all_to_all | solution.py:371
  42.9 3.5 %copy-start.1 = (bf16[4,384,384]{2,1,0:T(8,128)(2,1)}, bf16[4,384,384]{2,1,0:T(8,128)(2,1)S(1)}, u32[]{:S(2)}) copy-start(bf16[4,384,384]{2,1,0:T(8,128)(2,1)S(1)} %all-to-all-done.kv) | copy-start | bytes 3538948
  42.9 35.9 %all-to-all-start.1 = ((bf16[4,400,384]{2,1,0:T(8,128)(2,1)}), bf16[4,400,384]{2,1,0:T(8,128)(2,1)S(1)}, u32[]{:S(2)}, u32[]{:S(2)}) async-start(bf16[4,400,384]{2,1,0:T(8,128)(2,1)} %pack_qg.1), calls=%async_computation.1 | async-start | bytes 2457600 | tf_op jit(solution)/shard_map/all_to_all | solution.py:371
  46.6 11.1 %collective-permute-start.1 = (bf16[384,384]{1,0:T(8,128)(2,1)S(1)}, bf16[384,384]{1,0:T(8,128)(2,1)S(1)}, u32[]{:S(2)}, u32[]{:S(2)}) collective-permute-start(bf16[384,384]{1,0:T(8,128)(2,1)S(1)} %get-tuple-element.19), channel_id=1, source_target_pairs={{0,4},{1,5},{2,6},{3,7},{4,8},{5,9},{6,10},{7,11},{8,12},{9,13},{1... | collective-permute-start | bytes 884744 | tf_op jit(solution)/shard_map/ppermute | solution.py:344
  49.2 29.6 %collective-permute-start.3 = (bf16[384,384]{1,0:T(8,128)(2,1)S(1)}, bf16[384,384]{1,0:T(8,128)(2,1)S(1)}, u32[]{:S(2)}, u32[]{:S(2)}) collective-permute-start(bf16[384,384]{1,0:T(8,128)(2,1)S(1)} %get-tuple-element.18), channel_id=1, source_target_pairs={{4,0},{5,1},{6,2},{7,3},{8,4},{9,5},{10,6},{11,7},{12,8},{13,9},{1... | collective-permute-start | bytes 884744 | tf_op jit(solution)/shard_map/ppermute | solution.py:344
  52.4 26.4 %collective-permute-start = (bf16[384,384]{1,0:T(8,128)(2,1)S(1)}, bf16[384,384]{1,0:T(8,128)(2,1)S(1)}, u32[]{:S(2)}, u32[]{:S(2)}) collective-permute-start(bf16[384,384]{1,0:T(8,128)(2,1)S(1)} %get-tuple-element.20), channel_id=1, source_target_pairs={{0,4},{1,5},{2,6},{3,7},{4,8},{5,9},{6,10},{7,11},{8,12},{9,13},{1... | collective-permute-start | bytes 884744 | tf_op jit(solution)/shard_map/ppermute | solution.py:344
  57.7 21.1 %copy-start.3 = (bf16[384,384]{1,0:T(8,128)(2,1)}, bf16[384,384]{1,0:T(8,128)(2,1)S(1)}, u32[]{:S(2)}) copy-start(bf16[384,384]{1,0:T(8,128)(2,1)S(1)} %collective-permute-done.1.before_3) | copy-start | bytes 884740
  57.7 21.1 %collective-permute-start.2 = (bf16[384,384]{1,0:T(8,128)(2,1)S(1)}, bf16[384,384]{1,0:T(8,128)(2,1)S(1)}, u32[]{:S(2)}, u32[]{:S(2)}) collective-permute-start(bf16[384,384]{1,0:T(8,128)(2,1)S(1)} %collective-permute-done.1.before_3), channel_id=1, source_target_pairs={{0,128},{1,129},{2,130},{3,131},{256,387},{257,384},{258,385},{259... | collective-permute-start | bytes 884744 | tf_op jit(solution)/shard_map/ppermute | solution.py:344
  78.8 1.1 copy-start.2
  78.8 1.1 copy-start.4
  78.8 1.2 copy-start.5
  78.8 1.3 copy-start.6
  88.9 3.9 %copy-start.9 = (bf16[384,384]{1,0:T(8,128)(2,1)S(1)}, bf16[384,384]{1,0:T(8,128)(2,1)}, u32[]{:S(2)}) copy-start(bf16[384,384]{1,0:T(8,128)(2,1)} %get-tuple-element.15) | copy-start | bytes 884740
  88.9 5.8 %copy-start.8 = (bf16[384,384]{1,0:T(8,128)(2,1)S(1)}, bf16[384,384]{1,0:T(8,128)(2,1)}, u32[]{:S(2)}) copy-start(bf16[384,384]{1,0:T(8,128)(2,1)} %get-tuple-element.14) | copy-start | bytes 884740
  88.9 7.7 %copy-start.7 = (bf16[384,384]{1,0:T(8,128)(2,1)S(1)}, bf16[384,384]{1,0:T(8,128)(2,1)}, u32[]{:S(2)}) copy-start(bf16[384,384]{1,0:T(8,128)(2,1)} %get-tuple-element.16) | copy-start | bytes 884740
  88.9 22.8 %copy-start = (bf16[4,384,384]{2,1,0:T(8,128)(2,1)S(1)}, bf16[4,384,384]{2,1,0:T(8,128)(2,1)}, u32[]{:S(2)}) copy-start(bf16[4,384,384]{2,1,0:T(8,128)(2,1)} %get-tuple-element.13.own) | copy-start | bytes 3538948
  89.0 35.9 %all-to-all-start.3 = ((bf16[4,384,384]{2,1,0:T(8,128)(2,1)}), bf16[4,384,384]{2,1,0:T(8,128)(2,1)S(1)}, u32[]{:S(2)}, u32[]{:S(2)}) async-start(bf16[4,384,384]{2,1,0:T(8,128)(2,1)} %get-tuple-element.17), calls=%async_computation.3 | async-start | bytes 2359296 | tf_op jit(solution)/shard_map/all_to_all | solution.py:371
  92.8 13.9 %collective-permute-start.5 = (bf16[384,384]{1,0:T(8,128)(2,1)S(1)}, bf16[384,384]{1,0:T(8,128)(2,1)S(1)}, u32[]{:S(2)}, u32[]{:S(2)}) collective-permute-start(bf16[384,384]{1,0:T(8,128)(2,1)S(1)} %copy-done.9), channel_id=1, source_target_pairs={{4,0},{5,1},{6,2},{7,3},{8,4},{9,5},{10,6},{11,7},{12,8},{13,9},{1... | collective-permute-start | bytes 884744 | tf_op jit(solution)/shard_map/ppermute | solution.py:344
  94.7 17.0 %collective-permute-start.4 = (bf16[384,384]{1,0:T(8,128)(2,1)S(1)}, bf16[384,384]{1,0:T(8,128)(2,1)S(1)}, u32[]{:S(2)}, u32[]{:S(2)}) collective-permute-start(bf16[384,384]{1,0:T(8,128)(2,1)S(1)} %copy-done.8), channel_id=1, source_target_pairs={{4,0},{5,1},{6,2},{7,3},{8,4},{9,5},{10,6},{11,7},{12,8},{13,9},{1... | collective-permute-start | bytes 884744 | tf_op jit(solution)/shard_map/ppermute | solution.py:344
  96.7 15.0 %collective-permute-start.7 = (bf16[384,384]{1,0:T(8,128)(2,1)S(1)}, bf16[384,384]{1,0:T(8,128)(2,1)S(1)}, u32[]{:S(2)}, u32[]{:S(2)}) collective-permute-start(bf16[384,384]{1,0:T(8,128)(2,1)S(1)} %copy-done.7), channel_id=1, source_target_pairs={{0,4},{1,5},{2,6},{3,7},{4,8},{5,9},{6,10},{7,11},{8,12},{9,13},{1... | collective-permute-start | bytes 884744 | tf_op jit(solution)/shard_map/ppermute | solution.py:344
  106.7 5.0 %collective-permute-start.6 = (bf16[384,384]{1,0:T(8,128)(2,1)S(1)}, bf16[384,384]{1,0:T(8,128)(2,1)S(1)}, u32[]{:S(2)}, u32[]{:S(2)}) collective-permute-start(bf16[384,384]{1,0:T(8,128)(2,1)S(1)} %collective-permute-done.5.from_after_3), channel_id=1, source_target_pairs={{252,124},{253,125},{254,126},{255,127},{508,381},{509,382},{510,3... | collective-permute-start | bytes 884744 | tf_op jit(solution)/shard_map/ppermute | solution.py:344

commit v5 on v4

--- a/solution.py
+++ b/solution.py
@@ -73,23 +73,35 @@
         copy.wait()
 
 
-def unpack_kernel(shift, kv, qg, vo, ao, vqg, vkg, vvg, aqg, akg, avg):
+def unpack_rows(packed, columns, outs):
+    row = 0
+    for out in outs:
+        rows = out.shape[0]
+        out[:, columns] = packed[row : row + rows]
+        row += rows
+
+
+def columns_of(member):
+    first = lax.rem(member, MEMBERS) * GROUP_WIDTH
+    return pl.ds(pl.multiple_of(first, GROUP_WIDTH), GROUP_WIDTH)
+
+
+def unpack_qg_kernel(shift, packed, *outs):
     for member in range(MEMBERS):
-        first = lax.rem(shift[0] + member, MEMBERS) * GROUP_WIDTH
-        columns = pl.ds(pl.multiple_of(first, GROUP_WIDTH), GROUP_WIDTH)
-        vo[:, columns] = qg[member, 0:128]
-        ao[:, columns] = qg[member, 128:192]
-        vqg[:, columns] = qg[member, 192:320]
-        aqg[:, columns] = qg[member, 320:384]
-        vkg[:, columns] = kv[member, 0:128]
-        vvg[:, columns] = kv[member, 128:256]
-        akg[:, columns] = kv[member, 256:320]
-        avg[:, columns] = kv[member, 320:384]
+        unpack_rows(packed.at[member], columns_of(shift[0] + member), outs)
+
+
+def unpack_kv_kernel(shift, me, *refs):
+    blocks, outs = refs[:MEMBERS], refs[MEMBERS:]
+    for distance, block in enumerate(blocks):
+        unpack_rows(block, columns_of(shift[0] + me[0] + MEMBERS - distance), outs)
 
 
 def merge_kernel(
-    last_group, group_ref, own, from_after_2, from_after_3, relayed_3, from_before, out
+    last_group, group_ref, me, own, from_after_2, from_after_3, relayed_3, from_before, *refs
 ):
+    outs, out = refs[:MEMBERS], refs[MEMBERS]
+
     def total(member, *received):
         parts = [own[member].astype(jnp.float32)]
         parts += [r[...].astype(jnp.float32) for r in received]
@@ -103,6 +115,9 @@
     @pl.when(group_ref[0] != last_group)
     def _():
         total(3, from_after_3, relayed_3)
+
+    for distance, target in enumerate(outs):
+        target[...] = out[lax.rem(me[0] + distance, MEMBERS)]
 
 
 def stacked(parts):
@@ -273,29 +288,28 @@
     )(shift, *arrays)
 
 
-def unpack(shift, kv, qg):
-    video = jax.ShapeDtypeStruct((VIDEO, HEADS * HEAD_SIZE), jnp.bfloat16)
-    audio = jax.ShapeDtypeStruct((AUDIO, HEADS * HEAD_SIZE), jnp.bfloat16)
-    shapes = (video, audio, video, video, video, audio, audio, audio)
+def unpack(kernel, rows, *arrays):
+    scalars = sum(array.dtype == jnp.int32 for array in arrays)
     return pl.pallas_call(
-        unpack_kernel,
-        out_shape=shapes,
-        in_specs=[whole(pltpu.SMEM)] + [whole()] * 2,
-        out_specs=[whole()] * 8,
+        kernel,
+        out_shape=[jax.ShapeDtypeStruct((r, HEADS * HEAD_SIZE), jnp.bfloat16) for r in rows],
+        in_specs=[whole(pltpu.SMEM)] * scalars + [whole()] * (len(arrays) - scalars),
+        out_specs=[whole()] * len(rows),
         compiler_params=SMALL,
         name="unpack",
-    )(shift, kv, qg)
-
-
-def merge(groups, group, *arrays):
+    )(*arrays)
+
+
+def merge(groups, *arrays):
     return pl.pallas_call(
         functools.partial(merge_kernel, groups - 1),
-        out_shape=PACKED_KV,
-        in_specs=[whole(pltpu.SMEM)] + [whole()] * 5,
-        out_specs=whole(),
+        out_shape=[BLOCK_KV] * MEMBERS,
+        in_specs=[whole(pltpu.SMEM)] * 2 + [whole()] * 5,
+        out_specs=[whole()] * MEMBERS,
+        scratch_shapes=[pltpu.VMEM((MEMBERS, ROWS, GROUP_WIDTH), jnp.bfloat16)],
         compiler_params=SMALL,
         name="merge",
-    )(group, *arrays)
+    )(*arrays)
 
 
 def attention(groups, group, *arrays):
@@ -371,6 +385,13 @@
     return lax.all_to_all(packed, "member", 0, 0)
 
 
+def send_round(blocks):
+    return [blocks[0]] + [
+        lax.ppermute(blocks[d], "member", [(i, (i + d) % MEMBERS) for i in range(MEMBERS)])
+        for d in range(1, MEMBERS)
+    ]
+
+
 def body(
     video_query,
     video_keys,
@@ -386,6 +407,7 @@
     groups = lax.axis_size(("tower", "group"))
     group = lax.axis_index(("tower", "group")).astype(jnp.int32).reshape(1)
     shift = slice_shift()
+    me = lax.axis_index("member").astype(jnp.int32).reshape(1)
     kv_packed = pack_kv(shift, video_keys, video_value, audio_key, audio_value)
     kv = exchange(kv_packed)
     qg_packed = pack_qg(
@@ -408,11 +430,34 @@
     from_after_3, relayed_back = to_group_by_relay(part_3, -1)
     from_after_2 = to_group(part_2, -1)
     from_before = to_group(after_part, 1)
-    merged = merge(
-        groups, group, kv_part, from_after_2, from_after_3, relayed_back, from_before
-    )
-    kv_back = exchange(merged)
-    return unpack(shift, kv_back, qg_back)
+    kvs_back = send_round(
+        merge(
+            groups,
+            group,
+            me,
+            kv_part,
+            from_after_2,
+            from_after_3,
+            relayed_back,
+            from_before,
+        )
+    )
+    video_output, audio_output, video_query_grad, audio_query_grad = unpack(
+        unpack_qg_kernel, (VIDEO, AUDIO, VIDEO, AUDIO), shift, qg_back
+    )
+    video_key_grad, video_value_grad, audio_key_grad, audio_value_grad = unpack(
+        unpack_kv_kernel, (VIDEO, VIDEO, AUDIO, AUDIO), shift, me, *kvs_back
+    )
+    return (
+        video_output,
+        audio_output,
+        video_query_grad,
+        video_key_grad,
+        video_value_grad,
+        audio_query_grad,
+        audio_key_grad,
+        audio_value_grad,
+    )
 
 
 def solution(mesh):

time: 158 us -> 152 us (0.962)
  the two profiles are of different devices: /device:TPU:120 before, /device:TPU:1 now
where the time goes in v5:
time: 152 us; the launch traced here: 151 us
  waiting for transfers between devices  70.2 us (46%)
  starting transfers between devices  62.5 us (41%)
  Pallas kernels  17.1 us (11%)
    all_to_all x3, starting transfers between devices, exchange(): return lax.all_to_all(packed, 'member', 0, 0)  26.3 us
    ppermute x3, waiting for transfers between devices, send_round(): lax.ppermute(blocks[d], 'member', [(i, (i + d) % MEMBERS) for i in range(...  26 us
    ppermute x8, waiting for transfers between devices, moved(): return lax.ppermute(block, ('clip', 'tower', 'group', 'member'), route)  25.1 us
    ppermute x8, starting transfers between devices, moved(): return lax.ppermute(block, ('clip', 'tower', 'group', 'member'), route)  21.8 us
    all_to_all x3, waiting for transfers between devices, exchange(): return lax.all_to_all(packed, 'member', 0, 0)  19.1 us
    ppermute x3, starting transfers between devices, send_round(): lax.ppermute(blocks[d], 'member', [(i, (i + d) % MEMBERS) for i in range(...  14.4 us
    pallas_call x1, Pallas kernels, attention(): pl.pallas_call(functools.partial(attention_kernel, groups - 1), grid=(GRO...  8.79 us
    pallas_call x1, Pallas kernels, pack_qg(): pl.pallas_call(pack_qg_kernel, out_shape=PACKED_QG, in_specs=[whole(pltpu...  3.17 us
  transfers between devices with their start and end apart: 14, of which 8 were waited for; matrix products, arithmetic and copies ran while one was open for 0% of the time, Pallas kernels for 3%

profile of v5, /device:TPU:1, one launch (start us, length us, event | category | flops | bytes accessed | tf_op | source)
XLA Modules:
  0.0 151.5 jit_solution(4801323667028468437)
XLA Ops:
  0.6 2.5 %pack_kv.1 = bf16[4,384,384]{2,1,0:T(8,128)(2,1)} custom-call(s32[1]{0:T(128)} %bitcast.shift, bf16[128,1536]{1,0:T(8,128)(2,1)} %vk.1, bf16[128,1536]{1,0:T(8,128)(2,1)} %vv.1, bf16[64,1536]{1,0:T(8,128)(2,1)} %ak.1, bf16[64,1536]{1,0:T(8,128)(2,1)} %av.1), custom_call_target="tpu_custom_call" | custom-call | tf_op jit(solution)/shard_map/pack_kv/pallas_call | solution.py:268
  3.2 10.9 %all-to-all-start = ((bf16[4,384,384]{2,1,0:T(8,128)(2,1)}), bf16[4,384,384]{2,1,0:T(8,128)(2,1)S(1)}, u32[]{:S(2)}, u32[]{:S(2)}) async-start(bf16[4,384,384]{2,1,0:T(8,128)(2,1)} %pack_kv.1), calls=%async_computation | async-start | bytes 2359296 | tf_op jit(solution)/shard_map/all_to_all | solution.py:385
  14.0 3.2 %pack_qg.1 = bf16[4,400,384]{2,1,0:T(8,128)(2,1)} custom-call(s32[1]{0:T(128)} %bitcast.shift, s32[1,2]{1,0:T(1,128)} %video_list.1, s32[1,2]{1,0:T(1,128)} %audio_list.1, bf16[128,1536]{1,0:T(8,128)(2,1)} %vq.1, bf16[64,1536]{1,0:T(8,128)(2,1)} %aq.1, bf16[128,1536]{1,0:T(8,128)(2,1)} %vg.1, bf16[64,1536]{1,0:T(8,128)(2,1)} %ag.1), custom_call_target="tpu_custom_call" | custom-call | tf_op jit(solution)/shard_map/pack_qg/pallas_call | solution.py:280
  17.2 17.4 %all-to-all-done.kv = bf16[4,384,384]{2,1,0:T(8,128)(2,1)S(1)} async-done(((bf16[4,384,384]{2,1,0:T(8,128)(2,1)}), bf16[4,384,384]{2,1,0:T(8,128)(2,1)S(1)}, u32[]{:S(2)}, u32[]{:S(2)}) %all-to-all-start) | async-done | bytes 1179680 | tf_op jit(solution)/shard_map/all_to_all | solution.py:385
  34.6 10.3 %all-to-all-start.1 = ((bf16[4,400,384]{2,1,0:T(8,128)(2,1)}), bf16[4,400,384]{2,1,0:T(8,128)(2,1)S(1)}, u32[]{:S(2)}, u32[]{:S(2)}) async-start(bf16[4,400,384]{2,1,0:T(8,128)(2,1)} %pack_qg.1), calls=%async_computation.1 | async-start | bytes 2457600 | tf_op jit(solution)/shard_map/all_to_all | solution.py:385
  44.9 0.1 slice_bitcast_fusion
  45.0 3.2 %collective-permute-start.1 = (bf16[384,384]{1,0:T(8,128)(2,1)S(1)}, bf16[384,384]{1,0:T(8,128)(2,1)S(1)}, u32[]{:S(2)}, u32[]{:S(2)}) collective-permute-start(bf16[384,384]{1,0:T(8,128)(2,1)S(1)} %get-tuple-element.43), channel_id=1, source_target_pairs={{0,4},{1,5},{2,6},{3,7},{4,8},{5,9},{6,10},{7,11},{8,12},{9,13},{1... | collective-permute-start | bytes 884744 | tf_op jit(solution)/shard_map/ppermute | solution.py:358
  48.2 1.3 collective-permute-start.3
  49.5 4.0 %collective-permute-start = (bf16[384,384]{1,0:T(8,128)(2,1)S(1)}, bf16[384,384]{1,0:T(8,128)(2,1)S(1)}, u32[]{:S(2)}, u32[]{:S(2)}) collective-permute-start(bf16[384,384]{1,0:T(8,128)(2,1)S(1)} %get-tuple-element.44), channel_id=1, source_target_pairs={{0,4},{1,5},{2,6},{3,7},{4,8},{5,9},{6,10},{7,11},{8,12},{9,13},{1... | collective-permute-start | bytes 884744 | tf_op jit(solution)/shard_map/ppermute | solution.py:358
  53.5 2.9 %collective-permute-done.1.before_3 = bf16[384,384]{1,0:T(8,128)(2,1)S(1)} collective-permute-done((bf16[384,384]{1,0:T(8,128)(2,1)S(1)}, bf16[384,384]{1,0:T(8,128)(2,1)S(1)}, u32[]{:S(2)}, u32[]{:S(2)}) %collective-permute-start.1) | collective-permute-done | bytes 294944 | tf_op jit(solution)/shard_map/ppermute | solution.py:358
  56.4 5.5 %collective-permute-start.2 = (bf16[384,384]{1,0:T(8,128)(2,1)S(1)}, bf16[384,384]{1,0:T(8,128)(2,1)S(1)}, u32[]{:S(2)}, u32[]{:S(2)}) collective-permute-start(bf16[384,384]{1,0:T(8,128)(2,1)S(1)} %collective-permute-done.1.before_3), channel_id=1, source_target_pairs={{0,128},{1,129},{2,130},{3,131},{256,387},{257,384},{258,385},{259... | collective-permute-start | bytes 884744 | tf_op jit(solution)/shard_map/ppermute | solution.py:358
  61.9 1.7 %all-to-all-done.1.qg = bf16[4,400,384]{2,1,0:T(8,128)(2,1)S(1)} async-done(((bf16[4,400,384]{2,1,0:T(8,128)(2,1)}), bf16[4,400,384]{2,1,0:T(8,128)(2,1)S(1)}, u32[]{:S(2)}, u32[]{:S(2)}) %all-to-all-start.1) | async-done | bytes 1228832 | tf_op jit(solution)/shard_map/all_to_all | solution.py:385
  63.6 0.0 collective-permute-done.before_2
  63.6 0.0 copy-start.5
  63.6 13.6 %collective-permute-done.2.relayed_3 = bf16[384,384]{1,0:T(8,128)(2,1)S(1)} collective-permute-done((bf16[384,384]{1,0:T(8,128)(2,1)S(1)}, bf16[384,384]{1,0:T(8,128)(2,1)S(1)}, u32[]{:S(2)}, u32[]{:S(2)}) %collective-permute-start.2) | collective-permute-done | bytes 294944 | tf_op jit(solution)/shard_map/ppermute | solution.py:358
  77.2 0.7 copy-done.6
  77.9 8.8 %attention.1 = (bf16[4,384,384]{2,1,0:T(8,128)(2,1)}, bf16[4,384,384]{2,1,0:T(8,128)(2,1)}, bf16[384,384]{1,0:T(8,128)(2,1)}, bf16[384,384]{1,0:T(8,128)(2,1)}, bf16[384,384]{1,0:T(8,128)(2,1)}) custom-call(s32[1]{0:T(128)} %bitcast.1.group_ref, bf16[4,384,384]{2,1,0:T(8,128)(2,1)} %copy-done.1, bf16[4,400,384]{2,1,0:T(8,128)(2,1)} %copy-done.2, ...), custom_call_target="tpu_custom_call" | custom-call | tf_op jit(solution)/shard_map/attention/pallas_call | solution.py:320
  86.7 5.1 %all-to-all-start.2 = ((bf16[4,384,384]{2,1,0:T(8,128)(2,1)}), bf16[4,384,384]{2,1,0:T(8,128)(2,1)S(1)}, u32[]{:S(2)}, u32[]{:S(2)}) async-start(bf16[4,384,384]{2,1,0:T(8,128)(2,1)} %get-tuple-element.25), calls=%async_computation.2 | async-start | bytes 2359296 | tf_op jit(solution)/shard_map/all_to_all | solution.py:385
  91.9 1.3 collective-permute-start.5
  93.1 1.3 collective-permute-start.4
  94.4 4.6 %collective-permute-start.7 = (bf16[384,384]{1,0:T(8,128)(2,1)}, bf16[384,384]{1,0:T(8,128)(2,1)S(1)}, u32[]{:S(2)}, u32[]{:S(2)}) collective-permute-start(bf16[384,384]{1,0:T(8,128)(2,1)} %get-tuple-element.32), channel_id=1, source_target_pairs={{0,4},{1,5},{2,6},{3,7},{4,8},{5,9},{6,10},{7,11},{8,12},{9,13},{1... | collective-permute-start | bytes 884744 | tf_op jit(solution)/shard_map/ppermute | solution.py:358
  99.1 3.0 %collective-permute-done.5.from_after_3 = bf16[384,384]{1,0:T(8,128)(2,1)S(1)} collective-permute-done((bf16[384,384]{1,0:T(8,128)(2,1)S(1)}, bf16[384,384]{1,0:T(8,128)(2,1)S(1)}, u32[]{:S(2)}, u32[]{:S(2)}) %collective-permute-start.5) | collective-permute-done | bytes 294944 | tf_op jit(solution)/shard_map/ppermute | solution.py:358
  102.1 0.7 collective-permute-start.6
  102.8 5.6 %collective-permute-done.4.from_after_2 = bf16[384,384]{1,0:T(8,128)(2,1)S(1)} collective-permute-done((bf16[384,384]{1,0:T(8,128)(2,1)}, bf16[384,384]{1,0:T(8,128)(2,1)S(1)}, u32[]{:S(2)}, u32[]{:S(2)}) %collective-permute-start.4) | collective-permute-done | bytes 294944 | tf_op jit(solution)/shard_map/ppermute | solution.py:358
  108.4 0.4 merge.1
  108.9 4.0 %collective-permute-start.8 = (bf16[384,384]{1,0:T(8,128)(2,1)S(1)}, bf16[384,384]{1,0:T(8,128)(2,1)S(1)}, u32[]{:S(2)}, u32[]{:S(2)}) collective-permute-start(bf16[384,384]{1,0:T(8,128)(2,1)S(1)} %get-tuple-element.34), channel_id=1, source_target_pairs={{0,1},{1,2},{2,3},{3,0},{4,5},{5,6},{6,7},{7,4},{8,9},{9,10},{10,1... | collective-permute-start | bytes 884744 | tf_op jit(solution)/shard_map/ppermute | solution.py:390
  112.8 5.2 %collective-permute-start.9 = (bf16[384,384]{1,0:T(8,128)(2,1)S(1)}, bf16[384,384]{1,0:T(8,128)(2,1)S(1)}, u32[]{:S(2)}, u32[]{:S(2)}) collective-permute-start(bf16[384,384]{1,0:T(8,128)(2,1)S(1)} %get-tuple-element.35), channel_id=1, source_target_pairs={{0,2},{1,3},{2,0},{3,1},{4,6},{5,7},{6,4},{7,5},{8,10},{9,11},{10,... | collective-permute-start | bytes 884744 | tf_op jit(solution)/shard_map/ppermute | solution.py:390
  118.0 5.2 %collective-permute-start.10 = (bf16[384,384]{1,0:T(8,128)(2,1)S(1)}, bf16[384,384]{1,0:T(8,128)(2,1)S(1)}, u32[]{:S(2)}, u32[]{:S(2)}) collective-permute-start(bf16[384,384]{1,0:T(8,128)(2,1)S(1)} %get-tuple-element.36), channel_id=1, source_target_pairs={{0,3},{1,0},{2,1},{3,2},{4,7},{5,4},{6,5},{7,6},{8,11},{9,8},{10,9... | collective-permute-start | bytes 884744 | tf_op jit(solution)/shard_map/ppermute | solution.py:390
  123.2 4.6 %collective-permute-done.8.refs_1_ = bf16[384,384]{1,0:T(8,128)(2,1)S(1)} collective-permute-done((bf16[384,384]{1,0:T(8,128)(2,1)S(1)}, bf16[384,384]{1,0:T(8,128)(2,1)S(1)}, u32[]{:S(2)}, u32[]{:S(2)}) %collective-permute-start.8) | collective-permute-done | bytes 294944 | tf_op jit(solution)/shard_map/ppermute | solution.py:390
  127.9 21.4 %collective-permute-done.9.refs_2_ = bf16[384,384]{1,0:T(8,128)(2,1)S(1)} collective-permute-done((bf16[384,384]{1,0:T(8,128)(2,1)S(1)}, bf16[384,384]{1,0:T(8,128)(2,1)S(1)}, u32[]{:S(2)}, u32[]{:S(2)}) %collective-permute-start.9) | collective-permute-done | bytes 294944 | tf_op jit(solution)/shard_map/ppermute | solution.py:390
  149.2 1.1 unpack.3
  150.4 1.1 unpack.2
  (19 shorter events, 0.0 us)
Async XLA Ops:
  3.2 31.5 %all-to-all-start = ((bf16[4,384,384]{2,1,0:T(8,128)(2,1)}), bf16[4,384,384]{2,1,0:T(8,128)(2,1)S(1)}, u32[]{:S(2)}, u32[]{:S(2)}) async-start(bf16[4,384,384]{2,1,0:T(8,128)(2,1)} %pack_kv.1), calls=%async_computation | async-start | bytes 2359296 | tf_op jit(solution)/shard_map/all_to_all | solution.py:385
  34.6 10.3 %copy-start.1 = (bf16[4,384,384]{2,1,0:T(8,128)(2,1)}, bf16[4,384,384]{2,1,0:T(8,128)(2,1)S(1)}, u32[]{:S(2)}) copy-start(bf16[4,384,384]{2,1,0:T(8,128)(2,1)S(1)} %all-to-all-done.kv) | copy-start | bytes 3538948
  34.6 28.9 %all-to-all-start.1 = ((bf16[4,400,384]{2,1,0:T(8,128)(2,1)}), bf16[4,400,384]{2,1,0:T(8,128)(2,1)S(1)}, u32[]{:S(2)}, u32[]{:S(2)}) async-start(bf16[4,400,384]{2,1,0:T(8,128)(2,1)} %pack_qg.1), calls=%async_computation.1 | async-start | bytes 2457600 | tf_op jit(solution)/shard_map/all_to_all | solution.py:385
  45.0 11.4 %collective-permute-start.1 = (bf16[384,384]{1,0:T(8,128)(2,1)S(1)}, bf16[384,384]{1,0:T(8,128)(2,1)S(1)}, u32[]{:S(2)}, u32[]{:S(2)}) collective-permute-start(bf16[384,384]{1,0:T(8,128)(2,1)S(1)} %get-tuple-element.43), channel_id=1, source_target_pairs={{0,4},{1,5},{2,6},{3,7},{4,8},{5,9},{6,10},{7,11},{8,12},{9,13},{1... | collective-permute-start | bytes 884744 | tf_op jit(solution)/shard_map/ppermute | solution.py:358
  48.2 15.4 %collective-permute-start.3 = (bf16[384,384]{1,0:T(8,128)(2,1)S(1)}, bf16[384,384]{1,0:T(8,128)(2,1)S(1)}, u32[]{:S(2)}, u32[]{:S(2)}) collective-permute-start(bf16[384,384]{1,0:T(8,128)(2,1)S(1)} %get-tuple-element.42), channel_id=1, source_target_pairs={{4,0},{5,1},{6,2},{7,3},{8,4},{9,5},{10,6},{11,7},{12,8},{13,9},{1... | collective-permute-start | bytes 884744 | tf_op jit(solution)/shard_map/ppermute | solution.py:358
  49.5 14.1 %collective-permute-start = (bf16[384,384]{1,0:T(8,128)(2,1)S(1)}, bf16[384,384]{1,0:T(8,128)(2,1)S(1)}, u32[]{:S(2)}, u32[]{:S(2)}) collective-permute-start(bf16[384,384]{1,0:T(8,128)(2,1)S(1)} %get-tuple-element.44), channel_id=1, source_target_pairs={{0,4},{1,5},{2,6},{3,7},{4,8},{5,9},{6,10},{7,11},{8,12},{9,13},{1... | collective-permute-start | bytes 884744 | tf_op jit(solution)/shard_map/ppermute | solution.py:358
  56.4 20.8 %copy-start.3 = (bf16[384,384]{1,0:T(8,128)(2,1)}, bf16[384,384]{1,0:T(8,128)(2,1)S(1)}, u32[]{:S(2)}) copy-start(bf16[384,384]{1,0:T(8,128)(2,1)S(1)} %collective-permute-done.1.before_3) | copy-start | bytes 884740
  56.4 20.8 %collective-permute-start.2 = (bf16[384,384]{1,0:T(8,128)(2,1)S(1)}, bf16[384,384]{1,0:T(8,128)(2,1)S(1)}, u32[]{:S(2)}, u32[]{:S(2)}) collective-permute-start(bf16[384,384]{1,0:T(8,128)(2,1)S(1)} %collective-permute-done.1.before_3), channel_id=1, source_target_pairs={{0,128},{1,129},{2,130},{3,131},{256,387},{257,384},{258,385},{259... | collective-permute-start | bytes 884744 | tf_op jit(solution)/shard_map/ppermute | solution.py:358
  63.5 13.6 %copy-start.2 = (bf16[4,400,384]{2,1,0:T(8,128)(2,1)}, bf16[4,400,384]{2,1,0:T(8,128)(2,1)S(1)}, u32[]{:S(2)}) copy-start(bf16[4,400,384]{2,1,0:T(8,128)(2,1)S(1)} %all-to-all-done.1.qg) | copy-start | bytes 3686404
  63.6 13.6 %copy-start.4 = (bf16[384,384]{1,0:T(8,128)(2,1)}, bf16[384,384]{1,0:T(8,128)(2,1)S(1)}, u32[]{:S(2)}) copy-start(bf16[384,384]{1,0:T(8,128)(2,1)S(1)} %collective-permute-done.3.after) | copy-start | bytes 884740
  63.6 13.6 %copy-start.5 = (bf16[384,384]{1,0:T(8,128)(2,1)}, bf16[384,384]{1,0:T(8,128)(2,1)S(1)}, u32[]{:S(2)}) copy-start(bf16[384,384]{1,0:T(8,128)(2,1)S(1)} %collective-permute-done.before_2) | copy-start | bytes 884740
  77.2 0.7 copy-start.6
  86.7 5.2 %copy-start.7 = (bf16[384,384]{1,0:T(8,128)(2,1)S(1)}, bf16[384,384]{1,0:T(8,128)(2,1)}, u32[]{:S(2)}) copy-start(bf16[384,384]{1,0:T(8,128)(2,1)} %get-tuple-element.31) | copy-start | bytes 884740
  86.7 21.7 %copy-start = (bf16[4,384,384]{2,1,0:T(8,128)(2,1)S(1)}, bf16[4,384,384]{2,1,0:T(8,128)(2,1)}, u32[]{:S(2)}) copy-start(bf16[4,384,384]{2,1,0:T(8,128)(2,1)} %get-tuple-element.29.own) | copy-start | bytes 3538948
  86.7 63.7 %all-to-all-start.2 = ((bf16[4,384,384]{2,1,0:T(8,128)(2,1)}), bf16[4,384,384]{2,1,0:T(8,128)(2,1)S(1)}, u32[]{:S(2)}, u32[]{:S(2)}) async-start(bf16[4,384,384]{2,1,0:T(8,128)(2,1)} %get-tuple-element.25), calls=%async_computation.2 | async-start | bytes 2359296 | tf_op jit(solution)/shard_map/all_to_all | solution.py:385
  91.9 10.2 %collective-permute-start.5 = (bf16[384,384]{1,0:T(8,128)(2,1)S(1)}, bf16[384,384]{1,0:T(8,128)(2,1)S(1)}, u32[]{:S(2)}, u32[]{:S(2)}) collective-permute-start(bf16[384,384]{1,0:T(8,128)(2,1)S(1)} %copy-done.7), channel_id=1, source_target_pairs={{4,0},{5,1},{6,2},{7,3},{8,4},{9,5},{10,6},{11,7},{12,8},{13,9},{1... | collective-permute-start | bytes 884744 | tf_op jit(solution)/shard_map/ppermute | solution.py:358
  93.1 15.3 %collective-permute-start.4 = (bf16[384,384]{1,0:T(8,128)(2,1)}, bf16[384,384]{1,0:T(8,128)(2,1)S(1)}, u32[]{:S(2)}, u32[]{:S(2)}) collective-permute-start(bf16[384,384]{1,0:T(8,128)(2,1)} %get-tuple-element.30), channel_id=1, source_target_pairs={{4,0},{5,1},{6,2},{7,3},{8,4},{9,5},{10,6},{11,7},{12,8},{13,9},{1... | collective-permute-start | bytes 884744 | tf_op jit(solution)/shard_map/ppermute | solution.py:358
  94.4 14.0 %collective-permute-start.7 = (bf16[384,384]{1,0:T(8,128)(2,1)}, bf16[384,384]{1,0:T(8,128)(2,1)S(1)}, u32[]{:S(2)}, u32[]{:S(2)}) collective-permute-start(bf16[384,384]{1,0:T(8,128)(2,1)} %get-tuple-element.32), channel_id=1, source_target_pairs={{0,4},{1,5},{2,6},{3,7},{4,8},{5,9},{6,10},{7,11},{8,12},{9,13},{1... | collective-permute-start | bytes 884744 | tf_op jit(solution)/shard_map/ppermute | solution.py:358
  102.1 6.3 %collective-permute-start.6 = (bf16[384,384]{1,0:T(8,128)(2,1)S(1)}, bf16[384,384]{1,0:T(8,128)(2,1)S(1)}, u32[]{:S(2)}, u32[]{:S(2)}) collective-permute-start(bf16[384,384]{1,0:T(8,128)(2,1)S(1)} %collective-permute-done.5.from_after_3), channel_id=1, source_target_pairs={{252,124},{253,125},{254,126},{255,127},{508,381},{509,382},{510,3... | collective-permute-start | bytes 884744 | tf_op jit(solution)/shard_map/ppermute | solution.py:358
  108.9 19.0 %collective-permute-start.8 = (bf16[384,384]{1,0:T(8,128)(2,1)S(1)}, bf16[384,384]{1,0:T(8,128)(2,1)S(1)}, u32[]{:S(2)}, u32[]{:S(2)}) collective-permute-start(bf16[384,384]{1,0:T(8,128)(2,1)S(1)} %get-tuple-element.34), channel_id=1, source_target_pairs={{0,1},{1,2},{2,3},{3,0},{4,5},{5,6},{6,7},{7,4},{8,9},{9,10},{10,1... | collective-permute-start | bytes 884744 | tf_op jit(solution)/shard_map/ppermute | solution.py:390
  112.8 36.4 %collective-permute-start.9 = (bf16[384,384]{1,0:T(8,128)(2,1)S(1)}, bf16[384,384]{1,0:T(8,128)(2,1)S(1)}, u32[]{:S(2)}, u32[]{:S(2)}) collective-permute-start(bf16[384,384]{1,0:T(8,128)(2,1)S(1)} %get-tuple-element.35), channel_id=1, source_target_pairs={{0,2},{1,3},{2,0},{3,1},{4,6},{5,7},{6,4},{7,5},{8,10},{9,11},{10,... | collective-permute-start | bytes 884744 | tf_op jit(solution)/shard_map/ppermute | solution.py:390
  118.0 31.2 %collective-permute-start.10 = (bf16[384,384]{1,0:T(8,128)(2,1)S(1)}, bf16[384,384]{1,0:T(8,128)(2,1)S(1)}, u32[]{:S(2)}, u32[]{:S(2)}) collective-permute-start(bf16[384,384]{1,0:T(8,128)(2,1)S(1)} %get-tuple-element.36), channel_id=1, source_target_pairs={{0,3},{1,0},{2,1},{3,2},{4,7},{5,4},{6,5},{7,6},{8,11},{9,8},{10,9... | collective-permute-start | bytes 884744 | tf_op jit(solution)/shard_map/ppermute | solution.py:390

commit v6 on v5

--- a/solution.py
+++ b/solution.py
@@ -13,6 +13,7 @@
 WINDOW_BLOCKS = 4
 HALF_WINDOW = 2
 MEMBERS = 4
+DISTANCES = (0, 2, 1, 3)
 GROUP_HEADS = HEADS // MEMBERS
 GROUP_WIDTH = GROUP_HEADS * HEAD_SIZE
 EXTENDED = MEMBERS + WINDOW_BLOCKS - 1
@@ -93,7 +94,7 @@
 
 def unpack_kv_kernel(shift, me, *refs):
     blocks, outs = refs[:MEMBERS], refs[MEMBERS:]
-    for distance, block in enumerate(blocks):
+    for distance, block in zip(DISTANCES, blocks):
         unpack_rows(block, columns_of(shift[0] + me[0] + MEMBERS - distance), outs)
 
 
@@ -386,10 +387,11 @@
 
 
 def send_round(blocks):
-    return [blocks[0]] + [
-        lax.ppermute(blocks[d], "member", [(i, (i + d) % MEMBERS) for i in range(MEMBERS)])
-        for d in range(1, MEMBERS)
-    ]
+    received = {0: blocks[0]}
+    for d in range(1, MEMBERS):
+        route = [(i, (i + d) % MEMBERS) for i in range(MEMBERS)]
+        received[d] = lax.ppermute(blocks[d], "member", route)
+    return [received[d] for d in DISTANCES]
 
 
 def body(

time: 152 us -> 151 us (level)
  the two profiles are of different devices: /device:TPU:1 before, /device:TPU:7 now
where the time goes in v6:
time: 151 us
  waiting for transfers between devices  68.4 us (45%)
  starting transfers between devices  63 us (42%)
  Pallas kernels  17.1 us (11%)
    ppermute x3, waiting for transfers between devices, send_round(): received[d] = lax.ppermute(blocks[d], 'member', route)  35.6 us
    all_to_all x3, starting transfers between devices, exchange(): return lax.all_to_all(packed, 'member', 0, 0)  26.8 us
    all_to_all x3, waiting for transfers between devices, exchange(): return lax.all_to_all(packed, 'member', 0, 0)  25.4 us
    ppermute x8, starting transfers between devices, moved(): return lax.ppermute(block, ('clip', 'tower', 'group', 'member'), route)  21.3 us
    ppermute x3, starting transfers between devices, send_round(): received[d] = lax.ppermute(blocks[d], 'member', route)  15 us
    pallas_call x1, Pallas kernels, attention(): pl.pallas_call(functools.partial(attention_kernel, groups - 1), grid=(GRO...  8.79 us
    ppermute x8, waiting for transfers between devices, moved(): return lax.ppermute(block, ('clip', 'tower', 'group', 'member'), route)  7.32 us
    pallas_call x1, Pallas kernels, pack_qg(): pl.pallas_call(pack_qg_kernel, out_shape=PACKED_QG, in_specs=[whole(pltpu...  3.17 us
  transfers between devices with their start and end apart: 14, of which 8 were waited for; matrix products, arithmetic and copies ran while one was open for 0% of the time, Pallas kernels for 3%

profile of v6, /device:TPU:7, one launch (start us, length us, event | category | flops | bytes accessed | tf_op | source)
XLA Modules:
  0.0 150.7 jit_solution(12077365889250158348)
XLA Ops:
  0.6 2.5 %pack_kv.1 = bf16[4,384,384]{2,1,0:T(8,128)(2,1)} custom-call(s32[1]{0:T(128)} %bitcast.shift, bf16[128,1536]{1,0:T(8,128)(2,1)} %vk.1, bf16[128,1536]{1,0:T(8,128)(2,1)} %vv.1, bf16[64,1536]{1,0:T(8,128)(2,1)} %ak.1, bf16[64,1536]{1,0:T(8,128)(2,1)} %av.1), custom_call_target="tpu_custom_call" | custom-call | tf_op jit(solution)/shard_map/pack_kv/pallas_call | solution.py:269
  3.2 10.0 %all-to-all-start = ((bf16[4,384,384]{2,1,0:T(8,128)(2,1)}), bf16[4,384,384]{2,1,0:T(8,128)(2,1)S(1)}, u32[]{:S(2)}, u32[]{:S(2)}) async-start(bf16[4,384,384]{2,1,0:T(8,128)(2,1)} %pack_kv.1), calls=%async_computation | async-start | bytes 2359296 | tf_op jit(solution)/shard_map/all_to_all | solution.py:386
  13.2 3.2 %pack_qg.1 = bf16[4,400,384]{2,1,0:T(8,128)(2,1)} custom-call(s32[1]{0:T(128)} %bitcast.shift, s32[1,2]{1,0:T(1,128)} %video_list.1, s32[1,2]{1,0:T(1,128)} %audio_list.1, bf16[128,1536]{1,0:T(8,128)(2,1)} %vq.1, bf16[64,1536]{1,0:T(8,128)(2,1)} %aq.1, bf16[128,1536]{1,0:T(8,128)(2,1)} %vg.1, bf16[64,1536]{1,0:T(8,128)(2,1)} %ag.1), custom_call_target="tpu_custom_call" | custom-call | tf_op jit(solution)/shard_map/pack_qg/pallas_call | solution.py:281
  16.4 17.4 %all-to-all-done.kv = bf16[4,384,384]{2,1,0:T(8,128)(2,1)S(1)} async-done(((bf16[4,384,384]{2,1,0:T(8,128)(2,1)}), bf16[4,384,384]{2,1,0:T(8,128)(2,1)S(1)}, u32[]{:S(2)}, u32[]{:S(2)}) %all-to-all-start) | async-done | bytes 1179680 | tf_op jit(solution)/shard_map/all_to_all | solution.py:386
  33.8 10.3 %all-to-all-start.1 = ((bf16[4,400,384]{2,1,0:T(8,128)(2,1)}), bf16[4,400,384]{2,1,0:T(8,128)(2,1)S(1)}, u32[]{:S(2)}, u32[]{:S(2)}) async-start(bf16[4,400,384]{2,1,0:T(8,128)(2,1)} %pack_qg.1), calls=%async_computation.1 | async-start | bytes 2457600 | tf_op jit(solution)/shard_map/all_to_all | solution.py:386
  44.1 0.1 slice_bitcast_fusion
  44.2 3.2 %collective-permute-start.1 = (bf16[384,384]{1,0:T(8,128)(2,1)S(1)}, bf16[384,384]{1,0:T(8,128)(2,1)S(1)}, u32[]{:S(2)}, u32[]{:S(2)}) collective-permute-start(bf16[384,384]{1,0:T(8,128)(2,1)S(1)} %get-tuple-element.43), channel_id=1, source_target_pairs={{0,4},{1,5},{2,6},{3,7},{4,8},{5,9},{6,10},{7,11},{8,12},{9,13},{1... | collective-permute-start | bytes 884744 | tf_op jit(solution)/shard_map/ppermute | solution.py:359
  47.4 4.2 %collective-permute-start.3 = (bf16[384,384]{1,0:T(8,128)(2,1)S(1)}, bf16[384,384]{1,0:T(8,128)(2,1)S(1)}, u32[]{:S(2)}, u32[]{:S(2)}) collective-permute-start(bf16[384,384]{1,0:T(8,128)(2,1)S(1)} %get-tuple-element.42), channel_id=1, source_target_pairs={{4,0},{5,1},{6,2},{7,3},{8,4},{9,5},{10,6},{11,7},{12,8},{13,9},{1... | collective-permute-start | bytes 884744 | tf_op jit(solution)/shard_map/ppermute | solution.py:359
  51.6 1.9 %collective-permute-start = (bf16[384,384]{1,0:T(8,128)(2,1)S(1)}, bf16[384,384]{1,0:T(8,128)(2,1)S(1)}, u32[]{:S(2)}, u32[]{:S(2)}) collective-permute-start(bf16[384,384]{1,0:T(8,128)(2,1)S(1)} %get-tuple-element.44), channel_id=1, source_target_pairs={{0,4},{1,5},{2,6},{3,7},{4,8},{5,9},{6,10},{7,11},{8,12},{9,13},{1... | collective-permute-start | bytes 884744 | tf_op jit(solution)/shard_map/ppermute | solution.py:359
  53.5 0.5 collective-permute-done.1.before_3
  54.0 0.7 collective-permute-start.2
  54.7 8.0 %all-to-all-done.1.qg = bf16[4,400,384]{2,1,0:T(8,128)(2,1)S(1)} async-done(((bf16[4,400,384]{2,1,0:T(8,128)(2,1)}), bf16[4,400,384]{2,1,0:T(8,128)(2,1)S(1)}, u32[]{:S(2)}, u32[]{:S(2)}) %all-to-all-start.1) | async-done | bytes 1228832 | tf_op jit(solution)/shard_map/all_to_all | solution.py:386
  62.8 1.0 copy-done.2
  63.8 0.1 copy-done.5
  63.9 0.1 copy-done.6
  64.0 8.8 %attention.1 = (bf16[4,384,384]{2,1,0:T(8,128)(2,1)}, bf16[4,384,384]{2,1,0:T(8,128)(2,1)}, bf16[384,384]{1,0:T(8,128)(2,1)}, bf16[384,384]{1,0:T(8,128)(2,1)}, bf16[384,384]{1,0:T(8,128)(2,1)}) custom-call(s32[1]{0:T(128)} %bitcast.1.group_ref, bf16[4,384,384]{2,1,0:T(8,128)(2,1)} %copy-done.1, bf16[4,400,384]{2,1,0:T(8,128)(2,1)} %copy-done.2, ...), custom_call_target="tpu_custom_call" | custom-call | tf_op jit(solution)/shard_map/attention/pallas_call | solution.py:321
  72.8 6.4 %all-to-all-start.2 = ((bf16[4,384,384]{2,1,0:T(8,128)(2,1)}), bf16[4,384,384]{2,1,0:T(8,128)(2,1)S(1)}, u32[]{:S(2)}, u32[]{:S(2)}) async-start(bf16[4,384,384]{2,1,0:T(8,128)(2,1)} %get-tuple-element.25), calls=%async_computation.2 | async-start | bytes 2359296 | tf_op jit(solution)/shard_map/all_to_all | solution.py:386
  79.3 5.4 %collective-permute-start.5 = (bf16[384,384]{1,0:T(8,128)(2,1)S(1)}, bf16[384,384]{1,0:T(8,128)(2,1)S(1)}, u32[]{:S(2)}, u32[]{:S(2)}) collective-permute-start(bf16[384,384]{1,0:T(8,128)(2,1)S(1)} %copy-done.7), channel_id=1, source_target_pairs={{4,0},{5,1},{6,2},{7,3},{8,4},{9,5},{10,6},{11,7},{12,8},{13,9},{1... | collective-permute-start | bytes 884744 | tf_op jit(solution)/shard_map/ppermute | solution.py:359
  84.6 3.0 %collective-permute-start.4 = (bf16[384,384]{1,0:T(8,128)(2,1)}, bf16[384,384]{1,0:T(8,128)(2,1)S(1)}, u32[]{:S(2)}, u32[]{:S(2)}) collective-permute-start(bf16[384,384]{1,0:T(8,128)(2,1)} %get-tuple-element.30), channel_id=1, source_target_pairs={{4,0},{5,1},{6,2},{7,3},{8,4},{9,5},{10,6},{11,7},{12,8},{13,9},{1... | collective-permute-start | bytes 884744 | tf_op jit(solution)/shard_map/ppermute | solution.py:359
  87.6 2.3 %collective-permute-start.7 = (bf16[384,384]{1,0:T(8,128)(2,1)}, bf16[384,384]{1,0:T(8,128)(2,1)S(1)}, u32[]{:S(2)}, u32[]{:S(2)}) collective-permute-start(bf16[384,384]{1,0:T(8,128)(2,1)} %get-tuple-element.32), channel_id=1, source_target_pairs={{0,4},{1,5},{2,6},{3,7},{4,8},{5,9},{6,10},{7,11},{8,12},{9,13},{1... | collective-permute-start | bytes 884744 | tf_op jit(solution)/shard_map/ppermute | solution.py:359
  89.9 0.7 collective-permute-start.6
  90.6 1.7 %collective-permute-done.4.from_after_2 = bf16[384,384]{1,0:T(8,128)(2,1)S(1)} collective-permute-done((bf16[384,384]{1,0:T(8,128)(2,1)}, bf16[384,384]{1,0:T(8,128)(2,1)S(1)}, u32[]{:S(2)}, u32[]{:S(2)}) %collective-permute-start.4) | collective-permute-done | bytes 294944 | tf_op jit(solution)/shard_map/ppermute | solution.py:359
  92.3 5.1 %collective-permute-done.7.from_before = bf16[384,384]{1,0:T(8,128)(2,1)S(1)} collective-permute-done((bf16[384,384]{1,0:T(8,128)(2,1)}, bf16[384,384]{1,0:T(8,128)(2,1)S(1)}, u32[]{:S(2)}, u32[]{:S(2)}) %collective-permute-start.7) | collective-permute-done | bytes 294944 | tf_op jit(solution)/shard_map/ppermute | solution.py:359
  97.4 0.4 merge.1
  97.9 7.6 %collective-permute-start.8 = (bf16[384,384]{1,0:T(8,128)(2,1)S(1)}, bf16[384,384]{1,0:T(8,128)(2,1)S(1)}, u32[]{:S(2)}, u32[]{:S(2)}) collective-permute-start(bf16[384,384]{1,0:T(8,128)(2,1)S(1)} %get-tuple-element.34), channel_id=1, source_target_pairs={{0,2},{1,3},{2,0},{3,1},{4,6},{5,7},{6,4},{7,5},{8,10},{9,11},{10,... | collective-permute-start | bytes 884744 | tf_op jit(solution)/shard_map/ppermute | solution.py:393
  105.4 2.2 %collective-permute-start.9 = (bf16[384,384]{1,0:T(8,128)(2,1)S(1)}, bf16[384,384]{1,0:T(8,128)(2,1)S(1)}, u32[]{:S(2)}, u32[]{:S(2)}) collective-permute-start(bf16[384,384]{1,0:T(8,128)(2,1)S(1)} %get-tuple-element.35), channel_id=1, source_target_pairs={{0,1},{1,2},{2,3},{3,0},{4,5},{5,6},{6,7},{7,4},{8,9},{9,10},{10,1... | collective-permute-start | bytes 884744 | tf_op jit(solution)/shard_map/ppermute | solution.py:393
  107.6 5.2 %collective-permute-start.10 = (bf16[384,384]{1,0:T(8,128)(2,1)S(1)}, bf16[384,384]{1,0:T(8,128)(2,1)S(1)}, u32[]{:S(2)}, u32[]{:S(2)}) collective-permute-start(bf16[384,384]{1,0:T(8,128)(2,1)S(1)} %get-tuple-element.36), channel_id=1, source_target_pairs={{0,3},{1,0},{2,1},{3,2},{4,7},{5,4},{6,5},{7,6},{8,11},{9,8},{10,9... | collective-permute-start | bytes 884744 | tf_op jit(solution)/shard_map/ppermute | solution.py:393
  112.8 18.2 %collective-permute-done.8.refs_1_ = bf16[384,384]{1,0:T(8,128)(2,1)S(1)} collective-permute-done((bf16[384,384]{1,0:T(8,128)(2,1)S(1)}, bf16[384,384]{1,0:T(8,128)(2,1)S(1)}, u32[]{:S(2)}, u32[]{:S(2)}) %collective-permute-start.8) | collective-permute-done | bytes 294944 | tf_op jit(solution)/shard_map/ppermute | solution.py:393
  131.1 4.5 %collective-permute-done.9.refs_2_ = bf16[384,384]{1,0:T(8,128)(2,1)S(1)} collective-permute-done((bf16[384,384]{1,0:T(8,128)(2,1)S(1)}, bf16[384,384]{1,0:T(8,128)(2,1)S(1)}, u32[]{:S(2)}, u32[]{:S(2)}) %collective-permute-start.9) | collective-permute-done | bytes 294944 | tf_op jit(solution)/shard_map/ppermute | solution.py:393
  135.6 12.9 %collective-permute-done.10.refs_3_ = bf16[384,384]{1,0:T(8,128)(2,1)S(1)} collective-permute-done((bf16[384,384]{1,0:T(8,128)(2,1)S(1)}, bf16[384,384]{1,0:T(8,128)(2,1)S(1)}, u32[]{:S(2)}, u32[]{:S(2)}) %collective-permute-start.10) | collective-permute-done | bytes 294944 | tf_op jit(solution)/shard_map/ppermute | solution.py:393
  148.5 1.1 unpack.3
  149.6 1.1 unpack.2
  (19 shorter events, 0.1 us)
Async XLA Ops:
  3.2 30.6 %all-to-all-start = ((bf16[4,384,384]{2,1,0:T(8,128)(2,1)}), bf16[4,384,384]{2,1,0:T(8,128)(2,1)S(1)}, u32[]{:S(2)}, u32[]{:S(2)}) async-start(bf16[4,384,384]{2,1,0:T(8,128)(2,1)} %pack_kv.1), calls=%async_computation | async-start | bytes 2359296 | tf_op jit(solution)/shard_map/all_to_all | solution.py:386
  33.8 10.3 %copy-start.1 = (bf16[4,384,384]{2,1,0:T(8,128)(2,1)}, bf16[4,384,384]{2,1,0:T(8,128)(2,1)S(1)}, u32[]{:S(2)}) copy-start(bf16[4,384,384]{2,1,0:T(8,128)(2,1)S(1)} %all-to-all-done.kv) | copy-start | bytes 3538948
  33.8 28.9 %all-to-all-start.1 = ((bf16[4,400,384]{2,1,0:T(8,128)(2,1)}), bf16[4,400,384]{2,1,0:T(8,128)(2,1)S(1)}, u32[]{:S(2)}, u32[]{:S(2)}) async-start(bf16[4,400,384]{2,1,0:T(8,128)(2,1)} %pack_qg.1), calls=%async_computation.1 | async-start | bytes 2457600 | tf_op jit(solution)/shard_map/all_to_all | solution.py:386
  44.2 9.9 %collective-permute-start.1 = (bf16[384,384]{1,0:T(8,128)(2,1)S(1)}, bf16[384,384]{1,0:T(8,128)(2,1)S(1)}, u32[]{:S(2)}, u32[]{:S(2)}) collective-permute-start(bf16[384,384]{1,0:T(8,128)(2,1)S(1)} %get-tuple-element.43), channel_id=1, source_target_pairs={{0,4},{1,5},{2,6},{3,7},{4,8},{5,9},{6,10},{7,11},{8,12},{9,13},{1... | collective-permute-start | bytes 884744 | tf_op jit(solution)/shard_map/ppermute | solution.py:359
  47.4 15.4 %collective-permute-start.3 = (bf16[384,384]{1,0:T(8,128)(2,1)S(1)}, bf16[384,384]{1,0:T(8,128)(2,1)S(1)}, u32[]{:S(2)}, u32[]{:S(2)}) collective-permute-start(bf16[384,384]{1,0:T(8,128)(2,1)S(1)} %get-tuple-element.42), channel_id=1, source_target_pairs={{4,0},{5,1},{6,2},{7,3},{8,4},{9,5},{10,6},{11,7},{12,8},{13,9},{1... | collective-permute-start | bytes 884744 | tf_op jit(solution)/shard_map/ppermute | solution.py:359
  51.6 11.2 %collective-permute-start = (bf16[384,384]{1,0:T(8,128)(2,1)S(1)}, bf16[384,384]{1,0:T(8,128)(2,1)S(1)}, u32[]{:S(2)}, u32[]{:S(2)}) collective-permute-start(bf16[384,384]{1,0:T(8,128)(2,1)S(1)} %get-tuple-element.44), channel_id=1, source_target_pairs={{0,4},{1,5},{2,6},{3,7},{4,8},{5,9},{6,10},{7,11},{8,12},{9,13},{1... | collective-permute-start | bytes 884744 | tf_op jit(solution)/shard_map/ppermute | solution.py:359
  54.0 8.7 %copy-start.3 = (bf16[384,384]{1,0:T(8,128)(2,1)}, bf16[384,384]{1,0:T(8,128)(2,1)S(1)}, u32[]{:S(2)}) copy-start(bf16[384,384]{1,0:T(8,128)(2,1)S(1)} %collective-permute-done.1.before_3) | copy-start | bytes 884740
  54.0 8.7 %collective-permute-start.2 = (bf16[384,384]{1,0:T(8,128)(2,1)S(1)}, bf16[384,384]{1,0:T(8,128)(2,1)S(1)}, u32[]{:S(2)}, u32[]{:S(2)}) collective-permute-start(bf16[384,384]{1,0:T(8,128)(2,1)S(1)} %collective-permute-done.1.before_3), channel_id=1, source_target_pairs={{0,128},{1,129},{2,130},{3,131},{256,387},{257,384},{258,385},{259... | collective-permute-start | bytes 884744 | tf_op jit(solution)/shard_map/ppermute | solution.py:359
  62.7 1.0 copy-start.2
  62.7 1.1 copy-start.4
  62.7 1.2 copy-start.5
  62.8 1.3 copy-start.6
  72.8 6.5 %copy-start.7 = (bf16[384,384]{1,0:T(8,128)(2,1)S(1)}, bf16[384,384]{1,0:T(8,128)(2,1)}, u32[]{:S(2)}) copy-start(bf16[384,384]{1,0:T(8,128)(2,1)} %get-tuple-element.31) | copy-start | bytes 884740
  72.8 24.6 %copy-start = (bf16[4,384,384]{2,1,0:T(8,128)(2,1)S(1)}, bf16[4,384,384]{2,1,0:T(8,128)(2,1)}, u32[]{:S(2)}) copy-start(bf16[4,384,384]{2,1,0:T(8,128)(2,1)} %get-tuple-element.29.own) | copy-start | bytes 3538948
  72.8 76.8 %all-to-all-start.2 = ((bf16[4,384,384]{2,1,0:T(8,128)(2,1)}), bf16[4,384,384]{2,1,0:T(8,128)(2,1)S(1)}, u32[]{:S(2)}, u32[]{:S(2)}) async-start(bf16[4,384,384]{2,1,0:T(8,128)(2,1)} %get-tuple-element.25), calls=%async_computation.2 | async-start | bytes 2359296 | tf_op jit(solution)/shard_map/all_to_all | solution.py:386
  79.3 10.7 %collective-permute-start.5 = (bf16[384,384]{1,0:T(8,128)(2,1)S(1)}, bf16[384,384]{1,0:T(8,128)(2,1)S(1)}, u32[]{:S(2)}, u32[]{:S(2)}) collective-permute-start(bf16[384,384]{1,0:T(8,128)(2,1)S(1)} %copy-done.7), channel_id=1, source_target_pairs={{4,0},{5,1},{6,2},{7,3},{8,4},{9,5},{10,6},{11,7},{12,8},{13,9},{1... | collective-permute-start | bytes 884744 | tf_op jit(solution)/shard_map/ppermute | solution.py:359
  84.6 7.7 %collective-permute-start.4 = (bf16[384,384]{1,0:T(8,128)(2,1)}, bf16[384,384]{1,0:T(8,128)(2,1)S(1)}, u32[]{:S(2)}, u32[]{:S(2)}) collective-permute-start(bf16[384,384]{1,0:T(8,128)(2,1)} %get-tuple-element.30), channel_id=1, source_target_pairs={{4,0},{5,1},{6,2},{7,3},{8,4},{9,5},{10,6},{11,7},{12,8},{13,9},{1... | collective-permute-start | bytes 884744 | tf_op jit(solution)/shard_map/ppermute | solution.py:359
  87.6 9.8 %collective-permute-start.7 = (bf16[384,384]{1,0:T(8,128)(2,1)}, bf16[384,384]{1,0:T(8,128)(2,1)S(1)}, u32[]{:S(2)}, u32[]{:S(2)}) collective-permute-start(bf16[384,384]{1,0:T(8,128)(2,1)} %get-tuple-element.32), channel_id=1, source_target_pairs={{0,4},{1,5},{2,6},{3,7},{4,8},{5,9},{6,10},{7,11},{8,12},{9,13},{1... | collective-permute-start | bytes 884744 | tf_op jit(solution)/shard_map/ppermute | solution.py:359
  89.9 7.5 %collective-permute-start.6 = (bf16[384,384]{1,0:T(8,128)(2,1)S(1)}, bf16[384,384]{1,0:T(8,128)(2,1)S(1)}, u32[]{:S(2)}, u32[]{:S(2)}) collective-permute-start(bf16[384,384]{1,0:T(8,128)(2,1)S(1)} %collective-permute-done.5.from_after_3), channel_id=1, source_target_pairs={{252,124},{253,125},{254,126},{255,127},{508,381},{509,382},{510,3... | collective-permute-start | bytes 884744 | tf_op jit(solution)/shard_map/ppermute | solution.py:359
  97.9 33.2 %collective-permute-start.8 = (bf16[384,384]{1,0:T(8,128)(2,1)S(1)}, bf16[384,384]{1,0:T(8,128)(2,1)S(1)}, u32[]{:S(2)}, u32[]{:S(2)}) collective-permute-start(bf16[384,384]{1,0:T(8,128)(2,1)S(1)} %get-tuple-element.34), channel_id=1, source_target_pairs={{0,2},{1,3},{2,0},{3,1},{4,6},{5,7},{6,4},{7,5},{8,10},{9,11},{10,... | collective-permute-start | bytes 884744 | tf_op jit(solution)/shard_map/ppermute | solution.py:393
  105.4 30.2 %collective-permute-start.9 = (bf16[384,384]{1,0:T(8,128)(2,1)S(1)}, bf16[384,384]{1,0:T(8,128)(2,1)S(1)}, u32[]{:S(2)}, u32[]{:S(2)}) collective-permute-start(bf16[384,384]{1,0:T(8,128)(2,1)S(1)} %get-tuple-element.35), channel_id=1, source_target_pairs={{0,1},{1,2},{2,3},{3,0},{4,5},{5,6},{6,7},{7,4},{8,9},{9,10},{10,1... | collective-permute-start | bytes 884744 | tf_op jit(solution)/shard_map/ppermute | solution.py:393
  107.6 40.8 %collective-permute-start.10 = (bf16[384,384]{1,0:T(8,128)(2,1)S(1)}, bf16[384,384]{1,0:T(8,128)(2,1)S(1)}, u32[]{:S(2)}, u32[]{:S(2)}) collective-permute-start(bf16[384,384]{1,0:T(8,128)(2,1)S(1)} %get-tuple-element.36), channel_id=1, source_target_pairs={{0,3},{1,0},{2,1},{3,2},{4,7},{5,4},{6,5},{7,6},{8,11},{9,8},{10,9... | collective-permute-start | bytes 884744 | tf_op jit(solution)/shard_map/ppermute | solution.py:393

commit v7 on v6

--- a/solution.py
+++ b/solution.py
@@ -21,7 +21,6 @@
 AUDIO = 64
 STACK = VIDEO + AUDIO
 ROWS = 2 * STACK
-LIST_ROWS = 16
 SCALE = HEAD_SIZE ** -0.5
 LOG2_SCALE = SCALE * 1.4426950408889634
 MASKED = -1e30
@@ -60,16 +59,11 @@
         copy.wait()
 
 
-def pack_qg_kernel(shift, video_list, audio_list, vq, aq, vg, ag, out, sems):
+def pack_qg_kernel(shift, vq, aq, vg, ag, out, sems):
     copies = []
     for member in range(MEMBERS):
         first = lax.rem(shift[0] + member, MEMBERS) * GROUP_WIDTH
         start_packing(copies, sems.at[member], first, (vq, aq, vg, ag), out.at[member])
-    video_first = jnp.full((8, GROUP_WIDTH), video_list[0, 0].astype(jnp.float32))
-    audio_first = jnp.full((8, GROUP_WIDTH), audio_list[0, 0].astype(jnp.float32))
-    firsts = jnp.concatenate([video_first, audio_first], axis=0).astype(jnp.bfloat16)
-    for member in range(MEMBERS):
-        out[member, ROWS : ROWS + LIST_ROWS] = firsts
     for copy in copies:
         copy.wait()
 
@@ -125,16 +119,13 @@
     return parts[0] if len(parts) == 1 else jnp.concatenate(parts, axis=0)
 
 
-def masks_of(window_start, firsts):
-    firsts = firsts.astype(jnp.float32)
+def masks_of(window_start, video_first, audio_first):
     video_slot = lax.broadcasted_iota(jnp.int32, (1, WINDOW_BLOCKS * VIDEO), 1) // VIDEO
     audio_slot = lax.broadcasted_iota(jnp.int32, (1, WINDOW_BLOCKS * AUDIO), 1) // AUDIO
-    video_first = jnp.concatenate([firsts[0:1]] * 2, axis=1)
-    audio_first = jnp.concatenate([firsts[8:9]] * 4, axis=1)
-    video_place = (audio_slot + window_start).astype(jnp.float32) - video_first
-    audio_place = (video_slot + window_start).astype(jnp.float32) - audio_first
-    cross_mask = jnp.where((video_place == 0.0) | (video_place == 1.0), 0.0, MASKED)
-    audio_mask = jnp.where((audio_place == 0.0) | (audio_place == 1.0), 0.0, MASKED)
+    video_place = audio_slot + window_start - video_first
+    audio_place = video_slot + window_start - audio_first
+    cross_mask = jnp.where((video_place == 0) | (video_place == 1), 0.0, MASKED)
+    audio_mask = jnp.where((audio_place == 0) | (audio_place == 1), 0.0, MASKED)
     return cross_mask, audio_mask
 
 
@@ -157,6 +148,7 @@
 def attention_kernel(
     last_group,
     group_ref,
+    firsts,
     kv,
     qg,
     before_2,
@@ -191,7 +183,7 @@
     rounded, score_grads, cross_rounded, cross_score_grads = [], [], [], []
     for m in members:
         cross_mask, audio_mask = masks_of(
-            group * MEMBERS + m - HALF_WINDOW, qg[m, ROWS : ROWS + LIST_ROWS]
+            group * MEMBERS + m - HALF_WINDOW, firsts[m, 0], firsts[m, 1]
         )
         scaled = product(queries[m], keys[m], 1, 1) * LOG2_SCALE
         cross_scaled = product(video_queries[m], audio_keys[m], 1, 1) * LOG2_SCALE
@@ -262,9 +254,6 @@
 
 PACKED_KV = jax.ShapeDtypeStruct((MEMBERS, ROWS, GROUP_WIDTH), jnp.bfloat16)
 BLOCK_KV = jax.ShapeDtypeStruct((ROWS, GROUP_WIDTH), jnp.bfloat16)
-PACKED_QG = jax.ShapeDtypeStruct((MEMBERS, ROWS + LIST_ROWS, GROUP_WIDTH), jnp.bfloat16)
-
-
 def pack_kv(shift, *arrays):
     return pl.pallas_call(
         pack_kv_kernel,
@@ -280,8 +269,8 @@
 def pack_qg(shift, *arrays):
     return pl.pallas_call(
         pack_qg_kernel,
-        out_shape=PACKED_QG,
-        in_specs=[whole(pltpu.SMEM)] * 3 + [whole(pl.ANY)] * 4,
+        out_shape=PACKED_KV,
+        in_specs=[whole(pltpu.SMEM)] + [whole(pl.ANY)] * 4,
         out_specs=whole(),
         scratch_shapes=[pltpu.SemaphoreType.DMA((MEMBERS, 4))],
         compiler_params=LARGE,
@@ -324,8 +313,9 @@
         out_shape=[PACKED_KV] * 2 + [BLOCK_KV] * 3,
         in_specs=[
             whole(pltpu.SMEM),
+            whole(pltpu.SMEM),
             head_block(MEMBERS, ROWS),
-            head_block(MEMBERS, ROWS + LIST_ROWS),
+            head_block(MEMBERS, ROWS),
             *[head_block(ROWS)] * 4,
         ],
         out_specs=[head_block(MEMBERS, ROWS)] * 2 + [head_block(ROWS)] * 3,
@@ -414,8 +404,6 @@
     kv = exchange(kv_packed)
     qg_packed = pack_qg(
         shift,
-        video_lists,
-        audio_lists,
         video_query,
         audio_query,
         video_cotangent,
@@ -425,8 +413,10 @@
     before_2 = to_group(kv[2], 1)
     after = to_group(kv[0], -1)
     qg = exchange(qg_packed)
+    own_firsts = jnp.concatenate([video_lists[:, :1], audio_lists[:, :1]], axis=1)
+    firsts = lax.all_gather(own_firsts, "member", axis=0, tiled=True)
     qg_part, kv_part, part_2, part_3, after_part = attention(
-        groups, group, kv, qg, before_2, before_3, relayed_3, after
+        groups, group, firsts, kv, qg, before_2, before_3, relayed_3, after
     )
     qg_back = exchange(qg_part)
     from_after_3, relayed_back = to_group_by_relay(part_3, -1)

time: 151 us -> 157 us (1.040)
  the two profiles are of different devices: /device:TPU:7 before, /device:TPU:63 now
where the time goes in v7:
time: 157 us; the launch traced here: 156 us
  starting transfers between devices  73.4 us (47%)
  waiting for transfers between devices  54 us (34%)
  Pallas kernels  16.4 us (10%)
  blocking collectives  9.94 us (6%)
    all_to_all x3, starting transfers between devices, exchange(): return lax.all_to_all(packed, 'member', 0, 0)  32.2 us
    ppermute x8, starting transfers between devices, moved(): return lax.ppermute(block, ('clip', 'tower', 'group', 'member'), route)  29.8 us
    ppermute x3, waiting for transfers between devices, send_round(): received[d] = lax.ppermute(blocks[d], 'member', route)  19.3 us
    all_to_all x3, waiting for transfers between devices, exchange(): return lax.all_to_all(packed, 'member', 0, 0)  18.1 us
    ppermute x8, waiting for transfers between devices, moved(): return lax.ppermute(block, ('clip', 'tower', 'group', 'member'), route)  16.6 us
    ppermute x3, starting transfers between devices, send_round(): received[d] = lax.ppermute(blocks[d], 'member', route)  11.4 us
    all_gather x1, blocking collectives, body(): firsts = lax.all_gather(own_firsts, 'member', axis=0, tiled=True)  9.94 us
    pallas_call x1, Pallas kernels, attention(): pl.pallas_call(functools.partial(attention_kernel, groups - 1), grid=(GRO...  8.82 us
  transfers between devices with their start and end apart: 14, of which 6 were waited for; matrix products, arithmetic and copies ran while one was open for 0% of the time, Pallas kernels for 3%

profile of v7, /device:TPU:63, one launch (start us, length us, event | category | flops | bytes accessed | tf_op | source)
XLA Modules:
  0.0 156.2 jit_solution(1903078940283443728)
XLA Ops:
  0.6 2.5 %pack_kv.1 = bf16[4,384,384]{2,1,0:T(8,128)(2,1)} custom-call(s32[1]{0:T(128)} %bitcast.shift, bf16[128,1536]{1,0:T(8,128)(2,1)} %vk.1, bf16[128,1536]{1,0:T(8,128)(2,1)} %vv.1, bf16[64,1536]{1,0:T(8,128)(2,1)} %ak.1, bf16[64,1536]{1,0:T(8,128)(2,1)} %av.1), custom_call_target="tpu_custom_call" | custom-call | tf_op jit(solution)/shard_map/pack_kv/pallas_call | solution.py:258
  3.1 10.0 %all-to-all-start = ((bf16[4,384,384]{2,1,0:T(8,128)(2,1)}), bf16[4,384,384]{2,1,0:T(8,128)(2,1)S(1)}, u32[]{:S(2)}, u32[]{:S(2)}) async-start(bf16[4,384,384]{2,1,0:T(8,128)(2,1)} %pack_kv.1), calls=%async_computation | async-start | bytes 2359296 | tf_op jit(solution)/shard_map/all_to_all | solution.py:376
  13.2 2.5 %pack_qg.1 = bf16[4,384,384]{2,1,0:T(8,128)(2,1)} custom-call(s32[1]{0:T(128)} %bitcast.shift, bf16[128,1536]{1,0:T(8,128)(2,1)} %vq.1, bf16[64,1536]{1,0:T(8,128)(2,1)} %aq.1, bf16[128,1536]{1,0:T(8,128)(2,1)} %vg.1, bf16[64,1536]{1,0:T(8,128)(2,1)} %ag.1), custom_call_target="tpu_custom_call" | custom-call | tf_op jit(solution)/shard_map/pack_qg/pallas_call | solution.py:270
  15.7 18.1 %all-to-all-done.kv = bf16[4,384,384]{2,1,0:T(8,128)(2,1)S(1)} async-done(((bf16[4,384,384]{2,1,0:T(8,128)(2,1)}), bf16[4,384,384]{2,1,0:T(8,128)(2,1)S(1)}, u32[]{:S(2)}, u32[]{:S(2)}) %all-to-all-start) | async-done | bytes 1179680 | tf_op jit(solution)/shard_map/all_to_all | solution.py:376
  33.8 10.3 %all-to-all-start.1 = ((bf16[4,384,384]{2,1,0:T(8,128)(2,1)}), bf16[4,384,384]{2,1,0:T(8,128)(2,1)S(1)}, u32[]{:S(2)}, u32[]{:S(2)}) async-start(bf16[4,384,384]{2,1,0:T(8,128)(2,1)} %pack_qg.1), calls=%async_computation.1 | async-start | bytes 2359296 | tf_op jit(solution)/shard_map/all_to_all | solution.py:376
  44.0 0.1 slice_bitcast_fusion
  44.1 1.9 %collective-permute-start.1 = (bf16[384,384]{1,0:T(8,128)(2,1)S(1)}, bf16[384,384]{1,0:T(8,128)(2,1)S(1)}, u32[]{:S(2)}, u32[]{:S(2)}) collective-permute-start(bf16[384,384]{1,0:T(8,128)(2,1)S(1)} %get-tuple-element.43), channel_id=1, source_target_pairs={{0,4},{1,5},{2,6},{3,7},{4,8},{5,9},{6,10},{7,11},{8,12},{9,13},{1... | collective-permute-start | bytes 884744 | tf_op jit(solution)/shard_map/ppermute | solution.py:349
  46.1 3.4 %collective-permute-start.3 = (bf16[384,384]{1,0:T(8,128)(2,1)S(1)}, bf16[384,384]{1,0:T(8,128)(2,1)S(1)}, u32[]{:S(2)}, u32[]{:S(2)}) collective-permute-start(bf16[384,384]{1,0:T(8,128)(2,1)S(1)} %get-tuple-element.42), channel_id=1, source_target_pairs={{4,0},{5,1},{6,2},{7,3},{8,4},{9,5},{10,6},{11,7},{12,8},{13,9},{1... | collective-permute-start | bytes 884744 | tf_op jit(solution)/shard_map/ppermute | solution.py:349
  49.4 7.3 %collective-permute-start = (bf16[384,384]{1,0:T(8,128)(2,1)S(1)}, bf16[384,384]{1,0:T(8,128)(2,1)S(1)}, u32[]{:S(2)}, u32[]{:S(2)}) collective-permute-start(bf16[384,384]{1,0:T(8,128)(2,1)S(1)} %get-tuple-element.44), channel_id=1, source_target_pairs={{0,4},{1,5},{2,6},{3,7},{4,8},{5,9},{6,10},{7,11},{8,12},{9,13},{1... | collective-permute-start | bytes 884744 | tf_op jit(solution)/shard_map/ppermute | solution.py:349
  56.8 0.7 collective-permute-start.2
  57.5 0.1 add_bitcast_fusion
  57.6 9.9 %all-gather = s32[4,1,2]{2,1,0:T(1,128)} all-gather(s32[1,1,2]{2,1,0:T(1,128)S(1)} %add_bitcast_fusion), channel_id=1, replica_groups=mesh['clip'=2,'tower'=2,'group'=32,'member'=4] {'member'}, dimensions={0}, use_global_device_ids=true | all-gather | bytes 40 | tf_op jit(solution)/shard_map/all_gather | solution.py:417
  67.7 1.0 copy-done.2
  68.7 0.1 copy-done.5
  68.8 0.1 copy-done.6
  68.9 8.8 %attention.1 = (bf16[4,384,384]{2,1,0:T(8,128)(2,1)}, bf16[4,384,384]{2,1,0:T(8,128)(2,1)}, bf16[384,384]{1,0:T(8,128)(2,1)}, bf16[384,384]{1,0:T(8,128)(2,1)}, bf16[384,384]{1,0:T(8,128)(2,1)}) custom-call(s32[1]{0:T(128)} %bitcast.1.group_ref, s32[4,2]{1,0:T(4,128)} %bitcast.14, bf16[4,384,384]{2,1,0:T(8,128)(2,1)} %copy-done.1, ...), custom_call_target="tpu_custom_call" | custom-call | tf_op jit(solution)/shard_map/attention/pallas_call | solution.py:310
  77.7 11.9 %all-to-all-start.2 = ((bf16[4,384,384]{2,1,0:T(8,128)(2,1)}), bf16[4,384,384]{2,1,0:T(8,128)(2,1)S(1)}, u32[]{:S(2)}, u32[]{:S(2)}) async-start(bf16[4,384,384]{2,1,0:T(8,128)(2,1)} %get-tuple-element.25), calls=%async_computation.2 | async-start | bytes 2359296 | tf_op jit(solution)/shard_map/all_to_all | solution.py:376
  89.6 3.0 %collective-permute-start.5 = (bf16[384,384]{1,0:T(8,128)(2,1)S(1)}, bf16[384,384]{1,0:T(8,128)(2,1)S(1)}, u32[]{:S(2)}, u32[]{:S(2)}) collective-permute-start(bf16[384,384]{1,0:T(8,128)(2,1)S(1)} %copy-done.7), channel_id=1, source_target_pairs={{4,0},{5,1},{6,2},{7,3},{8,4},{9,5},{10,6},{11,7},{12,8},{13,9},{1... | collective-permute-start | bytes 884744 | tf_op jit(solution)/shard_map/ppermute | solution.py:349
  92.6 3.0 %collective-permute-start.4 = (bf16[384,384]{1,0:T(8,128)(2,1)}, bf16[384,384]{1,0:T(8,128)(2,1)S(1)}, u32[]{:S(2)}, u32[]{:S(2)}) collective-permute-start(bf16[384,384]{1,0:T(8,128)(2,1)} %get-tuple-element.30), channel_id=1, source_target_pairs={{4,0},{5,1},{6,2},{7,3},{8,4},{9,5},{10,6},{11,7},{12,8},{13,9},{1... | collective-permute-start | bytes 884744 | tf_op jit(solution)/shard_map/ppermute | solution.py:349
  95.5 9.3 %collective-permute-start.7 = (bf16[384,384]{1,0:T(8,128)(2,1)}, bf16[384,384]{1,0:T(8,128)(2,1)S(1)}, u32[]{:S(2)}, u32[]{:S(2)}) collective-permute-start(bf16[384,384]{1,0:T(8,128)(2,1)} %get-tuple-element.32), channel_id=1, source_target_pairs={{0,4},{1,5},{2,6},{3,7},{4,8},{5,9},{6,10},{7,11},{8,12},{9,13},{1... | collective-permute-start | bytes 884744 | tf_op jit(solution)/shard_map/ppermute | solution.py:349
  104.8 1.3 collective-permute-start.6
  106.1 6.4 %collective-permute-done.4.from_after_2 = bf16[384,384]{1,0:T(8,128)(2,1)S(1)} collective-permute-done((bf16[384,384]{1,0:T(8,128)(2,1)}, bf16[384,384]{1,0:T(8,128)(2,1)S(1)}, u32[]{:S(2)}, u32[]{:S(2)}) %collective-permute-start.4) | collective-permute-done | bytes 294944 | tf_op jit(solution)/shard_map/ppermute | solution.py:349
  112.6 10.2 %collective-permute-done.6.relayed_3 = bf16[384,384]{1,0:T(8,128)(2,1)S(1)} collective-permute-done((bf16[384,384]{1,0:T(8,128)(2,1)S(1)}, bf16[384,384]{1,0:T(8,128)(2,1)S(1)}, u32[]{:S(2)}, u32[]{:S(2)}) %collective-permute-start.6) | collective-permute-done | bytes 294944 | tf_op jit(solution)/shard_map/ppermute | solution.py:349
  122.8 0.4 merge.1
  123.2 4.0 %collective-permute-start.8 = (bf16[384,384]{1,0:T(8,128)(2,1)S(1)}, bf16[384,384]{1,0:T(8,128)(2,1)S(1)}, u32[]{:S(2)}, u32[]{:S(2)}) collective-permute-start(bf16[384,384]{1,0:T(8,128)(2,1)S(1)} %get-tuple-element.34), channel_id=1, source_target_pairs={{0,2},{1,3},{2,0},{3,1},{4,6},{5,7},{6,4},{7,5},{8,10},{9,11},{10,... | collective-permute-start | bytes 884744 | tf_op jit(solution)/shard_map/ppermute | solution.py:383
  127.2 4.0 %collective-permute-start.9 = (bf16[384,384]{1,0:T(8,128)(2,1)S(1)}, bf16[384,384]{1,0:T(8,128)(2,1)S(1)}, u32[]{:S(2)}, u32[]{:S(2)}) collective-permute-start(bf16[384,384]{1,0:T(8,128)(2,1)S(1)} %get-tuple-element.35), channel_id=1, source_target_pairs={{0,1},{1,2},{2,3},{3,0},{4,5},{5,6},{6,7},{7,4},{8,9},{9,10},{10,1... | collective-permute-start | bytes 884744 | tf_op jit(solution)/shard_map/ppermute | solution.py:383
  131.2 3.4 %collective-permute-start.10 = (bf16[384,384]{1,0:T(8,128)(2,1)S(1)}, bf16[384,384]{1,0:T(8,128)(2,1)S(1)}, u32[]{:S(2)}, u32[]{:S(2)}) collective-permute-start(bf16[384,384]{1,0:T(8,128)(2,1)S(1)} %get-tuple-element.36), channel_id=1, source_target_pairs={{0,3},{1,0},{2,1},{3,2},{4,7},{5,4},{6,5},{7,6},{8,11},{9,8},{10,9... | collective-permute-start | bytes 884744 | tf_op jit(solution)/shard_map/ppermute | solution.py:383
  134.6 9.5 %collective-permute-done.8.refs_1_ = bf16[384,384]{1,0:T(8,128)(2,1)S(1)} collective-permute-done((bf16[384,384]{1,0:T(8,128)(2,1)S(1)}, bf16[384,384]{1,0:T(8,128)(2,1)S(1)}, u32[]{:S(2)}, u32[]{:S(2)}) %collective-permute-start.8) | collective-permute-done | bytes 294944 | tf_op jit(solution)/shard_map/ppermute | solution.py:383
  144.1 2.6 %collective-permute-done.9.refs_2_ = bf16[384,384]{1,0:T(8,128)(2,1)S(1)} collective-permute-done((bf16[384,384]{1,0:T(8,128)(2,1)S(1)}, bf16[384,384]{1,0:T(8,128)(2,1)S(1)}, u32[]{:S(2)}, u32[]{:S(2)}) %collective-permute-start.9) | collective-permute-done | bytes 294944 | tf_op jit(solution)/shard_map/ppermute | solution.py:383
  146.7 7.2 %collective-permute-done.10.refs_3_ = bf16[384,384]{1,0:T(8,128)(2,1)S(1)} collective-permute-done((bf16[384,384]{1,0:T(8,128)(2,1)S(1)}, bf16[384,384]{1,0:T(8,128)(2,1)S(1)}, u32[]{:S(2)}, u32[]{:S(2)}) %collective-permute-start.10) | collective-permute-done | bytes 294944 | tf_op jit(solution)/shard_map/ppermute | solution.py:383
  153.9 1.1 unpack.3
  155.0 1.1 unpack.2
  (25 shorter events, 0.1 us)
Async XLA Ops:
  3.1 30.6 %all-to-all-start = ((bf16[4,384,384]{2,1,0:T(8,128)(2,1)}), bf16[4,384,384]{2,1,0:T(8,128)(2,1)S(1)}, u32[]{:S(2)}, u32[]{:S(2)}) async-start(bf16[4,384,384]{2,1,0:T(8,128)(2,1)} %pack_kv.1), calls=%async_computation | async-start | bytes 2359296 | tf_op jit(solution)/shard_map/all_to_all | solution.py:376
  33.8 10.4 %copy-start.1 = (bf16[4,384,384]{2,1,0:T(8,128)(2,1)}, bf16[4,384,384]{2,1,0:T(8,128)(2,1)S(1)}, u32[]{:S(2)}) copy-start(bf16[4,384,384]{2,1,0:T(8,128)(2,1)S(1)} %all-to-all-done.kv) | copy-start | bytes 3538948
  33.8 33.8 %all-to-all-start.1 = ((bf16[4,384,384]{2,1,0:T(8,128)(2,1)}), bf16[4,384,384]{2,1,0:T(8,128)(2,1)S(1)}, u32[]{:S(2)}, u32[]{:S(2)}) async-start(bf16[4,384,384]{2,1,0:T(8,128)(2,1)} %pack_qg.1), calls=%async_computation.1 | async-start | bytes 2359296 | tf_op jit(solution)/shard_map/all_to_all | solution.py:376
  44.0 13.5 %copy-start.8 = (s32[1,2]{1,0:T(1,128)S(1)}, s32[1,2]{1,0:T(1,128)}, u32[]{:S(2)}) copy-start(s32[1,2]{1,0:T(1,128)} %param.19) | copy-start | bytes 28
  44.0 13.5 %copy-start.9 = (s32[1,2]{1,0:T(1,128)S(1)}, s32[1,2]{1,0:T(1,128)}, u32[]{:S(2)}) copy-start(s32[1,2]{1,0:T(1,128)} %param.18) | copy-start | bytes 28
  44.1 12.7 %collective-permute-start.1 = (bf16[384,384]{1,0:T(8,128)(2,1)S(1)}, bf16[384,384]{1,0:T(8,128)(2,1)S(1)}, u32[]{:S(2)}, u32[]{:S(2)}) collective-permute-start(bf16[384,384]{1,0:T(8,128)(2,1)S(1)} %get-tuple-element.43), channel_id=1, source_target_pairs={{0,4},{1,5},{2,6},{3,7},{4,8},{5,9},{6,10},{7,11},{8,12},{9,13},{1... | collective-permute-start | bytes 884744 | tf_op jit(solution)/shard_map/ppermute | solution.py:349
  46.1 21.5 %collective-permute-start.3 = (bf16[384,384]{1,0:T(8,128)(2,1)S(1)}, bf16[384,384]{1,0:T(8,128)(2,1)S(1)}, u32[]{:S(2)}, u32[]{:S(2)}) collective-permute-start(bf16[384,384]{1,0:T(8,128)(2,1)S(1)} %get-tuple-element.42), channel_id=1, source_target_pairs={{4,0},{5,1},{6,2},{7,3},{8,4},{9,5},{10,6},{11,7},{12,8},{13,9},{1... | collective-permute-start | bytes 884744 | tf_op jit(solution)/shard_map/ppermute | solution.py:349
  49.4 18.2 %collective-permute-start = (bf16[384,384]{1,0:T(8,128)(2,1)S(1)}, bf16[384,384]{1,0:T(8,128)(2,1)S(1)}, u32[]{:S(2)}, u32[]{:S(2)}) collective-permute-start(bf16[384,384]{1,0:T(8,128)(2,1)S(1)} %get-tuple-element.44), channel_id=1, source_target_pairs={{0,4},{1,5},{2,6},{3,7},{4,8},{5,9},{6,10},{7,11},{8,12},{9,13},{1... | collective-permute-start | bytes 884744 | tf_op jit(solution)/shard_map/ppermute | solution.py:349
  56.8 10.8 %copy-start.3 = (bf16[384,384]{1,0:T(8,128)(2,1)}, bf16[384,384]{1,0:T(8,128)(2,1)S(1)}, u32[]{:S(2)}) copy-start(bf16[384,384]{1,0:T(8,128)(2,1)S(1)} %collective-permute-done.1.before_3) | copy-start | bytes 884740
  56.8 10.8 %collective-permute-start.2 = (bf16[384,384]{1,0:T(8,128)(2,1)S(1)}, bf16[384,384]{1,0:T(8,128)(2,1)S(1)}, u32[]{:S(2)}, u32[]{:S(2)}) collective-permute-start(bf16[384,384]{1,0:T(8,128)(2,1)S(1)} %collective-permute-done.1.before_3), channel_id=1, source_target_pairs={{0,128},{1,129},{2,130},{3,131},{256,387},{257,384},{258,385},{259... | collective-permute-start | bytes 884744 | tf_op jit(solution)/shard_map/ppermute | solution.py:349
  67.6 1.0 copy-start.2
  67.6 1.1 copy-start.4
  67.6 1.2 copy-start.5
  67.6 1.2 copy-start.6
  77.7 11.9 %copy-start.7 = (bf16[384,384]{1,0:T(8,128)(2,1)S(1)}, bf16[384,384]{1,0:T(8,128)(2,1)}, u32[]{:S(2)}) copy-start(bf16[384,384]{1,0:T(8,128)(2,1)} %get-tuple-element.31) | copy-start | bytes 884740
  77.7 45.1 %copy-start = (bf16[4,384,384]{2,1,0:T(8,128)(2,1)S(1)}, bf16[4,384,384]{2,1,0:T(8,128)(2,1)}, u32[]{:S(2)}) copy-start(bf16[4,384,384]{2,1,0:T(8,128)(2,1)} %get-tuple-element.29.own) | copy-start | bytes 3538948
  77.7 77.3 %all-to-all-start.2 = ((bf16[4,384,384]{2,1,0:T(8,128)(2,1)}), bf16[4,384,384]{2,1,0:T(8,128)(2,1)S(1)}, u32[]{:S(2)}, u32[]{:S(2)}) async-start(bf16[4,384,384]{2,1,0:T(8,128)(2,1)} %get-tuple-element.25), calls=%async_computation.2 | async-start | bytes 2359296 | tf_op jit(solution)/shard_map/all_to_all | solution.py:376
  89.6 15.2 %collective-permute-start.5 = (bf16[384,384]{1,0:T(8,128)(2,1)S(1)}, bf16[384,384]{1,0:T(8,128)(2,1)S(1)}, u32[]{:S(2)}, u32[]{:S(2)}) collective-permute-start(bf16[384,384]{1,0:T(8,128)(2,1)S(1)} %copy-done.7), channel_id=1, source_target_pairs={{4,0},{5,1},{6,2},{7,3},{8,4},{9,5},{10,6},{11,7},{12,8},{13,9},{1... | collective-permute-start | bytes 884744 | tf_op jit(solution)/shard_map/ppermute | solution.py:349
  92.6 20.0 %collective-permute-start.4 = (bf16[384,384]{1,0:T(8,128)(2,1)}, bf16[384,384]{1,0:T(8,128)(2,1)S(1)}, u32[]{:S(2)}, u32[]{:S(2)}) collective-permute-start(bf16[384,384]{1,0:T(8,128)(2,1)} %get-tuple-element.30), channel_id=1, source_target_pairs={{4,0},{5,1},{6,2},{7,3},{8,4},{9,5},{10,6},{11,7},{12,8},{13,9},{1... | collective-permute-start | bytes 884744 | tf_op jit(solution)/shard_map/ppermute | solution.py:349
  95.5 17.0 %collective-permute-start.7 = (bf16[384,384]{1,0:T(8,128)(2,1)}, bf16[384,384]{1,0:T(8,128)(2,1)S(1)}, u32[]{:S(2)}, u32[]{:S(2)}) collective-permute-start(bf16[384,384]{1,0:T(8,128)(2,1)} %get-tuple-element.32), channel_id=1, source_target_pairs={{0,4},{1,5},{2,6},{3,7},{4,8},{5,9},{6,10},{7,11},{8,12},{9,13},{1... | collective-permute-start | bytes 884744 | tf_op jit(solution)/shard_map/ppermute | solution.py:349
  104.8 17.9 %collective-permute-start.6 = (bf16[384,384]{1,0:T(8,128)(2,1)S(1)}, bf16[384,384]{1,0:T(8,128)(2,1)S(1)}, u32[]{:S(2)}, u32[]{:S(2)}) collective-permute-start(bf16[384,384]{1,0:T(8,128)(2,1)S(1)} %collective-permute-done.5.from_after_3), channel_id=1, source_target_pairs={{252,124},{253,125},{254,126},{255,127},{508,381},{509,382},{510,3... | collective-permute-start | bytes 884744 | tf_op jit(solution)/shard_map/ppermute | solution.py:349
  123.2 20.9 %collective-permute-start.8 = (bf16[384,384]{1,0:T(8,128)(2,1)S(1)}, bf16[384,384]{1,0:T(8,128)(2,1)S(1)}, u32[]{:S(2)}, u32[]{:S(2)}) collective-permute-start(bf16[384,384]{1,0:T(8,128)(2,1)S(1)} %get-tuple-element.34), channel_id=1, source_target_pairs={{0,2},{1,3},{2,0},{3,1},{4,6},{5,7},{6,4},{7,5},{8,10},{9,11},{10,... | collective-permute-start | bytes 884744 | tf_op jit(solution)/shard_map/ppermute | solution.py:383
  127.2 19.5 %collective-permute-start.9 = (bf16[384,384]{1,0:T(8,128)(2,1)S(1)}, bf16[384,384]{1,0:T(8,128)(2,1)S(1)}, u32[]{:S(2)}, u32[]{:S(2)}) collective-permute-start(bf16[384,384]{1,0:T(8,128)(2,1)S(1)} %get-tuple-element.35), channel_id=1, source_target_pairs={{0,1},{1,2},{2,3},{3,0},{4,5},{5,6},{6,7},{7,4},{8,9},{9,10},{10,1... | collective-permute-start | bytes 884744 | tf_op jit(solution)/shard_map/ppermute | solution.py:383
  131.2 22.7 %collective-permute-start.10 = (bf16[384,384]{1,0:T(8,128)(2,1)S(1)}, bf16[384,384]{1,0:T(8,128)(2,1)S(1)}, u32[]{:S(2)}, u32[]{:S(2)}) collective-permute-start(bf16[384,384]{1,0:T(8,128)(2,1)S(1)} %get-tuple-element.36), channel_id=1, source_target_pairs={{0,3},{1,0},{2,1},{3,2},{4,7},{5,4},{6,5},{7,6},{8,11},{9,8},{10,9... | collective-permute-start | bytes 884744 | tf_op jit(solution)/shard_map/ppermute | solution.py:383
